TPU v7x, 512 devices: a whole 4x8x8 slice. The times are simulated.
512 devices in a mesh: section: 8 (over z), cp: 16 (over x, y_lo), tp: 4 (over y_hi, core).
Axes of the slice: x: 4, y: 8 (y_hi: 2, y_lo: 4; y = y_hi * 4 + y_lo), z: 8, core: 2. Of those that a mesh axis runs over, the one named last changes fastest.
Arguments:
- queries: bfloat16 [2, 8, 512, 4096], P(None, 'section', 'cp', 'tp'), may hold values from -90 to 90
- key_rows: bfloat16 [8, 24576, 512], P('section', 'cp', 'tp'), may hold values from -13 to 13
- value_rows: bfloat16 [8, 24576, 512], P('section', 'cp', 'tp'), may hold values from -8 to 8
- section_rows: bfloat16 [8, 512, 4096], P('section', 'cp', 'tp'), may hold values from -60 to 60
- fresh_rows: bfloat16 [512, 4096], P('cp', 'tp'), may hold values from -60 to 60
- norm_gain: bfloat16 [8, 4096], P('section', 'tp'), may hold values from 0.25 to 1.75
- segment_lengths: int32 [9], replicated, may hold values from 256 to 512, as said below
Outputs:
- residual: bfloat16 [2, 8, 512, 4096], P(None, 'section', 'cp', 'tp')
- normed: bfloat16 [2, 8, 512, 4096], P(None, 'section', 'cp', 'tp')
Inputs may be any that keep to these rules, and one draw needn't show every extreme that they name: `segment_lengths`: every segment has 256 to 512 live rows and some segment has all 512.
All inputs are finite; a program needn't handle non-finite values.
Results may differ from a plain program's by a relative error of at most 0.008.
Values may be sent and summed in bfloat16 or wider, within the bound.
No kernel may reach another device: no remote copies, remote signals or barrier semaphores. Data moves between devices by JAX's collectives and lax.ppermute only.
A program may use at most 64 MiB of HBM per device.

v0:
```python
import jax
import jax.numpy as jnp
from jax import lax
from jax.sharding import PartitionSpec as P

HD = 128


NEGATIVE = -1e30
EPSILON = 1e-05


def passed_along(shard, axis, by):
    length = lax.axis_size(axis)
    return lax.ppermute(shard, axis, [(i, (i + by) % length) for i in range(length)])


def passed_along_2(value, axis, steps):
    count = lax.axis_size(axis)
    initial, last = (max(0, -steps), min(count, count - steps))
    return lax.ppermute(value, axis, [(source, source + steps) for source in range(initial, last)])


def update(running, query_block, query_pos, key_part, value_part, key_start):
    outputs, row_tops, totals = running
    kv_dev = query_block.shape[1]
    key_heads = key_part.reshape(key_part.shape[0], kv_dev, HD)
    value_heads = value_part.reshape(value_part.shape[0], kv_dev, HD)
    score_scale = HD ** (-0.5)
    scores = (
        jnp.einsum("rgjd,ngd->rgjn", query_block, key_heads, preferred_element_type=jnp.float32)
        * score_scale
    )
    key_pos = key_start + jnp.arange(key_part.shape[0], dtype=jnp.int32)
    visible = (key_pos[None, :] <= query_pos[:, None])[:, None, None, :]
    scores = jnp.where(visible, scores, NEGATIVE)
    new_top = jnp.maximum(row_tops, jnp.max(scores, axis=-1))
    weights = jnp.where(visible, jnp.exp(scores - new_top[..., None]), 0.0)
    rescale = jnp.exp(row_tops - new_top)
    totals = totals * rescale + jnp.sum(weights, axis=-1)
    mixed = jnp.einsum(
        "rgjn,ngd->rgjd",
        weights.astype(jnp.bfloat16),
        value_heads,
        preferred_element_type=jnp.float32,
    )
    outputs = outputs * rescale[..., None] + mixed
    return (outputs, new_top, totals)


def attend(running, query_block, query_pos, key_part, value_part, key_start):
    return update(running, query_block, query_pos, key_part, value_part, key_start)


def body(queries, key_rows, value_rows, section_rows, fresh_rows, norm_gain, segment_lengths):
    cycle_size = lax.axis_size("cp")
    cp_index = lax.axis_index("cp")
    section_count = lax.axis_size("section")
    section_id = lax.axis_index("section")
    rows_dev = section_rows.shape[1]
    width_dev = section_rows.shape[2]
    ctx_dev = key_rows.shape[1]
    kv_dev = key_rows.shape[2] // HD
    group_size = width_dev // HD // kv_dev
    total_keys = ctx_dev * cycle_size
    prefix = total_keys - jnp.sum(segment_lengths)
    starts = prefix + jnp.cumsum(segment_lengths) - segment_lengths
    first_seg = section_count - 1 - section_id
    start_pair = jnp.stack([starts[first_seg], starts[first_seg + 1]])
    length_pair = jnp.stack([segment_lengths[first_seg], segment_lengths[first_seg + 1]])
    local_rows = jnp.arange(rows_dev, dtype=jnp.int32)

    def positions(anchor):
        row_ids = anchor * rows_dev + local_rows
        return (start_pair[:, None] + row_ids[None, :]).reshape(-1)

    query_block = queries[:, 0].reshape(2 * rows_dev, kv_dev, group_size, HD)
    own_keys = key_rows[0]
    own_values = value_rows[0]
    initial = (
        jnp.zeros((2 * rows_dev, kv_dev, group_size, HD), jnp.float32),
        jnp.full((2 * rows_dev, kv_dev, group_size), NEGATIVE, jnp.float32),
        jnp.zeros((2 * rows_dev, kv_dev, group_size), jnp.float32),
    )
    own_start = cp_index * ctx_dev
    running = attend(initial, query_block, positions(cp_index), own_keys, own_values, own_start)

    def cycle_step(step_id, carry):
        travel, held = carry
        travel = passed_along(travel, "cp", 1)
        held = passed_along((held[0], held[1], held[2]), "cp", 1)
        anchor = (cp_index - step_id) % cycle_size
        held = attend(held, travel, positions(anchor), own_keys, own_values, own_start)
        return (travel, held)

    travel, running = lax.fori_loop(1, cycle_size, cycle_step, (query_block, running))
    running = (
        passed_along(running[0].astype(jnp.bfloat16), "cp", 1).astype(jnp.float32),
        passed_along(running[1].astype(jnp.bfloat16), "cp", 1).astype(jnp.float32),
        passed_along(running[2].astype(jnp.bfloat16), "cp", 1).astype(jnp.float32),
    )
    outputs, row_tops, totals = running
    attended = (outputs / totals[..., None]).reshape(2, rows_dev, width_dev)
    live_rows = (cp_index * rows_dev + local_rows)[None, :] < length_pair[:, None]
    attended = jnp.where(live_rows[..., None], attended, 0.0)
    sum_one = section_rows[0].astype(jnp.float32) + attended[0]
    residual_one = sum_one.astype(jnp.bfloat16)
    passed = passed_along_2(residual_one, "section", 1)
    incoming = jnp.where(section_id == 0, fresh_rows, passed)
    sum_two = incoming.astype(jnp.float32) + attended[1]
    row_sums = jnp.stack([sum_one, sum_two])
    squares = lax.psum(jnp.sum(row_sums * row_sums, axis=-1), "tp")
    full_width = width_dev * lax.axis_size("tp")
    normed = (
        row_sums
        * lax.rsqrt(squares / full_width + EPSILON)[..., None]
        * norm_gain[0].astype(jnp.float32)
    )
    residual = jnp.stack([residual_one, sum_two.astype(jnp.bfloat16)])
    return (residual[:, None], normed.astype(jnp.bfloat16)[:, None])


def solution(mesh):
    in_specs = (
        P(None, "section", "cp", "tp"),
        P("section", "cp", "tp"),
        P("section", "cp", "tp"),
        P("section", "cp", "tp"),
        P("cp", "tp"),
        P("section", "tp"),
        P(),
    )
    out_specs = (P(None, "section", "cp", "tp"), P(None, "section", "cp", "tp"))
    return jax.shard_map(body, mesh=mesh, in_specs=in_specs, out_specs=out_specs, check_vma=False)
```

profile of v0, /device:TPU:257, one launch (start us, length us, event | category | flops | bytes accessed | tf_op | source)
XLA Modules:
  0.0 345.1 jit_solution(13061398949003130689)
XLA Ops:
  11.8 273.9 %while.22 = (s32[]{:T(128)}, bf16[64,1,8,128]{3,0,2,1:T(8,128)(2,1)S(1)}, f32[64,1,8,128]{3,2,0,1:T(8,128)S(1)}, f32[64,1,8]{0,2,1:T(8,128)S(1)}, f32[64,1,8]{0,...) while((s32[]{:T(128)}, ...), condition=%wide.region_7.8_spmd.clone, body=%wide.region_4.7_spmd.clone.sunk | while | flops 409963648 | bytes 13694658 | solution.py:96
  11.8 3.3 collective-permute-start
  15.1 3.2 collective-permute-start.1
  18.3 3.2 collective-permute-start.3
  21.5 2.8 collective-permute-start.2
  27.0 6.7 %collective-permute-done.2 = f32[64,1,8,128]{3,2,0,1:T(8,128)S(1)} collective-permute-done((f32[64,1,8,128]{3,2,0,1:T(8,128)S(1)}, f32[64,1,8,128]{3,2,0,1:T(8,128)S(1)}, u32[]{:S(2)}, u32[]{:S(2)}) %collective-permute-start.2) | collective-permute-done | bytes 262176 | tf_op jit(solution)/shard_map/while/body/eval_jaxpr/ppermute | solution.py:15
  39.6 5.4 %collective-permute-start.2 = (f32[64,1,8,128]{3,2,0,1:T(8,128)S(1)}, f32[64,1,8,128]{3,2,0,1:T(8,128)S(1)}, u32[]{:S(2)}, u32[]{:S(2)}) collective-permute-start(f32[64,1,8,128]{3,2,0,1:T(8,128)S(1)} %get-tuple-element.427), channel_id=1, source_target_pairs={{0,4},{4,8},{8,12},{12,16},{16,20},{20,24},{24,28},{28,32},{32,36}... | collective-permute-start | bytes 786440 | tf_op jit(solution)/shard_map/while/body/eval_jaxpr/ppermute | solution.py:15
  47.7 3.0 collective-permute-done.2
  56.7 4.9 %collective-permute-start.2 = (f32[64,1,8,128]{3,2,0,1:T(8,128)S(1)}, f32[64,1,8,128]{3,2,0,1:T(8,128)S(1)}, u32[]{:S(2)}, u32[]{:S(2)}) collective-permute-start(f32[64,1,8,128]{3,2,0,1:T(8,128)S(1)} %get-tuple-element.427), channel_id=1, source_target_pairs={{0,4},{4,8},{8,12},{12,16},{16,20},{20,24},{24,28},{28,32},{32,36}... | collective-permute-start | bytes 786440 | tf_op jit(solution)/shard_map/while/body/eval_jaxpr/ppermute | solution.py:15
  64.2 3.5 %collective-permute-done.2 = f32[64,1,8,128]{3,2,0,1:T(8,128)S(1)} collective-permute-done((f32[64,1,8,128]{3,2,0,1:T(8,128)S(1)}, f32[64,1,8,128]{3,2,0,1:T(8,128)S(1)}, u32[]{:S(2)}, u32[]{:S(2)}) %collective-permute-start.2) | collective-permute-done | bytes 262176 | tf_op jit(solution)/shard_map/while/body/eval_jaxpr/ppermute | solution.py:15
  69.9 2.3 collective-permute-start.1
  74.1 4.6 %collective-permute-start.2 = (f32[64,1,8,128]{3,2,0,1:T(8,128)S(1)}, f32[64,1,8,128]{3,2,0,1:T(8,128)S(1)}, u32[]{:S(2)}, u32[]{:S(2)}) collective-permute-start(f32[64,1,8,128]{3,2,0,1:T(8,128)S(1)} %get-tuple-element.427), channel_id=1, source_target_pairs={{0,4},{4,8},{8,12},{12,16},{16,20},{20,24},{24,28},{28,32},{32,36}... | collective-permute-start | bytes 786440 | tf_op jit(solution)/shard_map/while/body/eval_jaxpr/ppermute | solution.py:15
  81.4 4.9 %collective-permute-done.2 = f32[64,1,8,128]{3,2,0,1:T(8,128)S(1)} collective-permute-done((f32[64,1,8,128]{3,2,0,1:T(8,128)S(1)}, f32[64,1,8,128]{3,2,0,1:T(8,128)S(1)}, u32[]{:S(2)}, u32[]{:S(2)}) %collective-permute-start.2) | collective-permute-done | bytes 262176 | tf_op jit(solution)/shard_map/while/body/eval_jaxpr/ppermute | solution.py:15
  92.2 4.2 %collective-permute-start.2 = (f32[64,1,8,128]{3,2,0,1:T(8,128)S(1)}, f32[64,1,8,128]{3,2,0,1:T(8,128)S(1)}, u32[]{:S(2)}, u32[]{:S(2)}) collective-permute-start(f32[64,1,8,128]{3,2,0,1:T(8,128)S(1)} %get-tuple-element.427), channel_id=1, source_target_pairs={{0,4},{4,8},{8,12},{12,16},{16,20},{20,24},{24,28},{28,32},{32,36}... | collective-permute-start | bytes 786440 | tf_op jit(solution)/shard_map/while/body/eval_jaxpr/ppermute | solution.py:15
  99.0 4.6 %collective-permute-done.2 = f32[64,1,8,128]{3,2,0,1:T(8,128)S(1)} collective-permute-done((f32[64,1,8,128]{3,2,0,1:T(8,128)S(1)}, f32[64,1,8,128]{3,2,0,1:T(8,128)S(1)}, u32[]{:S(2)}, u32[]{:S(2)}) %collective-permute-start.2) | collective-permute-done | bytes 262176 | tf_op jit(solution)/shard_map/while/body/eval_jaxpr/ppermute | solution.py:15
  107.6 2.1 collective-permute-start.3
  109.7 4.9 %collective-permute-start.2 = (f32[64,1,8,128]{3,2,0,1:T(8,128)S(1)}, f32[64,1,8,128]{3,2,0,1:T(8,128)S(1)}, u32[]{:S(2)}, u32[]{:S(2)}) collective-permute-start(f32[64,1,8,128]{3,2,0,1:T(8,128)S(1)} %get-tuple-element.427), channel_id=1, source_target_pairs={{0,4},{4,8},{8,12},{12,16},{16,20},{20,24},{24,28},{28,32},{32,36}... | collective-permute-start | bytes 786440 | tf_op jit(solution)/shard_map/while/body/eval_jaxpr/ppermute | solution.py:15
  117.3 3.4 collective-permute-done.2
  122.9 3.2 collective-permute-start.1
  126.1 2.2 collective-permute-start.3
  128.4 4.3 %collective-permute-start.2 = (f32[64,1,8,128]{3,2,0,1:T(8,128)S(1)}, f32[64,1,8,128]{3,2,0,1:T(8,128)S(1)}, u32[]{:S(2)}, u32[]{:S(2)}) collective-permute-start(f32[64,1,8,128]{3,2,0,1:T(8,128)S(1)} %get-tuple-element.427), channel_id=1, source_target_pairs={{0,4},{4,8},{8,12},{12,16},{16,20},{20,24},{24,28},{28,32},{32,36}... | collective-permute-start | bytes 786440 | tf_op jit(solution)/shard_map/while/body/eval_jaxpr/ppermute | solution.py:15
  135.3 4.1 %collective-permute-done.2 = f32[64,1,8,128]{3,2,0,1:T(8,128)S(1)} collective-permute-done((f32[64,1,8,128]{3,2,0,1:T(8,128)S(1)}, f32[64,1,8,128]{3,2,0,1:T(8,128)S(1)}, u32[]{:S(2)}, u32[]{:S(2)}) %collective-permute-start.2) | collective-permute-done | bytes 262176 | tf_op jit(solution)/shard_map/while/body/eval_jaxpr/ppermute | solution.py:15
  141.5 2.3 collective-permute-start.1
  143.8 3.9 %collective-permute-start.3 = (f32[64,1,8]{0,2,1:T(8,128)S(1)}, f32[64,1,8]{0,2,1:T(8,128)S(1)}, u32[]{:S(2)}, u32[]{:S(2)}) collective-permute-start(f32[64,1,8]{0,2,1:T(8,128)S(1)} %get-tuple-element.429), channel_id=1, source_target_pairs={{0,4},{4,8},{8,12},{12,16},{16,20},{20,24},{24,28},{28,32},{32,36}... | collective-permute-start | bytes 6152 | tf_op jit(solution)/shard_map/while/body/eval_jaxpr/ppermute | solution.py:15
  147.7 3.5 %collective-permute-start.2 = (f32[64,1,8,128]{3,2,0,1:T(8,128)S(1)}, f32[64,1,8,128]{3,2,0,1:T(8,128)S(1)}, u32[]{:S(2)}, u32[]{:S(2)}) collective-permute-start(f32[64,1,8,128]{3,2,0,1:T(8,128)S(1)} %get-tuple-element.427), channel_id=1, source_target_pairs={{0,4},{4,8},{8,12},{12,16},{16,20},{20,24},{24,28},{28,32},{32,36}... | collective-permute-start | bytes 786440 | tf_op jit(solution)/shard_map/while/body/eval_jaxpr/ppermute | solution.py:15
  153.8 4.9 %collective-permute-done.2 = f32[64,1,8,128]{3,2,0,1:T(8,128)S(1)} collective-permute-done((f32[64,1,8,128]{3,2,0,1:T(8,128)S(1)}, f32[64,1,8,128]{3,2,0,1:T(8,128)S(1)}, u32[]{:S(2)}, u32[]{:S(2)}) %collective-permute-start.2) | collective-permute-done | bytes 262176 | tf_op jit(solution)/shard_map/while/body/eval_jaxpr/ppermute | solution.py:15
  162.8 2.3 collective-permute-start.3
  165.1 4.6 %collective-permute-start.2 = (f32[64,1,8,128]{3,2,0,1:T(8,128)S(1)}, f32[64,1,8,128]{3,2,0,1:T(8,128)S(1)}, u32[]{:S(2)}, u32[]{:S(2)}) collective-permute-start(f32[64,1,8,128]{3,2,0,1:T(8,128)S(1)} %get-tuple-element.427), channel_id=1, source_target_pairs={{0,4},{4,8},{8,12},{12,16},{16,20},{20,24},{24,28},{28,32},{32,36}... | collective-permute-start | bytes 786440 | tf_op jit(solution)/shard_map/while/body/eval_jaxpr/ppermute | solution.py:15
  172.4 3.8 %collective-permute-done.2 = f32[64,1,8,128]{3,2,0,1:T(8,128)S(1)} collective-permute-done((f32[64,1,8,128]{3,2,0,1:T(8,128)S(1)}, f32[64,1,8,128]{3,2,0,1:T(8,128)S(1)}, u32[]{:S(2)}, u32[]{:S(2)}) %collective-permute-start.2) | collective-permute-done | bytes 262176 | tf_op jit(solution)/shard_map/while/body/eval_jaxpr/ppermute | solution.py:15
  180.2 2.0 collective-permute-start.3
  182.3 6.5 %collective-permute-start.2 = (f32[64,1,8,128]{3,2,0,1:T(8,128)S(1)}, f32[64,1,8,128]{3,2,0,1:T(8,128)S(1)}, u32[]{:S(2)}, u32[]{:S(2)}) collective-permute-start(f32[64,1,8,128]{3,2,0,1:T(8,128)S(1)} %get-tuple-element.427), channel_id=1, source_target_pairs={{0,4},{4,8},{8,12},{12,16},{16,20},{20,24},{24,28},{28,32},{32,36}... | collective-permute-start | bytes 786440 | tf_op jit(solution)/shard_map/while/body/eval_jaxpr/ppermute | solution.py:15
  191.4 2.7 collective-permute-done.2
  198.1 3.5 %collective-permute-start.3 = (f32[64,1,8]{0,2,1:T(8,128)S(1)}, f32[64,1,8]{0,2,1:T(8,128)S(1)}, u32[]{:S(2)}, u32[]{:S(2)}) collective-permute-start(f32[64,1,8]{0,2,1:T(8,128)S(1)} %get-tuple-element.429), channel_id=1, source_target_pairs={{0,4},{4,8},{8,12},{12,16},{16,20},{20,24},{24,28},{28,32},{32,36}... | collective-permute-start | bytes 6152 | tf_op jit(solution)/shard_map/while/body/eval_jaxpr/ppermute | solution.py:15
  201.6 5.5 %collective-permute-start.2 = (f32[64,1,8,128]{3,2,0,1:T(8,128)S(1)}, f32[64,1,8,128]{3,2,0,1:T(8,128)S(1)}, u32[]{:S(2)}, u32[]{:S(2)}) collective-permute-start(f32[64,1,8,128]{3,2,0,1:T(8,128)S(1)} %get-tuple-element.427), channel_id=1, source_target_pairs={{0,4},{4,8},{8,12},{12,16},{16,20},{20,24},{24,28},{28,32},{32,36}... | collective-permute-start | bytes 786440 | tf_op jit(solution)/shard_map/while/body/eval_jaxpr/ppermute | solution.py:15
  209.8 4.8 %collective-permute-done.2 = f32[64,1,8,128]{3,2,0,1:T(8,128)S(1)} collective-permute-done((f32[64,1,8,128]{3,2,0,1:T(8,128)S(1)}, f32[64,1,8,128]{3,2,0,1:T(8,128)S(1)}, u32[]{:S(2)}, u32[]{:S(2)}) %collective-permute-start.2) | collective-permute-done | bytes 262176 | tf_op jit(solution)/shard_map/while/body/eval_jaxpr/ppermute | solution.py:15
  220.5 4.6 %collective-permute-start.2 = (f32[64,1,8,128]{3,2,0,1:T(8,128)S(1)}, f32[64,1,8,128]{3,2,0,1:T(8,128)S(1)}, u32[]{:S(2)}, u32[]{:S(2)}) collective-permute-start(f32[64,1,8,128]{3,2,0,1:T(8,128)S(1)} %get-tuple-element.427), channel_id=1, source_target_pairs={{0,4},{4,8},{8,12},{12,16},{16,20},{20,24},{24,28},{28,32},{32,36}... | collective-permute-start | bytes 786440 | tf_op jit(solution)/shard_map/while/body/eval_jaxpr/ppermute | solution.py:15
  227.8 3.8 %collective-permute-done.2 = f32[64,1,8,128]{3,2,0,1:T(8,128)S(1)} collective-permute-done((f32[64,1,8,128]{3,2,0,1:T(8,128)S(1)}, f32[64,1,8,128]{3,2,0,1:T(8,128)S(1)}, u32[]{:S(2)}, u32[]{:S(2)}) %collective-permute-start.2) | collective-permute-done | bytes 262176 | tf_op jit(solution)/shard_map/while/body/eval_jaxpr/ppermute | solution.py:15
  237.6 4.1 %collective-permute-start.2 = (f32[64,1,8,128]{3,2,0,1:T(8,128)S(1)}, f32[64,1,8,128]{3,2,0,1:T(8,128)S(1)}, u32[]{:S(2)}, u32[]{:S(2)}) collective-permute-start(f32[64,1,8,128]{3,2,0,1:T(8,128)S(1)} %get-tuple-element.427), channel_id=1, source_target_pairs={{0,4},{4,8},{8,12},{12,16},{16,20},{20,24},{24,28},{28,32},{32,36}... | collective-permute-start | bytes 786440 | tf_op jit(solution)/shard_map/while/body/eval_jaxpr/ppermute | solution.py:15
  244.3 4.4 %collective-permute-done.2 = f32[64,1,8,128]{3,2,0,1:T(8,128)S(1)} collective-permute-done((f32[64,1,8,128]{3,2,0,1:T(8,128)S(1)}, f32[64,1,8,128]{3,2,0,1:T(8,128)S(1)}, u32[]{:S(2)}, u32[]{:S(2)}) %collective-permute-start.2) | collective-permute-done | bytes 262176 | tf_op jit(solution)/shard_map/while/body/eval_jaxpr/ppermute | solution.py:15
  252.8 2.3 collective-permute-start.3
  255.1 5.7 %collective-permute-start.2 = (f32[64,1,8,128]{3,2,0,1:T(8,128)S(1)}, f32[64,1,8,128]{3,2,0,1:T(8,128)S(1)}, u32[]{:S(2)}, u32[]{:S(2)}) collective-permute-start(f32[64,1,8,128]{3,2,0,1:T(8,128)S(1)} %get-tuple-element.427), channel_id=1, source_target_pairs={{0,4},{4,8},{8,12},{12,16},{16,20},{20,24},{24,28},{28,32},{32,36}... | collective-permute-start | bytes 786440 | tf_op jit(solution)/shard_map/while/body/eval_jaxpr/ppermute | solution.py:15
  263.4 3.3 collective-permute-done.2
  272.7 6.2 %collective-permute-start.2 = (f32[64,1,8,128]{3,2,0,1:T(8,128)S(1)}, f32[64,1,8,128]{3,2,0,1:T(8,128)S(1)}, u32[]{:S(2)}, u32[]{:S(2)}) collective-permute-start(f32[64,1,8,128]{3,2,0,1:T(8,128)S(1)} %get-tuple-element.427), channel_id=1, source_target_pairs={{0,4},{4,8},{8,12},{12,16},{16,20},{20,24},{24,28},{28,32},{32,36}... | collective-permute-start | bytes 786440 | tf_op jit(solution)/shard_map/while/body/eval_jaxpr/ppermute | solution.py:15
  281.5 3.9 %collective-permute-done.2 = f32[64,1,8,128]{3,2,0,1:T(8,128)S(1)} collective-permute-done((f32[64,1,8,128]{3,2,0,1:T(8,128)S(1)}, f32[64,1,8,128]{3,2,0,1:T(8,128)S(1)}, u32[]{:S(2)}, u32[]{:S(2)}) %collective-permute-start.2) | collective-permute-done | bytes 262176 | tf_op jit(solution)/shard_map/while/body/eval_jaxpr/ppermute | solution.py:15
  290.9 4.9 %collective-permute-done.5 = bf16[64,1,8]{0,2,1:T(8,128)(2,1)S(1)} collective-permute-done((bf16[64,1,8]{0,2,1:T(8,128)(2,1)S(1)}, bf16[64,1,8]{0,2,1:T(8,128)(2,1)S(1)}, u32[]{:S(2)}, u32[]{:S(2)}) %collective-permute-start.5) | collective-permute-done | bytes 1056 | tf_op jit(solution)/shard_map/ppermute | solution.py:15
  296.3 3.1 collective-permute-start.6
  299.5 3.0 collective-permute-done.6
  302.6 41.0 %psum.7 = f32[2,32]{1,0:T(2,128)S(1)} all-reduce(f32[2,32]{1,0:T(2,128)S(1)} %fusion.31), channel_id=1, replica_groups=mesh['section'=8,'cp'=16,'tp'=4] {'tp'}, use_global_device_ids=true, to_apply=%region_9.10 | all-reduce | flops 64 | bytes 512 | tf_op jit(solution)/shard_map/psum | solution.py:112
  (320 shorter events, 120.0 us)
Async XLA Ops:
  11.8 12.9 %collective-permute-start = (bf16[64,1,8,128]{3,0,2,1:T(8,128)(2,1)S(1)}, bf16[64,1,8,128]{3,0,2,1:T(8,128)(2,1)S(1)}, u32[]{:S(2)}, u32[]{:S(2)}) collective-permute-start(bf16[64,1,8,128]{3,0,2,1:T(8,128)(2,1)S(1)} %get-tuple-element.426), channel_id=1, source_target_pairs={{0,4},{4,8},{8,12},{12,16},{16,20},{20,24},{24,28},{28,32},{32,36}... | collective-permute-start | bytes 393224 | tf_op jit(solution)/shard_map/while/body/eval_jaxpr/ppermute | solution.py:15
  15.1 10.3 %collective-permute-start.1 = (f32[64,1,8]{0,2,1:T(8,128)S(1)}, f32[64,1,8]{0,2,1:T(8,128)S(1)}, u32[]{:S(2)}, u32[]{:S(2)}) collective-permute-start(f32[64,1,8]{0,2,1:T(8,128)S(1)} %get-tuple-element.428), channel_id=1, source_target_pairs={{0,4},{4,8},{8,12},{12,16},{16,20},{20,24},{24,28},{28,32},{32,36}... | collective-permute-start | bytes 6152 | tf_op jit(solution)/shard_map/while/body/eval_jaxpr/ppermute | solution.py:15
  21.5 12.1 %collective-permute-start.2 = (f32[64,1,8,128]{3,2,0,1:T(8,128)S(1)}, f32[64,1,8,128]{3,2,0,1:T(8,128)S(1)}, u32[]{:S(2)}, u32[]{:S(2)}) collective-permute-start(f32[64,1,8,128]{3,2,0,1:T(8,128)S(1)} %get-tuple-element.427), channel_id=1, source_target_pairs={{0,4},{4,8},{8,12},{12,16},{16,20},{20,24},{24,28},{28,32},{32,36}... | collective-permute-start | bytes 786440 | tf_op jit(solution)/shard_map/while/body/eval_jaxpr/ppermute | solution.py:15
  33.8 11.6 %collective-permute-start = (bf16[64,1,8,128]{3,0,2,1:T(8,128)(2,1)S(1)}, bf16[64,1,8,128]{3,0,2,1:T(8,128)(2,1)S(1)}, u32[]{:S(2)}, u32[]{:S(2)}) collective-permute-start(bf16[64,1,8,128]{3,0,2,1:T(8,128)(2,1)S(1)} %get-tuple-element.426), channel_id=1, source_target_pairs={{0,4},{4,8},{8,12},{12,16},{16,20},{20,24},{24,28},{28,32},{32,36}... | collective-permute-start | bytes 393224 | tf_op jit(solution)/shard_map/while/body/eval_jaxpr/ppermute | solution.py:15
  35.8 10.4 %collective-permute-start.1 = (f32[64,1,8]{0,2,1:T(8,128)S(1)}, f32[64,1,8]{0,2,1:T(8,128)S(1)}, u32[]{:S(2)}, u32[]{:S(2)}) collective-permute-start(f32[64,1,8]{0,2,1:T(8,128)S(1)} %get-tuple-element.428), channel_id=1, source_target_pairs={{0,4},{4,8},{8,12},{12,16},{16,20},{20,24},{24,28},{28,32},{32,36}... | collective-permute-start | bytes 6152 | tf_op jit(solution)/shard_map/while/body/eval_jaxpr/ppermute | solution.py:15
  37.7 10.0 %collective-permute-start.3 = (f32[64,1,8]{0,2,1:T(8,128)S(1)}, f32[64,1,8]{0,2,1:T(8,128)S(1)}, u32[]{:S(2)}, u32[]{:S(2)}) collective-permute-start(f32[64,1,8]{0,2,1:T(8,128)S(1)} %get-tuple-element.429), channel_id=1, source_target_pairs={{0,4},{4,8},{8,12},{12,16},{16,20},{20,24},{24,28},{28,32},{32,36}... | collective-permute-start | bytes 6152 | tf_op jit(solution)/shard_map/while/body/eval_jaxpr/ppermute | solution.py:15
  39.6 11.1 %collective-permute-start.2 = (f32[64,1,8,128]{3,2,0,1:T(8,128)S(1)}, f32[64,1,8,128]{3,2,0,1:T(8,128)S(1)}, u32[]{:S(2)}, u32[]{:S(2)}) collective-permute-start(f32[64,1,8,128]{3,2,0,1:T(8,128)S(1)} %get-tuple-element.427), channel_id=1, source_target_pairs={{0,4},{4,8},{8,12},{12,16},{16,20},{20,24},{24,28},{28,32},{32,36}... | collective-permute-start | bytes 786440 | tf_op jit(solution)/shard_map/while/body/eval_jaxpr/ppermute | solution.py:15
  50.9 11.1 %collective-permute-start = (bf16[64,1,8,128]{3,0,2,1:T(8,128)(2,1)S(1)}, bf16[64,1,8,128]{3,0,2,1:T(8,128)(2,1)S(1)}, u32[]{:S(2)}, u32[]{:S(2)}) collective-permute-start(bf16[64,1,8,128]{3,0,2,1:T(8,128)(2,1)S(1)} %get-tuple-element.426), channel_id=1, source_target_pairs={{0,4},{4,8},{8,12},{12,16},{16,20},{20,24},{24,28},{28,32},{32,36}... | collective-permute-start | bytes 393224 | tf_op jit(solution)/shard_map/while/body/eval_jaxpr/ppermute | solution.py:15
  56.7 11.1 %collective-permute-start.2 = (f32[64,1,8,128]{3,2,0,1:T(8,128)S(1)}, f32[64,1,8,128]{3,2,0,1:T(8,128)S(1)}, u32[]{:S(2)}, u32[]{:S(2)}) collective-permute-start(f32[64,1,8,128]{3,2,0,1:T(8,128)S(1)} %get-tuple-element.427), channel_id=1, source_target_pairs={{0,4},{4,8},{8,12},{12,16},{16,20},{20,24},{24,28},{28,32},{32,36}... | collective-permute-start | bytes 786440 | tf_op jit(solution)/shard_map/while/body/eval_jaxpr/ppermute | solution.py:15
  67.9 11.1 %collective-permute-start = (bf16[64,1,8,128]{3,0,2,1:T(8,128)(2,1)S(1)}, bf16[64,1,8,128]{3,0,2,1:T(8,128)(2,1)S(1)}, u32[]{:S(2)}, u32[]{:S(2)}) collective-permute-start(bf16[64,1,8,128]{3,0,2,1:T(8,128)(2,1)S(1)} %get-tuple-element.426), channel_id=1, source_target_pairs={{0,4},{4,8},{8,12},{12,16},{16,20},{20,24},{24,28},{28,32},{32,36}... | collective-permute-start | bytes 393224 | tf_op jit(solution)/shard_map/while/body/eval_jaxpr/ppermute | solution.py:15
  69.9 9.9 %collective-permute-start.1 = (f32[64,1,8]{0,2,1:T(8,128)S(1)}, f32[64,1,8]{0,2,1:T(8,128)S(1)}, u32[]{:S(2)}, u32[]{:S(2)}) collective-permute-start(f32[64,1,8]{0,2,1:T(8,128)S(1)} %get-tuple-element.428), channel_id=1, source_target_pairs={{0,4},{4,8},{8,12},{12,16},{16,20},{20,24},{24,28},{28,32},{32,36}... | collective-permute-start | bytes 6152 | tf_op jit(solution)/shard_map/while/body/eval_jaxpr/ppermute | solution.py:15
  74.1 12.1 %collective-permute-start.2 = (f32[64,1,8,128]{3,2,0,1:T(8,128)S(1)}, f32[64,1,8,128]{3,2,0,1:T(8,128)S(1)}, u32[]{:S(2)}, u32[]{:S(2)}) collective-permute-start(f32[64,1,8,128]{3,2,0,1:T(8,128)S(1)} %get-tuple-element.427), channel_id=1, source_target_pairs={{0,4},{4,8},{8,12},{12,16},{16,20},{20,24},{24,28},{28,32},{32,36}... | collective-permute-start | bytes 786440 | tf_op jit(solution)/shard_map/while/body/eval_jaxpr/ppermute | solution.py:15
  86.5 10.3 %collective-permute-start = (bf16[64,1,8,128]{3,0,2,1:T(8,128)(2,1)S(1)}, bf16[64,1,8,128]{3,0,2,1:T(8,128)(2,1)S(1)}, u32[]{:S(2)}, u32[]{:S(2)}) collective-permute-start(bf16[64,1,8,128]{3,0,2,1:T(8,128)(2,1)S(1)} %get-tuple-element.426), channel_id=1, source_target_pairs={{0,4},{4,8},{8,12},{12,16},{16,20},{20,24},{24,28},{28,32},{32,36}... | collective-permute-start | bytes 393224 | tf_op jit(solution)/shard_map/while/body/eval_jaxpr/ppermute | solution.py:15
  92.2 11.3 %collective-permute-start.2 = (f32[64,1,8,128]{3,2,0,1:T(8,128)S(1)}, f32[64,1,8,128]{3,2,0,1:T(8,128)S(1)}, u32[]{:S(2)}, u32[]{:S(2)}) collective-permute-start(f32[64,1,8,128]{3,2,0,1:T(8,128)S(1)} %get-tuple-element.427), channel_id=1, source_target_pairs={{0,4},{4,8},{8,12},{12,16},{16,20},{20,24},{24,28},{28,32},{32,36}... | collective-permute-start | bytes 786440 | tf_op jit(solution)/shard_map/while/body/eval_jaxpr/ppermute | solution.py:15
  103.8 11.2 %collective-permute-start = (bf16[64,1,8,128]{3,0,2,1:T(8,128)(2,1)S(1)}, bf16[64,1,8,128]{3,0,2,1:T(8,128)(2,1)S(1)}, u32[]{:S(2)}, u32[]{:S(2)}) collective-permute-start(bf16[64,1,8,128]{3,0,2,1:T(8,128)(2,1)S(1)} %get-tuple-element.426), channel_id=1, source_target_pairs={{0,4},{4,8},{8,12},{12,16},{16,20},{20,24},{24,28},{28,32},{32,36}... | collective-permute-start | bytes 393224 | tf_op jit(solution)/shard_map/while/body/eval_jaxpr/ppermute | solution.py:15
  105.7 10.0 %collective-permute-start.1 = (f32[64,1,8]{0,2,1:T(8,128)S(1)}, f32[64,1,8]{0,2,1:T(8,128)S(1)}, u32[]{:S(2)}, u32[]{:S(2)}) collective-permute-start(f32[64,1,8]{0,2,1:T(8,128)S(1)} %get-tuple-element.428), channel_id=1, source_target_pairs={{0,4},{4,8},{8,12},{12,16},{16,20},{20,24},{24,28},{28,32},{32,36}... | collective-permute-start | bytes 6152 | tf_op jit(solution)/shard_map/while/body/eval_jaxpr/ppermute | solution.py:15
  109.7 11.0 %collective-permute-start.2 = (f32[64,1,8,128]{3,2,0,1:T(8,128)S(1)}, f32[64,1,8,128]{3,2,0,1:T(8,128)S(1)}, u32[]{:S(2)}, u32[]{:S(2)}) collective-permute-start(f32[64,1,8,128]{3,2,0,1:T(8,128)S(1)} %get-tuple-element.427), channel_id=1, source_target_pairs={{0,4},{4,8},{8,12},{12,16},{16,20},{20,24},{24,28},{28,32},{32,36}... | collective-permute-start | bytes 786440 | tf_op jit(solution)/shard_map/while/body/eval_jaxpr/ppermute | solution.py:15
  121.0 12.1 %collective-permute-start = (bf16[64,1,8,128]{3,0,2,1:T(8,128)(2,1)S(1)}, bf16[64,1,8,128]{3,0,2,1:T(8,128)(2,1)S(1)}, u32[]{:S(2)}, u32[]{:S(2)}) collective-permute-start(bf16[64,1,8,128]{3,0,2,1:T(8,128)(2,1)S(1)} %get-tuple-element.426), channel_id=1, source_target_pairs={{0,4},{4,8},{8,12},{12,16},{16,20},{20,24},{24,28},{28,32},{32,36}... | collective-permute-start | bytes 393224 | tf_op jit(solution)/shard_map/while/body/eval_jaxpr/ppermute | solution.py:15
  122.9 10.9 %collective-permute-start.1 = (f32[64,1,8]{0,2,1:T(8,128)S(1)}, f32[64,1,8]{0,2,1:T(8,128)S(1)}, u32[]{:S(2)}, u32[]{:S(2)}) collective-permute-start(f32[64,1,8]{0,2,1:T(8,128)S(1)} %get-tuple-element.428), channel_id=1, source_target_pairs={{0,4},{4,8},{8,12},{12,16},{16,20},{20,24},{24,28},{28,32},{32,36}... | collective-permute-start | bytes 6152 | tf_op jit(solution)/shard_map/while/body/eval_jaxpr/ppermute | solution.py:15
  128.4 11.0 %collective-permute-start.2 = (f32[64,1,8,128]{3,2,0,1:T(8,128)S(1)}, f32[64,1,8,128]{3,2,0,1:T(8,128)S(1)}, u32[]{:S(2)}, u32[]{:S(2)}) collective-permute-start(f32[64,1,8,128]{3,2,0,1:T(8,128)S(1)} %get-tuple-element.427), channel_id=1, source_target_pairs={{0,4},{4,8},{8,12},{12,16},{16,20},{20,24},{24,28},{28,32},{32,36}... | collective-permute-start | bytes 786440 | tf_op jit(solution)/shard_map/while/body/eval_jaxpr/ppermute | solution.py:15
  139.6 11.9 %collective-permute-start = (bf16[64,1,8,128]{3,0,2,1:T(8,128)(2,1)S(1)}, bf16[64,1,8,128]{3,0,2,1:T(8,128)(2,1)S(1)}, u32[]{:S(2)}, u32[]{:S(2)}) collective-permute-start(bf16[64,1,8,128]{3,0,2,1:T(8,128)(2,1)S(1)} %get-tuple-element.426), channel_id=1, source_target_pairs={{0,4},{4,8},{8,12},{12,16},{16,20},{20,24},{24,28},{28,32},{32,36}... | collective-permute-start | bytes 393224 | tf_op jit(solution)/shard_map/while/body/eval_jaxpr/ppermute | solution.py:15
  141.5 10.7 %collective-permute-start.1 = (f32[64,1,8]{0,2,1:T(8,128)S(1)}, f32[64,1,8]{0,2,1:T(8,128)S(1)}, u32[]{:S(2)}, u32[]{:S(2)}) collective-permute-start(f32[64,1,8]{0,2,1:T(8,128)S(1)} %get-tuple-element.428), channel_id=1, source_target_pairs={{0,4},{4,8},{8,12},{12,16},{16,20},{20,24},{24,28},{28,32},{32,36}... | collective-permute-start | bytes 6152 | tf_op jit(solution)/shard_map/while/body/eval_jaxpr/ppermute | solution.py:15
  143.8 10.0 %collective-permute-start.3 = (f32[64,1,8]{0,2,1:T(8,128)S(1)}, f32[64,1,8]{0,2,1:T(8,128)S(1)}, u32[]{:S(2)}, u32[]{:S(2)}) collective-permute-start(f32[64,1,8]{0,2,1:T(8,128)S(1)} %get-tuple-element.429), channel_id=1, source_target_pairs={{0,4},{4,8},{8,12},{12,16},{16,20},{20,24},{24,28},{28,32},{32,36}... | collective-permute-start | bytes 6152 | tf_op jit(solution)/shard_map/while/body/eval_jaxpr/ppermute | solution.py:15
  147.7 11.0 %collective-permute-start.2 = (f32[64,1,8,128]{3,2,0,1:T(8,128)S(1)}, f32[64,1,8,128]{3,2,0,1:T(8,128)S(1)}, u32[]{:S(2)}, u32[]{:S(2)}) collective-permute-start(f32[64,1,8,128]{3,2,0,1:T(8,128)S(1)} %get-tuple-element.427), channel_id=1, source_target_pairs={{0,4},{4,8},{8,12},{12,16},{16,20},{20,24},{24,28},{28,32},{32,36}... | collective-permute-start | bytes 786440 | tf_op jit(solution)/shard_map/while/body/eval_jaxpr/ppermute | solution.py:15
  159.0 11.1 %collective-permute-start = (bf16[64,1,8,128]{3,0,2,1:T(8,128)(2,1)S(1)}, bf16[64,1,8,128]{3,0,2,1:T(8,128)(2,1)S(1)}, u32[]{:S(2)}, u32[]{:S(2)}) collective-permute-start(bf16[64,1,8,128]{3,0,2,1:T(8,128)(2,1)S(1)} %get-tuple-element.426), channel_id=1, source_target_pairs={{0,4},{4,8},{8,12},{12,16},{16,20},{20,24},{24,28},{28,32},{32,36}... | collective-permute-start | bytes 393224 | tf_op jit(solution)/shard_map/while/body/eval_jaxpr/ppermute | solution.py:15
  160.9 9.9 %collective-permute-start.1 = (f32[64,1,8]{0,2,1:T(8,128)S(1)}, f32[64,1,8]{0,2,1:T(8,128)S(1)}, u32[]{:S(2)}, u32[]{:S(2)}) collective-permute-start(f32[64,1,8]{0,2,1:T(8,128)S(1)} %get-tuple-element.428), channel_id=1, source_target_pairs={{0,4},{4,8},{8,12},{12,16},{16,20},{20,24},{24,28},{28,32},{32,36}... | collective-permute-start | bytes 6152 | tf_op jit(solution)/shard_map/while/body/eval_jaxpr/ppermute | solution.py:15
  165.1 11.0 %collective-permute-start.2 = (f32[64,1,8,128]{3,2,0,1:T(8,128)S(1)}, f32[64,1,8,128]{3,2,0,1:T(8,128)S(1)}, u32[]{:S(2)}, u32[]{:S(2)}) collective-permute-start(f32[64,1,8,128]{3,2,0,1:T(8,128)S(1)} %get-tuple-element.427), channel_id=1, source_target_pairs={{0,4},{4,8},{8,12},{12,16},{16,20},{20,24},{24,28},{28,32},{32,36}... | collective-permute-start | bytes 786440 | tf_op jit(solution)/shard_map/while/body/eval_jaxpr/ppermute | solution.py:15
  176.4 12.7 %collective-permute-start = (bf16[64,1,8,128]{3,0,2,1:T(8,128)(2,1)S(1)}, bf16[64,1,8,128]{3,0,2,1:T(8,128)(2,1)S(1)}, u32[]{:S(2)}, u32[]{:S(2)}) collective-permute-start(bf16[64,1,8,128]{3,0,2,1:T(8,128)(2,1)S(1)} %get-tuple-element.426), channel_id=1, source_target_pairs={{0,4},{4,8},{8,12},{12,16},{16,20},{20,24},{24,28},{28,32},{32,36}... | collective-permute-start | bytes 393224 | tf_op jit(solution)/shard_map/while/body/eval_jaxpr/ppermute | solution.py:15
  178.3 11.5 %collective-permute-start.1 = (f32[64,1,8]{0,2,1:T(8,128)S(1)}, f32[64,1,8]{0,2,1:T(8,128)S(1)}, u32[]{:S(2)}, u32[]{:S(2)}) collective-permute-start(f32[64,1,8]{0,2,1:T(8,128)S(1)} %get-tuple-element.428), channel_id=1, source_target_pairs={{0,4},{4,8},{8,12},{12,16},{16,20},{20,24},{24,28},{28,32},{32,36}... | collective-permute-start | bytes 6152 | tf_op jit(solution)/shard_map/while/body/eval_jaxpr/ppermute | solution.py:15
  180.2 11.2 %collective-permute-start.3 = (f32[64,1,8]{0,2,1:T(8,128)S(1)}, f32[64,1,8]{0,2,1:T(8,128)S(1)}, u32[]{:S(2)}, u32[]{:S(2)}) collective-permute-start(f32[64,1,8]{0,2,1:T(8,128)S(1)} %get-tuple-element.429), channel_id=1, source_target_pairs={{0,4},{4,8},{8,12},{12,16},{16,20},{20,24},{24,28},{28,32},{32,36}... | collective-permute-start | bytes 6152 | tf_op jit(solution)/shard_map/while/body/eval_jaxpr/ppermute | solution.py:15
  182.3 11.8 %collective-permute-start.2 = (f32[64,1,8,128]{3,2,0,1:T(8,128)S(1)}, f32[64,1,8,128]{3,2,0,1:T(8,128)S(1)}, u32[]{:S(2)}, u32[]{:S(2)}) collective-permute-start(f32[64,1,8,128]{3,2,0,1:T(8,128)S(1)} %get-tuple-element.427), channel_id=1, source_target_pairs={{0,4},{4,8},{8,12},{12,16},{16,20},{20,24},{24,28},{28,32},{32,36}... | collective-permute-start | bytes 786440 | tf_op jit(solution)/shard_map/while/body/eval_jaxpr/ppermute | solution.py:15
  194.3 13.2 %collective-permute-start = (bf16[64,1,8,128]{3,0,2,1:T(8,128)(2,1)S(1)}, bf16[64,1,8,128]{3,0,2,1:T(8,128)(2,1)S(1)}, u32[]{:S(2)}, u32[]{:S(2)}) collective-permute-start(bf16[64,1,8,128]{3,0,2,1:T(8,128)(2,1)S(1)} %get-tuple-element.426), channel_id=1, source_target_pairs={{0,4},{4,8},{8,12},{12,16},{16,20},{20,24},{24,28},{28,32},{32,36}... | collective-permute-start | bytes 393224 | tf_op jit(solution)/shard_map/while/body/eval_jaxpr/ppermute | solution.py:15
  196.2 12.0 %collective-permute-start.1 = (f32[64,1,8]{0,2,1:T(8,128)S(1)}, f32[64,1,8]{0,2,1:T(8,128)S(1)}, u32[]{:S(2)}, u32[]{:S(2)}) collective-permute-start(f32[64,1,8]{0,2,1:T(8,128)S(1)} %get-tuple-element.428), channel_id=1, source_target_pairs={{0,4},{4,8},{8,12},{12,16},{16,20},{20,24},{24,28},{28,32},{32,36}... | collective-permute-start | bytes 6152 | tf_op jit(solution)/shard_map/while/body/eval_jaxpr/ppermute | solution.py:15
  198.1 11.6 %collective-permute-start.3 = (f32[64,1,8]{0,2,1:T(8,128)S(1)}, f32[64,1,8]{0,2,1:T(8,128)S(1)}, u32[]{:S(2)}, u32[]{:S(2)}) collective-permute-start(f32[64,1,8]{0,2,1:T(8,128)S(1)} %get-tuple-element.429), channel_id=1, source_target_pairs={{0,4},{4,8},{8,12},{12,16},{16,20},{20,24},{24,28},{28,32},{32,36}... | collective-permute-start | bytes 6152 | tf_op jit(solution)/shard_map/while/body/eval_jaxpr/ppermute | solution.py:15
  201.6 12.9 %collective-permute-start.2 = (f32[64,1,8,128]{3,2,0,1:T(8,128)S(1)}, f32[64,1,8,128]{3,2,0,1:T(8,128)S(1)}, u32[]{:S(2)}, u32[]{:S(2)}) collective-permute-start(f32[64,1,8,128]{3,2,0,1:T(8,128)S(1)} %get-tuple-element.427), channel_id=1, source_target_pairs={{0,4},{4,8},{8,12},{12,16},{16,20},{20,24},{24,28},{28,32},{32,36}... | collective-permute-start | bytes 786440 | tf_op jit(solution)/shard_map/while/body/eval_jaxpr/ppermute | solution.py:15
  214.7 10.7 %collective-permute-start = (bf16[64,1,8,128]{3,0,2,1:T(8,128)(2,1)S(1)}, bf16[64,1,8,128]{3,0,2,1:T(8,128)(2,1)S(1)}, u32[]{:S(2)}, u32[]{:S(2)}) collective-permute-start(bf16[64,1,8,128]{3,0,2,1:T(8,128)(2,1)S(1)} %get-tuple-element.426), channel_id=1, source_target_pairs={{0,4},{4,8},{8,12},{12,16},{16,20},{20,24},{24,28},{28,32},{32,36}... | collective-permute-start | bytes 393224 | tf_op jit(solution)/shard_map/while/body/eval_jaxpr/ppermute | solution.py:15
  220.5 11.1 %collective-permute-start.2 = (f32[64,1,8,128]{3,2,0,1:T(8,128)S(1)}, f32[64,1,8,128]{3,2,0,1:T(8,128)S(1)}, u32[]{:S(2)}, u32[]{:S(2)}) collective-permute-start(f32[64,1,8,128]{3,2,0,1:T(8,128)S(1)} %get-tuple-element.427), channel_id=1, source_target_pairs={{0,4},{4,8},{8,12},{12,16},{16,20},{20,24},{24,28},{28,32},{32,36}... | collective-permute-start | bytes 786440 | tf_op jit(solution)/shard_map/while/body/eval_jaxpr/ppermute | solution.py:15
  231.8 10.2 %collective-permute-start = (bf16[64,1,8,128]{3,0,2,1:T(8,128)(2,1)S(1)}, bf16[64,1,8,128]{3,0,2,1:T(8,128)(2,1)S(1)}, u32[]{:S(2)}, u32[]{:S(2)}) collective-permute-start(bf16[64,1,8,128]{3,0,2,1:T(8,128)(2,1)S(1)} %get-tuple-element.426), channel_id=1, source_target_pairs={{0,4},{4,8},{8,12},{12,16},{16,20},{20,24},{24,28},{28,32},{32,36}... | collective-permute-start | bytes 393224 | tf_op jit(solution)/shard_map/while/body/eval_jaxpr/ppermute | solution.py:15
  237.6 11.1 %collective-permute-start.2 = (f32[64,1,8,128]{3,2,0,1:T(8,128)S(1)}, f32[64,1,8,128]{3,2,0,1:T(8,128)S(1)}, u32[]{:S(2)}, u32[]{:S(2)}) collective-permute-start(f32[64,1,8,128]{3,2,0,1:T(8,128)S(1)} %get-tuple-element.427), channel_id=1, source_target_pairs={{0,4},{4,8},{8,12},{12,16},{16,20},{20,24},{24,28},{28,32},{32,36}... | collective-permute-start | bytes 786440 | tf_op jit(solution)/shard_map/while/body/eval_jaxpr/ppermute | solution.py:15
  248.9 12.2 %collective-permute-start = (bf16[64,1,8,128]{3,0,2,1:T(8,128)(2,1)S(1)}, bf16[64,1,8,128]{3,0,2,1:T(8,128)(2,1)S(1)}, u32[]{:S(2)}, u32[]{:S(2)}) collective-permute-start(bf16[64,1,8,128]{3,0,2,1:T(8,128)(2,1)S(1)} %get-tuple-element.426), channel_id=1, source_target_pairs={{0,4},{4,8},{8,12},{12,16},{16,20},{20,24},{24,28},{28,32},{32,36}... | collective-permute-start | bytes 393224 | tf_op jit(solution)/shard_map/while/body/eval_jaxpr/ppermute | solution.py:15
  250.8 11.0 %collective-permute-start.1 = (f32[64,1,8]{0,2,1:T(8,128)S(1)}, f32[64,1,8]{0,2,1:T(8,128)S(1)}, u32[]{:S(2)}, u32[]{:S(2)}) collective-permute-start(f32[64,1,8]{0,2,1:T(8,128)S(1)} %get-tuple-element.428), channel_id=1, source_target_pairs={{0,4},{4,8},{8,12},{12,16},{16,20},{20,24},{24,28},{28,32},{32,36}... | collective-permute-start | bytes 6152 | tf_op jit(solution)/shard_map/while/body/eval_jaxpr/ppermute | solution.py:15
  252.8 10.6 %collective-permute-start.3 = (f32[64,1,8]{0,2,1:T(8,128)S(1)}, f32[64,1,8]{0,2,1:T(8,128)S(1)}, u32[]{:S(2)}, u32[]{:S(2)}) collective-permute-start(f32[64,1,8]{0,2,1:T(8,128)S(1)} %get-tuple-element.429), channel_id=1, source_target_pairs={{0,4},{4,8},{8,12},{12,16},{16,20},{20,24},{24,28},{28,32},{32,36}... | collective-permute-start | bytes 6152 | tf_op jit(solution)/shard_map/while/body/eval_jaxpr/ppermute | solution.py:15
  255.1 11.7 %collective-permute-start.2 = (f32[64,1,8,128]{3,2,0,1:T(8,128)S(1)}, f32[64,1,8,128]{3,2,0,1:T(8,128)S(1)}, u32[]{:S(2)}, u32[]{:S(2)}) collective-permute-start(f32[64,1,8,128]{3,2,0,1:T(8,128)S(1)} %get-tuple-element.427), channel_id=1, source_target_pairs={{0,4},{4,8},{8,12},{12,16},{16,20},{20,24},{24,28},{28,32},{32,36}... | collective-permute-start | bytes 786440 | tf_op jit(solution)/shard_map/while/body/eval_jaxpr/ppermute | solution.py:15
  266.9 12.3 %collective-permute-start = (bf16[64,1,8,128]{3,0,2,1:T(8,128)(2,1)S(1)}, bf16[64,1,8,128]{3,0,2,1:T(8,128)(2,1)S(1)}, u32[]{:S(2)}, u32[]{:S(2)}) collective-permute-start(bf16[64,1,8,128]{3,0,2,1:T(8,128)(2,1)S(1)} %get-tuple-element.426), channel_id=1, source_target_pairs={{0,4},{4,8},{8,12},{12,16},{16,20},{20,24},{24,28},{28,32},{32,36}... | collective-permute-start | bytes 393224 | tf_op jit(solution)/shard_map/while/body/eval_jaxpr/ppermute | solution.py:15
  268.9 11.1 %collective-permute-start.1 = (f32[64,1,8]{0,2,1:T(8,128)S(1)}, f32[64,1,8]{0,2,1:T(8,128)S(1)}, u32[]{:S(2)}, u32[]{:S(2)}) collective-permute-start(f32[64,1,8]{0,2,1:T(8,128)S(1)} %get-tuple-element.428), channel_id=1, source_target_pairs={{0,4},{4,8},{8,12},{12,16},{16,20},{20,24},{24,28},{28,32},{32,36}... | collective-permute-start | bytes 6152 | tf_op jit(solution)/shard_map/while/body/eval_jaxpr/ppermute | solution.py:15
  270.8 10.7 %collective-permute-start.3 = (f32[64,1,8]{0,2,1:T(8,128)S(1)}, f32[64,1,8]{0,2,1:T(8,128)S(1)}, u32[]{:S(2)}, u32[]{:S(2)}) collective-permute-start(f32[64,1,8]{0,2,1:T(8,128)S(1)} %get-tuple-element.429), channel_id=1, source_target_pairs={{0,4},{4,8},{8,12},{12,16},{16,20},{20,24},{24,28},{28,32},{32,36}... | collective-permute-start | bytes 6152 | tf_op jit(solution)/shard_map/while/body/eval_jaxpr/ppermute | solution.py:15
  272.7 12.7 %collective-permute-start.2 = (f32[64,1,8,128]{3,2,0,1:T(8,128)S(1)}, f32[64,1,8,128]{3,2,0,1:T(8,128)S(1)}, u32[]{:S(2)}, u32[]{:S(2)}) collective-permute-start(f32[64,1,8,128]{3,2,0,1:T(8,128)S(1)} %get-tuple-element.427), channel_id=1, source_target_pairs={{0,4},{4,8},{8,12},{12,16},{16,20},{20,24},{24,28},{28,32},{32,36}... | collective-permute-start | bytes 786440 | tf_op jit(solution)/shard_map/while/body/eval_jaxpr/ppermute | solution.py:15
  285.7 10.3 %collective-permute-start.4 = (bf16[64,1,8,128]{3,2,0,1:T(8,128)(2,1)S(1)}, bf16[64,1,8,128]{3,2,0,1:T(8,128)(2,1)S(1)}, u32[]{:S(2)}, u32[]{:S(2)}) collective-permute-start(bf16[64,1,8,128]{3,2,0,1:T(8,128)(2,1)S(1)} %convert_element_type.64), channel_id=1, source_target_pairs={{0,4},{4,8},{8,12},{12,16},{16,20},{20,24},{24,28},{28,32},{32,36}... | collective-permute-start | bytes 393224 | tf_op jit(solution)/shard_map/ppermute | solution.py:15
  (20 other events, 1000.6 us)
where the time goes:
time: 347 us; the launch traced here: 345 us
  starting transfers between devices  176 us (51%)
  waiting for transfers between devices  69.7 us (20%)
  blocking collectives  41 us (12%)
  other arithmetic  26.1 us (8%)
  matrix products  22.8 us (7%)
  local copies, waits for them, and re-layouts  5.61 us (2%)
    ppermute x62, starting transfers between devices, passed_along(): lax.ppermute(shard, axis, [(i, (i + by) % length) for i in range(length)])  173 us
    ppermute x62, waiting for transfers between devices, passed_along(): lax.ppermute(shard, axis, [(i, (i + by) % length) for i in range(length)])  66.7 us
    psum x1, blocking collectives, body(): squares = lax.psum(jnp.sum(row_sums * row_sums, axis=-1), 'tp')  41 us
    dot_general x16, matrix products, update(): jnp.einsum('rgjd,ngd->rgjn', query_block, key_heads, preferred_element_ty...  12.5 us
    reduce_sum x16, other arithmetic, update(): totals = totals * rescale + jnp.sum(weights, axis=-1)  12.1 us
    dot_general x16, matrix products, update(): jnp.einsum('rgjn,ngd->rgjd', weights.astype(jnp.bfloat16), value_heads, p...  10.3 us
  transfers between devices with their start and end apart: 63, of which 17 were waited for; matrix products, arithmetic and copies ran while one was open for 11% of the time, Pallas kernels for 0%

commit v1 on v0

v1 whole, which is shorter than its diff:
```python
import functools

import jax
import jax.numpy as jnp
import numpy as np
from jax import lax
from jax.experimental import pallas as pl
from jax.experimental.pallas import tpu as pltpu
from jax.sharding import Mesh
from jax.sharding import PartitionSpec as P

HD = 128
NX, NY = 4, 4
HEADS_DEV = 8
ROWS = 32
WIDTH_DEV = HEADS_DEV * HD
KEYS = 1536
CTX = KEYS * NX * NY
N_SEG = 9
FULL_WIDTH = 4096
PACKED = WIDTH_DEV + 128
TILE = 512
NEGATIVE = -1e30
EPSILON = 1e-05
LOG2_SCALE = float(np.log2(np.e) / np.sqrt(HD))
VMEM_LIMIT = 56 * 2**20


def segment_of(tick):
    return 7 - lax.axis_index("section") + tick


def segment_start(lengths_ref, segment):
    start = jnp.int32(CTX)
    for j in range(N_SEG):
        start = start - jnp.where(j >= segment, lengths_ref[j], 0)
    return start


def attend_kernel(tick, lengths_ref, q_ref, k_ref, v_ref, o_ref):
    cx = lax.axis_index("cx")
    cy = lax.axis_index("cy")
    start = segment_start(lengths_ref, segment_of(tick))
    q = jnp.concatenate(
        [q_ref[j, :, h * HD : (h + 1) * HD] for j in range(NY) for h in range(HEADS_DEV)], 0
    )
    rows = q.shape[0]
    row_id = lax.broadcasted_iota(jnp.int32, (rows, 1), 0)
    per_owner = HEADS_DEV * ROWS
    in_segment = (cx * NY + row_id // per_owner) * ROWS + row_id % ROWS
    last_offset = start + in_segment - ((NX - 1) * NY + cy) * KEYS

    top = out = total = None
    for c in range(NX):
        for t in range(KEYS // TILE):
            kt = k_ref[c, t * TILE : (t + 1) * TILE, :]
            vt = v_ref[c, t * TILE : (t + 1) * TILE, :]
            s = lax.dot_general(q, kt, (((1,), (1,)), ((), ())), preferred_element_type=jnp.float32)
            if c == NX - 1:
                offset = t * TILE + lax.broadcasted_iota(jnp.int32, (1, TILE), 1)
                s = jnp.where(offset <= last_offset, s, NEGATIVE)
            part = s[:, :HD]
            for u in range(1, TILE // HD):
                part = jnp.maximum(part, s[:, u * HD : (u + 1) * HD])
            tile_top = jnp.max(part, axis=1, keepdims=True) * LOG2_SCALE
            new_top = tile_top if top is None else jnp.maximum(top, tile_top)
            p = jnp.exp2(s * LOG2_SCALE - new_top)
            lane_sum = p[:, :HD]
            for u in range(1, TILE // HD):
                lane_sum = lane_sum + p[:, u * HD : (u + 1) * HD]
            mixed = jnp.dot(p.astype(jnp.bfloat16), vt, preferred_element_type=jnp.float32)
            if top is None:
                out, total = mixed, lane_sum
            else:
                rescale = jnp.exp2(top - new_top)
                out = out * rescale + mixed
                total = total * rescale + lane_sum
            top = new_top
    total = jnp.sum(total, axis=1, keepdims=True)
    out = (out / total).astype(jnp.bfloat16)
    level = top + jnp.log2(total)

    lane = lax.broadcasted_iota(jnp.int32, (ROWS, 128), 1)
    for j in range(NY):
        packed = jnp.zeros((ROWS, 128), jnp.float32)
        for h in range(HEADS_DEV):
            at = (j * HEADS_DEV + h) * ROWS
            o_ref[j, :, h * HD : (h + 1) * HD] = out[at : at + ROWS]
            packed = jnp.where(lane % HEADS_DEV == h, level[at : at + ROWS], packed)
        high = packed.astype(jnp.bfloat16).astype(jnp.float32)
        middle = (packed - high).astype(jnp.bfloat16).astype(jnp.float32)
        low = packed - high - middle
        pieces = jnp.where(
            lane < HEADS_DEV,
            high,
            jnp.where(lane < 2 * HEADS_DEV, middle, jnp.where(lane < 3 * HEADS_DEV, low, 0.0)),
        )
        o_ref[j, :, WIDTH_DEV:] = pieces.astype(jnp.bfloat16)


def attend(tick, lengths, q_all, k_all, v_all):
    return pl.pallas_call(
        functools.partial(attend_kernel, tick),
        grid=(1,),
        in_specs=[
            pl.BlockSpec(memory_space=pltpu.SMEM),
            pl.BlockSpec((NY, None, ROWS, WIDTH_DEV), lambda i: (0, tick, 0, 0)),
            pl.BlockSpec((NX, KEYS, HD), lambda i: (0, 0, 0)),
            pl.BlockSpec((NX, KEYS, HD), lambda i: (0, 0, 0)),
        ],
        out_specs=pl.BlockSpec((NY, ROWS, PACKED), lambda i: (0, 0, 0)),
        out_shape=jax.ShapeDtypeStruct((NY, ROWS, PACKED), jnp.bfloat16),
        compiler_params=pltpu.CompilerParams(vmem_limit_bytes=VMEM_LIMIT),
        name=f"attend_{tick}",
    )(lengths, q_all, k_all, v_all)


def merged(parts_ref, live):
    levels = []
    for y in range(NY):
        pieces = parts_ref[y, :, WIDTH_DEV:].astype(jnp.float32)
        levels.append(
            pieces[:, :HEADS_DEV]
            + pieces[:, HEADS_DEV : 2 * HEADS_DEV]
            + pieces[:, 2 * HEADS_DEV : 3 * HEADS_DEV]
        )
    top = functools.reduce(jnp.maximum, levels)
    shares = [jnp.exp2(level - top) for level in levels]
    inverse = 1.0 / functools.reduce(jnp.add, shares)
    shares = [share * inverse for share in shares]
    columns = []
    for h in range(HEADS_DEV):
        total = jnp.zeros((ROWS, HD), jnp.float32)
        for y in range(NY):
            part = parts_ref[y, :, h * HD : (h + 1) * HD].astype(jnp.float32)
            total = total + shares[y][:, h : h + 1] * part
        columns.append(total)
    return jnp.where(live, jnp.concatenate(columns, 1), 0.0)


def live_rows(lengths_ref, tick):
    first = (lax.axis_index("cx") * NY + lax.axis_index("cy")) * ROWS
    row = first + lax.broadcasted_iota(jnp.int32, (ROWS, 1), 0)
    return row < lengths_ref[segment_of(tick)]


def merge_one_kernel(lengths_ref, parts_ref, rows_ref, residual_ref, sum_ref):
    total = rows_ref[...].astype(jnp.float32) + merged(parts_ref, live_rows(lengths_ref, 0))
    sum_ref[...] = total
    residual_ref[...] = total.astype(jnp.bfloat16)


def merge_two_kernel(
    lengths_ref, parts_ref, passed_ref, fresh_ref, one_ref, sum_one_ref, residual_ref, sum_ref, squares_ref
):
    first = lax.axis_index("section") == 0
    incoming = jnp.where(first, fresh_ref[...].astype(jnp.float32), passed_ref[...].astype(jnp.float32))
    total = incoming + merged(parts_ref, live_rows(lengths_ref, 1))
    sum_ref[...] = total
    residual_ref[0] = one_ref[...]
    residual_ref[1] = total.astype(jnp.bfloat16)
    sum_one = sum_one_ref[...]
    lane = lax.broadcasted_iota(jnp.int32, (ROWS, 128), 1)
    squares_ref[...] = jnp.where(
        lane < 64,
        jnp.sum(sum_one * sum_one, axis=1, keepdims=True),
        jnp.sum(total * total, axis=1, keepdims=True),
    )


def norm_kernel(squares_ref, sum_one_ref, sum_two_ref, gain_ref, normed_ref):
    scale = lax.rsqrt(squares_ref[...] / FULL_WIDTH + EPSILON)
    gain = gain_ref[...].astype(jnp.float32)
    normed_ref[0] = (sum_one_ref[...] * scale[:, 0:1] * gain).astype(jnp.bfloat16)
    normed_ref[1] = (sum_two_ref[...] * scale[:, 64:65] * gain).astype(jnp.bfloat16)


SMEM = pl.BlockSpec(memory_space=pltpu.SMEM)
VMEM = pl.BlockSpec(memory_space=pltpu.VMEM)


def shaped(shape, dtype):
    return jax.ShapeDtypeStruct(shape, dtype)


def body(queries, key_rows, value_rows, section_rows, fresh_rows, norm_gain, segment_lengths):
    q_own = jnp.broadcast_to(queries[:, 0], (NY, 2, ROWS, WIDTH_DEV))
    q_all = lax.all_to_all(q_own, "cy", 0, 0)
    k_all = lax.all_gather(key_rows[0], "cx")
    v_all = lax.all_gather(value_rows[0], "cx")

    parts_one = lax.all_to_all(attend(0, segment_lengths, q_all, k_all, v_all), "cy", 0, 0)
    parts_two = lax.all_to_all(attend(1, segment_lengths, q_all, k_all, v_all), "cy", 0, 0)

    rows_f32 = shaped((ROWS, WIDTH_DEV), jnp.float32)
    residual_one, sum_one = pl.pallas_call(
        merge_one_kernel,
        in_specs=[SMEM, VMEM, VMEM],
        out_specs=[VMEM, VMEM],
        out_shape=[shaped((ROWS, WIDTH_DEV), jnp.bfloat16), rows_f32],
        name="merge_one",
    )(segment_lengths, parts_one, section_rows[0])
    count = lax.axis_size("section")
    passed = lax.ppermute(residual_one, "section", [(i, i + 1) for i in range(count - 1)])
    residual, sum_two, squares = pl.pallas_call(
        merge_two_kernel,
        in_specs=[SMEM] + [VMEM] * 5,
        out_specs=[VMEM, VMEM, VMEM],
        out_shape=[
            shaped((2, ROWS, WIDTH_DEV), jnp.bfloat16),
            rows_f32,
            shaped((ROWS, 128), jnp.float32),
        ],
        name="merge_two",
    )(segment_lengths, parts_two, passed, fresh_rows, residual_one, sum_one)
    squares = lax.psum(squares, "tp")
    normed = pl.pallas_call(
        norm_kernel,
        in_specs=[VMEM] * 4,
        out_specs=VMEM,
        out_shape=shaped((2, ROWS, WIDTH_DEV), jnp.bfloat16),
        name="norm",
    )(squares, sum_one, sum_two, norm_gain)
    return residual[:, None], normed[:, None]


def solution(mesh):
    grid = Mesh(mesh.devices.reshape(8, NX, NY, 4), ("section", "cx", "cy", "tp"))
    cp = ("cx", "cy")
    in_specs = (
        P(None, "section", cp, "tp"),
        P("section", cp, "tp"),
        P("section", cp, "tp"),
        P("section", cp, "tp"),
        P(cp, "tp"),
        P("section", "tp"),
        P(),
    )
    out_specs = (P(None, "section", cp, "tp"), P(None, "section", cp, "tp"))
    return jax.shard_map(body, mesh=grid, in_specs=in_specs, out_specs=out_specs, check_vma=False)
```

time: 347 us -> 156 us (0.45)
  the two profiles are of different devices: /device:TPU:257 before, /device:TPU:64 now
where the time goes in v1:
time: 156 us; the launch traced here: 155 us
  waiting for transfers between devices  56 us (36%)
  blocking collectives  40.4 us (26%)
  Pallas kernels  29.8 us (19%)
  between operations  14.1 us (9%)
  starting transfers between devices  13.3 us (9%)
  local copies, waits for them, and re-layouts  1.69 us (1%)
    all_gather x1, waiting for transfers between devices, body(): v_all = lax.all_gather(value_rows[0], 'cx')  34.1 us
    pallas_call x2, Pallas kernels, attend(): pl.pallas_call(functools.partial(attend_kernel, tick), grid=(1,), in_spec...  23.9 us
    psum x1, blocking collectives, body(): squares = lax.psum(squares, 'tp')  21.2 us
    all_to_all x1, blocking collectives, body(): q_all = lax.all_to_all(q_own, 'cy', 0, 0)  19.3 us
    all_gather x1, waiting for transfers between devices, body(): k_all = lax.all_gather(key_rows[0], 'cx')  17 us
    all_to_all x1, starting transfers between devices, body(): lax.all_to_all(attend(1, segment_lengths, q_all, k_all, v_all), 'cy', 0, 0)  5.09 us
    all_to_all x1, starting transfers between devices, body(): lax.all_to_all(attend(0, segment_lengths, q_all, k_all, v_all), 'cy', 0, 0)  4.6 us
    ppermute x1, starting transfers between devices, body(): lax.ppermute(residual_one, 'section', [(i, i + 1) for i in range(count -...  3.54 us
  transfers between devices with their start and end apart: 5, of which 3 were waited for; matrix products, arithmetic and copies ran while one was open for 1% of the time, Pallas kernels for 9%

profile of v1, /device:TPU:64, one launch (start us, length us, event | category | flops | bytes accessed | tf_op | source)
XLA Modules:
  0.0 155.2 jit_solution(5279409556012332764)
XLA Ops:
  7.2 0.0 all-gather.3.cloned.1.call-start
  7.2 0.7 all-gather.3.cloned.1.call-update
  7.9 0.0 all-gather.5.cloned.1.call-start
  7.9 0.7 all-gather.5.cloned.1.call-update
  8.6 1.0 broadcast_in_dim.9
  9.6 19.3 %all_to_all.15.q_ref = bf16[4,2,32,1024]{3,2,1,0:T(8,128)(2,1)} all-to-all(bf16[4,2,32,1024]{3,2,1,0:T(8,128)(2,1)S(1)} %broadcast_in_dim.9), channel_id=1, replica_groups=mesh['section'=8,'cx'=4,'cy'=4,'tp'=4] {'cy'}, dimensions={0} | all-to-all | bytes 1048576 | tf_op jit(solution)/shard_map/all_to_all | solution.py:188
  28.9 17.0 %all-gather.3.cloned.1.call-done.k_ref = bf16[4,1536,128]{2,1,0:T(8,128)(2,1)} async-done(((bf16[1,1536,128]{2,1,0:T(8,128)(2,1)}), bf16[4,1536,128]{2,1,0:T(8,128)(2,1)}) %all-gather.3.cloned.1.call-update) | async-done | bytes 1572880 | tf_op jit(solution)/shard_map/all_gather | solution.py:189
  45.9 34.1 %all-gather.5.cloned.1.call-done.v_ref = bf16[4,1536,128]{2,1,0:T(8,128)(2,1)} async-done(((bf16[1,1536,128]{2,1,0:T(8,128)(2,1)}), bf16[4,1536,128]{2,1,0:T(8,128)(2,1)}) %all-gather.5.cloned.1.call-update) | async-done | bytes 1572880 | tf_op jit(solution)/shard_map/all_gather | solution.py:190
  80.0 11.9 %attend_0.1 = bf16[4,32,1152]{2,1,0:T(8,128)(2,1)} custom-call(s32[9]{0:T(128)} %lengths_ref.7, bf16[4,2,32,1024]{3,2,1,0:T(8,128)(2,1)} %all_to_all.15.q_ref, bf16[4,1536,128]{2,1,0:T(8,128)(2,1)} %all-gather.3.cloned.1.call-done.k_ref, bf16[4,1536,128]{2,1,0:T(8,128)(2,1)} %all-gather.5.cloned.1.call-done.v_ref), custom_call_target="tpu_custom_call" | custom-call | tf_op jit(solution)/shard_map/attend_0/pallas_call | solution.py:102
  91.9 4.6 %all-to-all-start.2 = ((bf16[4,32,1152]{2,1,0:T(8,128)(2,1)}), bf16[4,32,1152]{2,1,0:T(8,128)(2,1)S(1)}, u32[]{:S(2)}, u32[]{:S(2)}) async-start(bf16[4,32,1152]{2,1,0:T(8,128)(2,1)} %attend_0.1), calls=%async_computation.2 | async-start | bytes 589824 | tf_op jit(solution)/shard_map/all_to_all | solution.py:192
  96.5 12.0 %attend_1.1 = bf16[4,32,1152]{2,1,0:T(8,128)(2,1)} custom-call(s32[9]{0:T(128)} %lengths_ref.7, bf16[4,2,32,1024]{3,2,1,0:T(8,128)(2,1)} %all_to_all.15.q_ref, bf16[4,1536,128]{2,1,0:T(8,128)(2,1)} %all-gather.3.cloned.1.call-done.k_ref, bf16[4,1536,128]{2,1,0:T(8,128)(2,1)} %all-gather.5.cloned.1.call-done.v_ref), custom_call_target="tpu_custom_call" | custom-call | tf_op jit(solution)/shard_map/attend_1/pallas_call | solution.py:102
  108.5 0.0 all-to-all-done.2.parts_ref
  108.5 0.0 copy-start
  108.5 5.1 %all-to-all-start.1 = ((bf16[4,32,1152]{2,1,0:T(8,128)(2,1)}), bf16[4,32,1152]{2,1,0:T(8,128)(2,1)S(1)}, u32[]{:S(2)}, u32[]{:S(2)}) async-start(bf16[4,32,1152]{2,1,0:T(8,128)(2,1)} %attend_1.1), calls=%async_computation.1 | async-start | bytes 589824 | tf_op jit(solution)/shard_map/all_to_all | solution.py:193
  113.6 0.0 copy-done
  113.6 2.0 %merge_one.1 = (bf16[32,1024]{1,0:T(8,128)(2,1)}, f32[32,1024]{1,0:T(8,128)}) custom-call(s32[9]{0:T(128)} %lengths_ref.7, bf16[4,32,1152]{2,1,0:T(8,128)(2,1)} %copy-done, bf16[32,1024]{1,0:T(8,128)(2,1)} %bitcast.10), custom_call_target="tpu_custom_call" | custom-call | tf_op jit(solution)/shard_map/merge_one/pallas_call | solution.py:196
  115.6 3.5 %collective-permute-start = (bf16[32,1024]{1,0:T(8,128)(2,1)}, bf16[32,1024]{1,0:T(8,128)(2,1)S(1)}, u32[]{:S(2)}, u32[]{:S(2)}) collective-permute-start(bf16[32,1024]{1,0:T(8,128)(2,1)} %get-tuple-element.7.one_ref), channel_id=1, source_target_pairs={{0,64},{64,128},{128,192},{192,256},{256,320},{320,384},{384,448},... | collective-permute-start | bytes 196616 | tf_op jit(solution)/shard_map/ppermute | solution.py:204
  119.1 3.5 %all-to-all-done.1.parts_ref = bf16[4,32,1152]{2,1,0:T(8,128)(2,1)S(1)} async-done(((bf16[4,32,1152]{2,1,0:T(8,128)(2,1)}), bf16[4,32,1152]{2,1,0:T(8,128)(2,1)S(1)}, u32[]{:S(2)}, u32[]{:S(2)}) %all-to-all-start.1) | async-done | bytes 294944 | tf_op jit(solution)/shard_map/all_to_all | solution.py:193
  122.6 0.0 copy-start.1
  122.6 0.0 collective-permute-done.passed_ref
  122.6 0.0 copy-start.2
  122.6 0.7 copy-done.1
  123.3 0.0 copy-done.2
  123.4 2.1 %merge_two.1 = (bf16[2,32,1024]{2,1,0:T(8,128)(2,1)}, f32[32,1024]{1,0:T(8,128)}, f32[32,128]{1,0:T(8,128)}) custom-call(s32[9]{0:T(128)} %lengths_ref.7, bf16[4,32,1152]{2,1,0:T(8,128)(2,1)} %copy-done.1, bf16[32,1024]{1,0:T(8,128)(2,1)} %copy-done.2, bf16[32,1024]{1,0:T(8,128)(2,1)} %fresh_ref.1, bf16[32,1024]{1,0:T(8,128)(2,1)} %get-tuple-element.7.one_ref, ...), custom_call_target="tpu_custom_call" | custom-call | tf_op jit(solution)/shard_map/merge_two/pallas_call | solution.py:205
  125.5 21.2 %psum.7.squares_ref = f32[32,128]{1,0:T(8,128)} all-reduce(f32[32,128]{1,0:T(8,128)} %get-tuple-element.10), channel_id=1, replica_groups=mesh['section'=8,'cx'=4,'cy'=4,'tp'=4] {'tp'}, use_global_device_ids=true, to_apply=%region_0.0 | all-reduce | flops 4096 | bytes 32768 | tf_op jit(solution)/shard_map/psum | solution.py:216
  146.6 1.7 %norm.1 = bf16[2,32,1024]{2,1,0:T(8,128)(2,1)} custom-call(f32[32,128]{1,0:T(8,128)} %psum.7.squares_ref, f32[32,1024]{1,0:T(8,128)} %get-tuple-element.8.sum_one_ref, f32[32,1024]{1,0:T(8,128)} %get-tuple-element.11.sum_two_ref, bf16[1,1024]{1,0:T(2,128)(2,1)} %gain_ref.1), custom_call_target="tpu_custom_call" | custom-call | tf_op jit(solution)/shard_map/norm/pallas_call | solution.py:217
Async XLA Ops:
  7.2 38.7 %all-gather.3.cloned.1.call-start = ((), (), s32[]{:S(2)}) async-start(), calls=%async_computation.3 | async-start | bytes 1966080 | tf_op jit(solution)/shard_map/all_gather | solution.py:189
  7.9 72.1 %all-gather.5.cloned.1.call-start = ((), (), s32[]{:S(2)}) async-start(), calls=%async_computation.4 | async-start | bytes 1966080 | tf_op jit(solution)/shard_map/all_gather | solution.py:190
  91.9 16.6 %all-to-all-start.2 = ((bf16[4,32,1152]{2,1,0:T(8,128)(2,1)}), bf16[4,32,1152]{2,1,0:T(8,128)(2,1)S(1)}, u32[]{:S(2)}, u32[]{:S(2)}) async-start(bf16[4,32,1152]{2,1,0:T(8,128)(2,1)} %attend_0.1), calls=%async_computation.2 | async-start | bytes 589824 | tf_op jit(solution)/shard_map/all_to_all | solution.py:192
  108.5 5.1 %copy-start = (bf16[4,32,1152]{2,1,0:T(8,128)(2,1)}, bf16[4,32,1152]{2,1,0:T(8,128)(2,1)S(1)}, u32[]{:S(2)}) copy-start(bf16[4,32,1152]{2,1,0:T(8,128)(2,1)S(1)} %all-to-all-done.2.parts_ref) | copy-start | bytes 884740
  108.5 14.1 %all-to-all-start.1 = ((bf16[4,32,1152]{2,1,0:T(8,128)(2,1)}), bf16[4,32,1152]{2,1,0:T(8,128)(2,1)S(1)}, u32[]{:S(2)}, u32[]{:S(2)}) async-start(bf16[4,32,1152]{2,1,0:T(8,128)(2,1)} %attend_1.1), calls=%async_computation.1 | async-start | bytes 589824 | tf_op jit(solution)/shard_map/all_to_all | solution.py:193
  115.6 7.0 %collective-permute-start = (bf16[32,1024]{1,0:T(8,128)(2,1)}, bf16[32,1024]{1,0:T(8,128)(2,1)S(1)}, u32[]{:S(2)}, u32[]{:S(2)}) collective-permute-start(bf16[32,1024]{1,0:T(8,128)(2,1)} %get-tuple-element.7.one_ref), channel_id=1, source_target_pairs={{0,64},{64,128},{128,192},{192,256},{256,320},{320,384},{384,448},... | collective-permute-start | bytes 196616 | tf_op jit(solution)/shard_map/ppermute | solution.py:204
  122.6 0.7 copy-start.1
  122.6 0.7 copy-start.2
Sparse Core Ops, SparseCore 0:
  10.1 35.7 all-gather.2
  48.0 31.9 all-gather.4

commit v2 on v1

v2 whole, which is shorter than its diff:
```python
import functools

import jax
import jax.numpy as jnp
import numpy as np
from jax import lax
from jax.experimental import pallas as pl
from jax.experimental.pallas import tpu as pltpu
from jax.sharding import Mesh
from jax.sharding import PartitionSpec as P

HD = 128
NX, NY = 4, 4
HEADS_DEV = 8
ROWS = 32
WIDTH_DEV = HEADS_DEV * HD
KEYS = 1536
CTX = KEYS * NX * NY
N_SEG = 9
FULL_WIDTH = 4096
PACKED = 2 * WIDTH_DEV + 128
TILE = 512
NEGATIVE = -1e30
FLOOR = -1e28
TINY = 1e-30
EPSILON = 1e-05
LOG2_SCALE = float(np.log2(np.e) / np.sqrt(HD))
VMEM_LIMIT = 16 * 2**20
SMALL = pltpu.CompilerParams(vmem_limit_bytes=4 * 2**20)


def segment_of(tick):
    return 7 - lax.axis_index("section") + tick


def segment_start(lengths_ref, segment):
    start = jnp.int32(CTX)
    for j in range(N_SEG):
        start = start - jnp.where(j >= segment, lengths_ref[j], 0)
    return start


def init_state(rows):
    return jnp.zeros((rows, HD), jnp.float32), jnp.full((rows, HD), FLOOR, jnp.float32)


def update(state, started, q, k_tiles, v_tiles, last_offset):
    out, top = state
    lane = lax.broadcasted_iota(jnp.int32, out.shape, 1)
    total = jnp.where(lane == 0, 1.0, 0.0) if started else jnp.zeros(out.shape, jnp.float32)
    for t in range(KEYS // TILE):
        s = lax.dot_general(
            q, k_tiles(t), (((1,), (1,)), ((), ())), preferred_element_type=jnp.float32
        )
        if last_offset is not None:
            offset = t * TILE + lax.broadcasted_iota(jnp.int32, (1, TILE), 1)
            s = jnp.where(offset <= last_offset, s, NEGATIVE)
        part = s[:, :HD]
        for u in range(1, TILE // HD):
            part = jnp.maximum(part, s[:, u * HD : (u + 1) * HD])
        tile_top = jnp.max(part, axis=1, keepdims=True) * LOG2_SCALE
        new_top = jnp.maximum(top, jnp.broadcast_to(tile_top, top.shape))
        groups = [
            jnp.exp2(s[:, u * HD : (u + 1) * HD] * LOG2_SCALE - new_top)
            for u in range(TILE // HD)
        ]
        lane_sum = functools.reduce(jnp.add, groups)
        p = jnp.concatenate([group.astype(jnp.bfloat16) for group in groups], 1)
        mixed = jnp.dot(p, v_tiles(t), preferred_element_type=jnp.float32)
        rescale = jnp.exp2(top - new_top)
        out = out * rescale + mixed
        total = total * rescale + lane_sum
        top = new_top
    total = jnp.maximum(jnp.sum(total, axis=1, keepdims=True), TINY)
    return out * (1.0 / total), top + jnp.log2(total)


def write_packed(state, tick, outs):
    out, level = state
    out = out.astype(jnp.bfloat16)
    lane = lax.broadcasted_iota(jnp.int32, (ROWS, 128), 1)
    head = lane % HEADS_DEV
    piece = lane % (3 * HEADS_DEV) // HEADS_DEV
    for d, o_ref in enumerate(outs):
        levels = jnp.zeros((ROWS, 128), jnp.float32)
        for h in range(HEADS_DEV):
            at = (d * HEADS_DEV + h) * ROWS
            column = pl.multiple_of(tick * WIDTH_DEV + h * HD, HD)
            o_ref[:, pl.ds(column, HD)] = out[at : at + ROWS]
            levels = jnp.where(head == h, level[at : at + ROWS], levels)
        high = levels.astype(jnp.bfloat16).astype(jnp.float32)
        middle = (levels - high).astype(jnp.bfloat16).astype(jnp.float32)
        low = levels - high - middle
        pieces = jnp.where(piece == 0, high, jnp.where(piece == 1, middle, low))
        kept = jnp.where(tick == 0, 0.0, o_ref[:, 2 * WIDTH_DEV :].astype(jnp.float32))
        mine = lane // (3 * HEADS_DEV) == tick
        o_ref[:, 2 * WIDTH_DEV :] = jnp.where(mine, pieces, kept).astype(jnp.bfloat16)


def chunk_kernel(shift, first, last, *refs):
    lengths_ref, q_ref, kv_ref = refs[:3]
    state_in, outs = ([], refs[3:]) if first else (refs[3:5], refs[5:])
    cx = lax.axis_index("cx")
    cy = lax.axis_index("cy")
    key_start = ((cx + shift) % NX * NY + cy) * KEYS

    def one(tick):
        start = segment_start(lengths_ref, segment_of(tick))
        least = start + cx * NY * ROWS - key_start
        full = least >= KEYS - 1
        none = least + NY * ROWS - 1 < 0
        rows = NY * HEADS_DEV * ROWS

        def load():
            return init_state(rows) if first else tuple(ref[tick] for ref in state_in)

        def store(state):
            if last:
                write_packed(state, tick, outs)
            else:
                for ref, value in zip(outs, state, strict=True):
                    ref[tick] = value

        def run(masked):
            q = jnp.concatenate(
                [
                    q_ref[cy ^ d, tick, :, h * HD : (h + 1) * HD]
                    for d in range(NY)
                    for h in range(HEADS_DEV)
                ],
                0,
            )
            last_offset = None
            if masked:
                row_id = lax.broadcasted_iota(jnp.int32, (rows, 1), 0)
                owner = (row_id // (HEADS_DEV * ROWS)) ^ cy
                last_offset = least + owner * ROWS + row_id % ROWS
            store(
                update(
                    load(),
                    not first,
                    q,
                    lambda t: kv_ref[0, t * TILE : (t + 1) * TILE, :],
                    lambda t: kv_ref[1, t * TILE : (t + 1) * TILE, :],
                    last_offset,
                )
            )

        @pl.when(full)
        def _():
            run(False)

        @pl.when(jnp.logical_not(jnp.logical_or(full, none)))
        def _():
            run(True)

        @pl.when(none)
        def _():
            store(load())

    lax.fori_loop(0, 2, lambda tick, _: one(tick), None)


def stage_kernel(k_ref, v_ref, q_ref, kv_ref, q_own_ref, q_held, sems):
    q_copy = pltpu.make_async_copy(q_ref, q_held, sems.at[0])
    copies = [
        pltpu.make_async_copy(k_ref, kv_ref.at[0], sems.at[1]),
        pltpu.make_async_copy(v_ref, kv_ref.at[1], sems.at[2]),
    ]
    q_copy.start()
    for copy in copies:
        copy.start()
    q_copy.wait()
    for y in range(NY):
        copies.append(pltpu.make_async_copy(q_held, q_own_ref.at[y], sems.at[3 + y]))
        copies[-1].start()
    for copy in copies:
        copy.wait()


def in_vmem(x):
    return pltpu.with_memory_space_constraint(x, pltpu.VMEM)


def in_hbm(x):
    return pltpu.with_memory_space_constraint(x, pltpu.HBM)


def attend_chunk(lengths, q_all, kv, state, shift, last=False):
    first = state is None
    rows = NY * HEADS_DEV * ROWS
    if last:
        out_shape = [pltpu.VMEM((ROWS, PACKED), jnp.bfloat16)] * NY
    else:
        out_shape = [pltpu.VMEM((2, rows, HD), jnp.float32)] * 2
    operands = [q_all, kv] + ([] if first else list(state))
    return pl.pallas_call(
        functools.partial(chunk_kernel, shift, first, last),
        in_specs=[SMEM] + [VMEM] * len(operands),
        out_specs=[VMEM] * len(out_shape),
        out_shape=out_shape,
        compiler_params=pltpu.CompilerParams(vmem_limit_bytes=VMEM_LIMIT),
        name=f"attend_{shift}",
    )(lengths, *[in_vmem(x) for x in operands])


def merged(parts, tick, live):
    levels = []
    for part_ref in parts:
        pieces = part_ref[:, 2 * WIDTH_DEV :].astype(jnp.float32)
        levels.append(
            pieces
            + pltpu.roll(pieces, 128 - HEADS_DEV, 1)
            + pltpu.roll(pieces, 128 - 2 * HEADS_DEV, 1)
        )
    top = functools.reduce(jnp.maximum, levels)
    shares = [jnp.exp2(level - top) for level in levels]
    inverse = 1.0 / functools.reduce(jnp.add, shares)
    shares = [share * inverse for share in shares]
    columns = []
    for h in range(HEADS_DEV):
        total = jnp.zeros((ROWS, HD), jnp.float32)
        column = tick * WIDTH_DEV + h * HD
        lane = tick * 3 * HEADS_DEV + h
        for part_ref, share in zip(parts, shares, strict=True):
            part = part_ref[:, column : column + HD].astype(jnp.float32)
            total = total + share[:, lane : lane + 1] * part
        columns.append(total)
    return jnp.where(live, jnp.concatenate(columns, 1), 0.0)


def live_rows(lengths_ref, tick):
    first = (lax.axis_index("cx") * NY + lax.axis_index("cy")) * ROWS
    row = first + lax.broadcasted_iota(jnp.int32, (ROWS, 1), 0)
    return row < lengths_ref[segment_of(tick)]


def merge_kernel(lengths_ref, rows_ref, *refs):
    parts, (residual_ref, sum_ref, attended_ref) = refs[:NY], refs[NY:]
    total = rows_ref[...].astype(jnp.float32) + merged(parts, 0, live_rows(lengths_ref, 0))
    sum_ref[...] = total
    residual_ref[...] = total.astype(jnp.bfloat16)
    attended_ref[...] = merged(parts, 1, live_rows(lengths_ref, 1))


def add_kernel(
    attended_ref, passed_ref, fresh_ref, one_ref, sum_one_ref, residual_ref, sum_ref, squares_ref
):
    first = lax.axis_index("section") == 0
    incoming = jnp.where(first, fresh_ref[...].astype(jnp.float32), passed_ref[...].astype(jnp.float32))
    total = incoming + attended_ref[...]
    sum_ref[...] = total
    residual_ref[0] = one_ref[...]
    residual_ref[1] = total.astype(jnp.bfloat16)
    ones = jnp.ones((8, WIDTH_DEV), jnp.float32)
    for tick, rows in enumerate((sum_one_ref[...], total)):
        squares = lax.dot_general(
            ones,
            rows * rows,
            (((1,), (1,)), ((), ())),
            precision=lax.Precision.HIGHEST,
            preferred_element_type=jnp.float32,
        )
        squares_ref[tick : tick + 1, :] = squares[:1]


def norm_kernel(squares_ref, sum_one_ref, sum_two_ref, gain_ref, normed_ref):
    gain = gain_ref[...].astype(jnp.float32)
    row = lax.broadcasted_iota(jnp.int32, (ROWS, ROWS), 0)
    lane = lax.broadcasted_iota(jnp.int32, (ROWS, ROWS), 1)
    for tick, sum_ref in enumerate((sum_one_ref, sum_two_ref)):
        scale = lax.rsqrt(squares_ref[tick : tick + 1, :] / FULL_WIDTH + EPSILON)
        column = jnp.sum(jnp.where(row == lane, scale, 0.0), axis=1, keepdims=True)
        normed_ref[tick] = (sum_ref[...] * column * gain).astype(jnp.bfloat16)


SMEM = pl.BlockSpec(memory_space=pltpu.SMEM)
VMEM = pl.BlockSpec(memory_space=pltpu.VMEM)


def shaped(shape, dtype):
    return jax.ShapeDtypeStruct(shape, dtype)


def body(queries, key_rows, value_rows, section_rows, fresh_rows, norm_gain, segment_lengths):
    def along_x(value, by):
        return lax.ppermute(value, "cx", [(i, (i + by) % NX) for i in range(NX)])

    kv, q_own = pl.pallas_call(
        stage_kernel,
        in_specs=[pl.BlockSpec(memory_space=pl.ANY)] * 3,
        out_specs=[VMEM, pl.BlockSpec(memory_space=pl.ANY)],
        out_shape=[
            pltpu.VMEM((2, KEYS, HD), jnp.bfloat16),
            jax.ShapeDtypeStruct((NY, 2, ROWS, WIDTH_DEV), jnp.bfloat16),
        ],
        scratch_shapes=[
            pltpu.VMEM((2, ROWS, WIDTH_DEV), jnp.bfloat16),
            pltpu.SemaphoreType.DMA((3 + NY,)),
        ],
        compiler_params=SMALL,
        name="stage",
    )(*[in_hbm(x) for x in (key_rows[0], value_rows[0], queries[:, 0])])
    below = along_x(kv, 1)
    above = along_x(kv, -1)
    q_all = lax.all_to_all(q_own, "cy", 0, 0)
    below, q_all = lax.optimization_barrier((below, q_all))
    far = along_x(below, 1)

    state = attend_chunk(segment_lengths, q_all, kv, None, 0)
    state = attend_chunk(segment_lengths, q_all, below, state, NX - 1)
    state = attend_chunk(segment_lengths, q_all, above, state, 1)
    packed = attend_chunk(segment_lengths, q_all, far, state, 2, last=True)
    parts = [packed[0]] + [None] * (NY - 1)
    for d in (3, 2, 1):
        parts[d] = lax.ppermute(packed[d], "cy", [(i, i ^ d) for i in range(NY)])

    rows_bf16 = pltpu.VMEM((ROWS, WIDTH_DEV), jnp.bfloat16)
    rows_f32 = pltpu.VMEM((ROWS, WIDTH_DEV), jnp.float32)
    residual_one, sum_one, attended_two = pl.pallas_call(
        merge_kernel,
        in_specs=[SMEM] + [VMEM] * (1 + NY),
        out_specs=[VMEM] * 3,
        out_shape=[rows_bf16, rows_f32, rows_f32],
        compiler_params=SMALL,
        name="merge",
    )(segment_lengths, in_vmem(section_rows[0]), *[in_vmem(x) for x in parts])
    count = lax.axis_size("section")
    passed = lax.ppermute(residual_one, "section", [(i, i + 1) for i in range(count - 1)])
    residual, sum_two, squares = pl.pallas_call(
        add_kernel,
        in_specs=[VMEM] * 5,
        out_specs=[VMEM] * 3,
        out_shape=[
            jax.ShapeDtypeStruct((2, ROWS, WIDTH_DEV), jnp.bfloat16),
            rows_f32,
            pltpu.VMEM((2, ROWS), jnp.float32),
        ],
        compiler_params=SMALL,
        name="add",
    )(*[in_vmem(x) for x in (attended_two, passed, fresh_rows, residual_one, sum_one)])
    squares = lax.psum(squares, "tp")
    normed = pl.pallas_call(
        norm_kernel,
        in_specs=[VMEM] * 4,
        out_specs=VMEM,
        out_shape=jax.ShapeDtypeStruct((2, ROWS, WIDTH_DEV), jnp.bfloat16),
        compiler_params=SMALL,
        name="norm",
    )(in_vmem(squares), in_vmem(sum_one), in_vmem(sum_two), in_vmem(norm_gain))
    return residual[:, None], normed[:, None]


def solution(mesh):
    grid = Mesh(mesh.devices.reshape(8, NX, NY, 4), ("section", "cx", "cy", "tp"))
    cp = ("cx", "cy")
    in_specs = (
        P(None, "section", cp, "tp"),
        P("section", cp, "tp"),
        P("section", cp, "tp"),
        P("section", cp, "tp"),
        P(cp, "tp"),
        P("section", "tp"),
        P(),
    )
    out_specs = (P(None, "section", cp, "tp"), P(None, "section", cp, "tp"))
    return jax.shard_map(body, mesh=grid, in_specs=in_specs, out_specs=out_specs, check_vma=False)
```

time: 156 us -> 91.3 us (0.59)
  the two profiles are of different devices: /device:TPU:64 before, /device:TPU:200 now
where the time goes in v2:
time: 91.3 us; the launch traced here: 90.9 us
  starting transfers between devices  29.3 us (32%)
  Pallas kernels  26.1 us (29%)
  waiting for transfers between devices  23.7 us (26%)
  blocking collectives  11.2 us (12%)
    pallas_call x4, Pallas kernels, attend_chunk(): pl.pallas_call(functools.partial(chunk_kernel, shift, first, last), in_sp...  21.6 us
    ppermute x3, waiting for transfers between devices, along_x(): return lax.ppermute(value, 'cx', [(i, (i + by) % NX) for i in range(NX)])  13.3 us
    psum x1, blocking collectives, body(): squares = lax.psum(squares, 'tp')  11.2 us
    ppermute x3, starting transfers between devices, along_x(): return lax.ppermute(value, 'cx', [(i, (i + by) % NX) for i in range(NX)])  9.22 us
    ppermute x3, starting transfers between devices, body(): parts[d] = lax.ppermute(packed[d], 'cy', [(i, i ^ d) for i in range(NY)])  9.21 us
    ppermute x3, waiting for transfers between devices, body(): parts[d] = lax.ppermute(packed[d], 'cy', [(i, i ^ d) for i in range(NY)])  8.54 us
    ppermute x1, starting transfers between devices, body(): lax.ppermute(residual_one, 'section', [(i, i + 1) for i in range(count -...  5.49 us
    all_to_all x1, starting transfers between devices, body(): q_all = lax.all_to_all(q_own, 'cy', 0, 0)  5.33 us
  transfers between devices with their start and end apart: 8, of which 5 were waited for; matrix products, arithmetic and copies ran while one was open for 0% of the time, Pallas kernels for 18%

profile of v2, /device:TPU:200, one launch (start us, length us, event | category | flops | bytes accessed | tf_op | source)
XLA Modules:
  0.0 90.9 jit_solution(8731145842768618636)
XLA Ops:
  0.6 1.8 %stage.1 = (bf16[2,1536,128]{2,1,0:T(8,128)(2,1)S(1)}, bf16[4,2,32,1024]{3,2,1,0:T(8,128)(2,1)}) custom-call(bf16[1536,128]{1,0:T(8,128)(2,1)} %bitcast.11, bf16[1536,128]{1,0:T(8,128)(2,1)} %bitcast.12, bf16[2,32,1024]{2,1,0:T(8,128)(2,1)} %bitcast.13), custom_call_target="tpu_custom_call" | custom-call | tf_op jit(solution)/shard_map/stage/pallas_call | solution.py:289
  2.4 3.4 %collective-permute-start = (bf16[2,1536,128]{2,1,0:T(8,128)(2,1)S(1)}, bf16[2,1536,128]{2,1,0:T(8,128)(2,1)S(1)}, u32[]{:S(2)}, u32[]{:S(2)}) collective-permute-start(bf16[2,1536,128]{2,1,0:T(8,128)(2,1)S(1)} %get-tuple-element.22.refs_2_), channel_id=1, source_target_pairs={{0,16},{16,32},{32,48},{48,0},{1,17},{17,33},{33,49},{49,1},{2,18}... | collective-permute-start | bytes 2359304 | tf_op jit(solution)/shard_map/ppermute | solution.py:287
  5.8 0.0 copy-start.2
  5.8 5.3 %all-to-all-start = ((bf16[4,2,32,1024]{3,2,1,0:T(8,128)(2,1)}), bf16[4,2,32,1024]{3,2,1,0:T(8,128)(2,1)S(1)}, u32[]{:S(2)}, u32[]{:S(2)}) async-start(bf16[4,2,32,1024]{3,2,1,0:T(8,128)(2,1)} %get-tuple-element.23), calls=%async_computation | async-start | bytes 1048576 | tf_op jit(solution)/shard_map/all_to_all | solution.py:306
  11.1 3.6 %collective-permute-start.2 = (bf16[2,1536,128]{2,1,0:T(8,128)(2,1)S(1)}, bf16[2,1536,128]{2,1,0:T(8,128)(2,1)S(1)}, u32[]{:S(2)}, u32[]{:S(2)}) collective-permute-start(bf16[2,1536,128]{2,1,0:T(8,128)(2,1)S(1)} %get-tuple-element.22.refs_2_), channel_id=1, source_target_pairs={{0,48},{16,0},{32,16},{48,32},{1,49},{17,1},{33,17},{49,33},{2,50}... | collective-permute-start | bytes 2359304 | tf_op jit(solution)/shard_map/ppermute | solution.py:287
  14.8 10.0 %collective-permute-done.refs_2_ = bf16[2,1536,128]{2,1,0:T(8,128)(2,1)S(1)} collective-permute-done((bf16[2,1536,128]{2,1,0:T(8,128)(2,1)S(1)}, bf16[2,1536,128]{2,1,0:T(8,128)(2,1)S(1)}, u32[]{:S(2)}, u32[]{:S(2)}) %collective-permute-start) | collective-permute-done | bytes 786464 | tf_op jit(solution)/shard_map/ppermute | solution.py:287
  24.8 0.0 all-to-all-done.refs_1_
  24.8 2.2 %collective-permute-start.1 = (bf16[2,1536,128]{2,1,0:T(8,128)(2,1)S(1)}, bf16[2,1536,128]{2,1,0:T(8,128)(2,1)S(1)}, u32[]{:S(2)}, u32[]{:S(2)}) collective-permute-start(bf16[2,1536,128]{2,1,0:T(8,128)(2,1)S(1)} %collective-permute-done.refs_2_), channel_id=1, source_target_pairs={{0,16},{16,32},{32,48},{48,0},{1,17},{17,33},{33,49},{49,1},{2,18}... | collective-permute-start | bytes 2359304 | tf_op jit(solution)/shard_map/ppermute | solution.py:287
  27.0 0.0 copy-done.2
  27.0 5.2 %attend_0.1 = (f32[2,1024,128]{2,1,0:T(8,128)S(1)}, f32[2,1024,128]{2,1,0:T(8,128)S(1)}) custom-call(s32[9]{0:T(128)S(1)} %copy-done.2, bf16[4,2,32,1024]{3,2,1,0:T(8,128)(2,1)S(1)} %all-to-all-done.refs_1_, bf16[2,1536,128]{2,1,0:T(8,128)(2,1)S(1)} %get-tuple-element.22.refs_2_), custom_call_target="tpu_custom_call" | custom-call | tf_op jit(solution)/shard_map/attend_0/pallas_call | solution.py:197
  32.2 5.3 %attend_3.1 = (f32[2,1024,128]{2,1,0:T(8,128)S(1)}, f32[2,1024,128]{2,1,0:T(8,128)S(1)}) custom-call(s32[9]{0:T(128)S(1)} %copy-done.2, bf16[4,2,32,1024]{3,2,1,0:T(8,128)(2,1)S(1)} %all-to-all-done.refs_1_, bf16[2,1536,128]{2,1,0:T(8,128)(2,1)S(1)} %collective-permute-done.refs_2_, f32[2,1024,128]{2,1,0:T(8,128)S(1)} %get-tuple-element.26.refs_3_, ...), custom_call_target="tpu_custom_call" | custom-call | tf_op jit(solution)/shard_map/attend_3/pallas_call | solution.py:197
  37.5 0.0 collective-permute-done.2.refs_2_
  37.5 5.5 %attend_1.1 = (f32[2,1024,128]{2,1,0:T(8,128)S(1)}, f32[2,1024,128]{2,1,0:T(8,128)S(1)}) custom-call(s32[9]{0:T(128)S(1)} %copy-done.2, bf16[4,2,32,1024]{3,2,1,0:T(8,128)(2,1)S(1)} %all-to-all-done.refs_1_, bf16[2,1536,128]{2,1,0:T(8,128)(2,1)S(1)} %collective-permute-done.2.refs_2_, f32[2,1024,128]{2,1,0:T(8,128)S(1)} %get-tuple-element.28.refs_3_, ...), custom_call_target="tpu_custom_call" | custom-call | tf_op jit(solution)/shard_map/attend_1/pallas_call | solution.py:197
  43.0 3.3 %collective-permute-done.1.refs_2_ = bf16[2,1536,128]{2,1,0:T(8,128)(2,1)S(1)} collective-permute-done((bf16[2,1536,128]{2,1,0:T(8,128)(2,1)S(1)}, bf16[2,1536,128]{2,1,0:T(8,128)(2,1)S(1)}, u32[]{:S(2)}, u32[]{:S(2)}) %collective-permute-start.1) | collective-permute-done | bytes 786464 | tf_op jit(solution)/shard_map/ppermute | solution.py:287
  46.3 0.0 copy-start.1
  46.3 5.5 %attend_2.1 = (bf16[32,2176]{1,0:T(8,128)(2,1)S(1)}, bf16[32,2176]{1,0:T(8,128)(2,1)S(1)}, bf16[32,2176]{1,0:T(8,128)(2,1)S(1)}, bf16[32,2176]{1,0:T(8,128)(2,1)S(1)}) custom-call(s32[9]{0:T(128)S(1)} %copy-done.2, bf16[4,2,32,1024]{3,2,1,0:T(8,128)(2,1)S(1)} %all-to-all-done.refs_1_, bf16[2,1536,128]{2,1,0:T(8,128)(2,1)S(1)} %collective-permute-done.1.refs_2_, ...), custom_call_target="tpu_custom_call" | custom-call | tf_op jit(solution)/shard_map/attend_2/pallas_call | solution.py:197
  51.8 2.6 %collective-permute-start.3 = (bf16[32,2176]{1,0:T(8,128)(2,1)S(1)}, bf16[32,2176]{1,0:T(8,128)(2,1)S(1)}, u32[]{:S(2)}, u32[]{:S(2)}) collective-permute-start(bf16[32,2176]{1,0:T(8,128)(2,1)S(1)} %get-tuple-element.33), channel_id=1, source_target_pairs={{0,4},{4,0},{8,12},{12,8},{1,5},{5,1},{9,13},{13,9},{2,6},{6,2},{1... | collective-permute-start | bytes 417800 | tf_op jit(solution)/shard_map/ppermute | solution.py:316
  54.4 4.3 %collective-permute-start.4 = (bf16[32,2176]{1,0:T(8,128)(2,1)S(1)}, bf16[32,2176]{1,0:T(8,128)(2,1)S(1)}, u32[]{:S(2)}, u32[]{:S(2)}) collective-permute-start(bf16[32,2176]{1,0:T(8,128)(2,1)S(1)} %get-tuple-element.34), channel_id=1, source_target_pairs={{0,8},{4,12},{8,0},{12,4},{1,9},{5,13},{9,1},{13,5},{2,10},{6,14},... | collective-permute-start | bytes 417800 | tf_op jit(solution)/shard_map/ppermute | solution.py:316
  58.7 2.4 %collective-permute-start.5 = (bf16[32,2176]{1,0:T(8,128)(2,1)S(1)}, bf16[32,2176]{1,0:T(8,128)(2,1)S(1)}, u32[]{:S(2)}, u32[]{:S(2)}) collective-permute-start(bf16[32,2176]{1,0:T(8,128)(2,1)S(1)} %get-tuple-element.35), channel_id=1, source_target_pairs={{0,12},{4,8},{8,4},{12,0},{1,13},{5,9},{9,5},{13,1},{2,14},{6,10},... | collective-permute-start | bytes 417800 | tf_op jit(solution)/shard_map/ppermute | solution.py:316
  61.1 0.0 collective-permute-done.3.refs_1_
  61.1 6.0 %collective-permute-done.4.refs_2_ = bf16[32,2176]{1,0:T(8,128)(2,1)S(1)} collective-permute-done((bf16[32,2176]{1,0:T(8,128)(2,1)S(1)}, bf16[32,2176]{1,0:T(8,128)(2,1)S(1)}, u32[]{:S(2)}, u32[]{:S(2)}) %collective-permute-start.4) | collective-permute-done | bytes 139296 | tf_op jit(solution)/shard_map/ppermute | solution.py:316
  67.1 2.6 %collective-permute-done.5.refs_3_ = bf16[32,2176]{1,0:T(8,128)(2,1)S(1)} collective-permute-done((bf16[32,2176]{1,0:T(8,128)(2,1)S(1)}, bf16[32,2176]{1,0:T(8,128)(2,1)S(1)}, u32[]{:S(2)}, u32[]{:S(2)}) %collective-permute-start.5) | collective-permute-done | bytes 139296 | tf_op jit(solution)/shard_map/ppermute | solution.py:316
  69.6 0.0 copy-done.1
  69.6 0.0 copy-start
  69.6 1.1 %merge.1 = (bf16[32,1024]{1,0:T(8,128)(2,1)S(1)}, f32[32,1024]{1,0:T(8,128)S(1)}, f32[32,1024]{1,0:T(8,128)S(1)}) custom-call(s32[9]{0:T(128)S(1)} %copy-done.2, bf16[32,1024]{1,0:T(8,128)(2,1)S(1)} %bitcast.10, bf16[32,2176]{1,0:T(8,128)(2,1)S(1)} %get-tuple-element.32.refs_0_, bf16[32,2176]{1,0:T(8,128)(2,1)S(1)} %collective-permute-done.3.refs_1_, ...), custom_call_target="tpu_custom_call" | custom-call | tf_op jit(solution)/shard_map/merge/pallas_call | solution.py:320
  70.8 5.5 %collective-permute-start.6 = (bf16[32,1024]{1,0:T(8,128)(2,1)S(1)}, bf16[32,1024]{1,0:T(8,128)(2,1)S(1)}, u32[]{:S(2)}, u32[]{:S(2)}) collective-permute-start(bf16[32,1024]{1,0:T(8,128)(2,1)S(1)} %get-tuple-element.37.one_ref), channel_id=1, source_target_pairs={{0,64},{64,128},{128,192},{192,256},{256,320},{320,384},{384,448},... | collective-permute-start | bytes 196616 | tf_op jit(solution)/shard_map/ppermute | solution.py:329
  76.3 1.9 %collective-permute-done.6.passed_ref = bf16[32,1024]{1,0:T(8,128)(2,1)S(1)} collective-permute-done((bf16[32,1024]{1,0:T(8,128)(2,1)S(1)}, bf16[32,1024]{1,0:T(8,128)(2,1)S(1)}, u32[]{:S(2)}, u32[]{:S(2)}) %collective-permute-start.6) | collective-permute-done | bytes 65568 | tf_op jit(solution)/shard_map/ppermute | solution.py:329
  78.1 0.0 copy-done
  78.1 0.9 add.3
  79.0 0.0 copy-start.3
  79.0 11.2 %psum.7.squares_ref = f32[2,32]{1,0:T(2,128)S(1)} all-reduce(f32[2,32]{1,0:T(2,128)S(1)} %get-tuple-element.40), channel_id=1, replica_groups=mesh['section'=8,'cx'=4,'cy'=4,'tp'=4] {'tp'}, use_global_device_ids=true, to_apply=%region_0.0 | all-reduce | flops 64 | bytes 512 | tf_op jit(solution)/shard_map/psum | solution.py:342
  90.2 0.0 copy-done.3
  90.2 0.8 norm.1
Async XLA Ops:
  2.4 22.4 %collective-permute-start = (bf16[2,1536,128]{2,1,0:T(8,128)(2,1)S(1)}, bf16[2,1536,128]{2,1,0:T(8,128)(2,1)S(1)}, u32[]{:S(2)}, u32[]{:S(2)}) collective-permute-start(bf16[2,1536,128]{2,1,0:T(8,128)(2,1)S(1)} %get-tuple-element.22.refs_2_), channel_id=1, source_target_pairs={{0,16},{16,32},{32,48},{48,0},{1,17},{17,33},{33,49},{49,1},{2,18}... | collective-permute-start | bytes 2359304 | tf_op jit(solution)/shard_map/ppermute | solution.py:287
  5.8 21.2 %copy-start.2 = (s32[9]{0:T(128)S(1)}, s32[9]{0:T(128)}, u32[]{:S(2)}) copy-start(s32[9]{0:T(128)} %lengths_ref.1) | copy-start | bytes 112
  5.8 19.0 %all-to-all-start = ((bf16[4,2,32,1024]{3,2,1,0:T(8,128)(2,1)}), bf16[4,2,32,1024]{3,2,1,0:T(8,128)(2,1)S(1)}, u32[]{:S(2)}, u32[]{:S(2)}) async-start(bf16[4,2,32,1024]{3,2,1,0:T(8,128)(2,1)} %get-tuple-element.23), calls=%async_computation | async-start | bytes 1048576 | tf_op jit(solution)/shard_map/all_to_all | solution.py:306
  11.1 26.4 %collective-permute-start.2 = (bf16[2,1536,128]{2,1,0:T(8,128)(2,1)S(1)}, bf16[2,1536,128]{2,1,0:T(8,128)(2,1)S(1)}, u32[]{:S(2)}, u32[]{:S(2)}) collective-permute-start(bf16[2,1536,128]{2,1,0:T(8,128)(2,1)S(1)} %get-tuple-element.22.refs_2_), channel_id=1, source_target_pairs={{0,48},{16,0},{32,16},{48,32},{1,49},{17,1},{33,17},{49,33},{2,50}... | collective-permute-start | bytes 2359304 | tf_op jit(solution)/shard_map/ppermute | solution.py:287
  24.8 21.5 %collective-permute-start.1 = (bf16[2,1536,128]{2,1,0:T(8,128)(2,1)S(1)}, bf16[2,1536,128]{2,1,0:T(8,128)(2,1)S(1)}, u32[]{:S(2)}, u32[]{:S(2)}) collective-permute-start(bf16[2,1536,128]{2,1,0:T(8,128)(2,1)S(1)} %collective-permute-done.refs_2_), channel_id=1, source_target_pairs={{0,16},{16,32},{32,48},{48,0},{1,17},{17,33},{33,49},{49,1},{2,18}... | collective-permute-start | bytes 2359304 | tf_op jit(solution)/shard_map/ppermute | solution.py:287
  46.3 23.3 %copy-start.1 = (bf16[1,32,1024]{2,1,0:T(8,128)(2,1)S(1)}, bf16[1,32,1024]{2,1,0:T(8,128)(2,1)}, u32[]{:S(2)}) copy-start(bf16[1,32,1024]{2,1,0:T(8,128)(2,1)} %param.10) | copy-start | bytes 196612
  51.8 9.2 %collective-permute-start.3 = (bf16[32,2176]{1,0:T(8,128)(2,1)S(1)}, bf16[32,2176]{1,0:T(8,128)(2,1)S(1)}, u32[]{:S(2)}, u32[]{:S(2)}) collective-permute-start(bf16[32,2176]{1,0:T(8,128)(2,1)S(1)} %get-tuple-element.33), channel_id=1, source_target_pairs={{0,4},{4,0},{8,12},{12,8},{1,5},{5,1},{9,13},{13,9},{2,6},{6,2},{1... | collective-permute-start | bytes 417800 | tf_op jit(solution)/shard_map/ppermute | solution.py:316
  54.4 12.6 %collective-permute-start.4 = (bf16[32,2176]{1,0:T(8,128)(2,1)S(1)}, bf16[32,2176]{1,0:T(8,128)(2,1)S(1)}, u32[]{:S(2)}, u32[]{:S(2)}) collective-permute-start(bf16[32,2176]{1,0:T(8,128)(2,1)S(1)} %get-tuple-element.34), channel_id=1, source_target_pairs={{0,8},{4,12},{8,0},{12,4},{1,9},{5,13},{9,1},{13,5},{2,10},{6,14},... | collective-permute-start | bytes 417800 | tf_op jit(solution)/shard_map/ppermute | solution.py:316
  58.7 10.9 %collective-permute-start.5 = (bf16[32,2176]{1,0:T(8,128)(2,1)S(1)}, bf16[32,2176]{1,0:T(8,128)(2,1)S(1)}, u32[]{:S(2)}, u32[]{:S(2)}) collective-permute-start(bf16[32,2176]{1,0:T(8,128)(2,1)S(1)} %get-tuple-element.35), channel_id=1, source_target_pairs={{0,12},{4,8},{8,4},{12,0},{1,13},{5,9},{9,5},{13,1},{2,14},{6,10},... | collective-permute-start | bytes 417800 | tf_op jit(solution)/shard_map/ppermute | solution.py:316
  69.6 8.5 %copy-start = (bf16[32,1024]{1,0:T(8,128)(2,1)S(1)}, bf16[32,1024]{1,0:T(8,128)(2,1)}, u32[]{:S(2)}) copy-start(bf16[32,1024]{1,0:T(8,128)(2,1)} %fresh_ref.1) | copy-start | bytes 196612
  70.8 7.4 %collective-permute-start.6 = (bf16[32,1024]{1,0:T(8,128)(2,1)S(1)}, bf16[32,1024]{1,0:T(8,128)(2,1)S(1)}, u32[]{:S(2)}, u32[]{:S(2)}) collective-permute-start(bf16[32,1024]{1,0:T(8,128)(2,1)S(1)} %get-tuple-element.37.one_ref), channel_id=1, source_target_pairs={{0,64},{64,128},{128,192},{192,256},{256,320},{320,384},{384,448},... | collective-permute-start | bytes 196616 | tf_op jit(solution)/shard_map/ppermute | solution.py:329
  79.0 11.2 %copy-start.3 = (bf16[1,1024]{1,0:T(2,128)(2,1)S(1)}, bf16[1,1024]{1,0:T(2,128)(2,1)}, u32[]{:S(2)}) copy-start(bf16[1,1024]{1,0:T(2,128)(2,1)} %gain_ref.1) | copy-start | bytes 6148

commit v3 on v2

v3 whole, which is shorter than its diff:
```python
import functools

import jax
import jax.numpy as jnp
import numpy as np
from jax import lax
from jax.experimental import pallas as pl
from jax.experimental.pallas import tpu as pltpu
from jax.sharding import Mesh
from jax.sharding import PartitionSpec as P

HD = 128
NX, NY = 4, 4
HEADS_DEV = 8
ROWS = 32
WIDTH_DEV = HEADS_DEV * HD
KEYS = 1536
CTX = KEYS * NX * NY
N_SEG = 9
FULL_WIDTH = 4096
PACKED = 2 * WIDTH_DEV + 128
TILE = 1536
BLOCK = 2 * HEADS_DEV * ROWS
HALF = 2 * BLOCK
NEGATIVE = -1e30
FLOOR = -1e28
TINY = 1e-30
EPSILON = 1e-05
LOG2_SCALE = float(np.log2(np.e) / np.sqrt(HD))
VMEM_LIMIT = 24 * 2**20
LARGE = pltpu.CompilerParams(vmem_limit_bytes=VMEM_LIMIT)
SMALL = pltpu.CompilerParams(vmem_limit_bytes=4 * 2**20)


SMEM = pl.BlockSpec(memory_space=pltpu.SMEM)
VMEM = pl.BlockSpec(memory_space=pltpu.VMEM)
ANY = pl.BlockSpec(memory_space=pl.ANY)


def segment_of(tick):
    return 7 - lax.axis_index("section") + tick


def segment_start(lengths_ref, segment):
    start = jnp.int32(CTX)
    for j in range(N_SEG):
        start = start - jnp.where(j >= segment, lengths_ref[j], 0)
    return start


def update(q, k_ref, v_ref, last_offset, out_ref, top_ref, total_ref):
    def one(t, _):
        tile = pl.ds(pl.multiple_of(t * TILE, TILE), TILE)
        s = lax.dot_general(
            q, k_ref[tile], (((1,), (1,)), ((), ())), preferred_element_type=jnp.float32
        )
        if last_offset is not None:
            offset = t * TILE + lax.broadcasted_iota(jnp.int32, (1, TILE), 1)
            s = jnp.where(offset <= last_offset, s, NEGATIVE)
        part = s[:, :HD]
        for u in range(1, TILE // HD):
            part = jnp.maximum(part, s[:, u * HD : (u + 1) * HD])
        top = top_ref[...]
        tile_top = jnp.max(part, axis=1, keepdims=True) * LOG2_SCALE
        new_top = jnp.maximum(top, jnp.broadcast_to(tile_top, top.shape))
        groups = [
            jnp.exp2(s[:, u * HD : (u + 1) * HD] * LOG2_SCALE - new_top)
            for u in range(TILE // HD)
        ]
        lane_sum = functools.reduce(jnp.add, groups)
        p = jnp.concatenate([group.astype(jnp.bfloat16) for group in groups], 1)
        mixed = jnp.dot(p, v_ref[tile], preferred_element_type=jnp.float32)
        rescale = jnp.exp2(top - new_top)
        out_ref[...] = out_ref[...] * rescale + mixed
        total_ref[...] = total_ref[...] * rescale + lane_sum
        top_ref[...] = new_top

    lax.fori_loop(0, KEYS // TILE, one, None)


def finished(out_ref, top_ref, total_ref):
    total = jnp.maximum(jnp.sum(total_ref[...], axis=1, keepdims=True), TINY)
    return out_ref[...] * (1.0 / total), top_ref[...] + jnp.log2(total)


def write_packed(state, outs):
    out, level = state
    out = out.astype(jnp.bfloat16)
    lane = lax.broadcasted_iota(jnp.int32, (ROWS, 128), 1)
    head = lane % HEADS_DEV
    piece = lane % (3 * HEADS_DEV) // HEADS_DEV
    for i, o_ref in enumerate(outs):
        levels = jnp.zeros((ROWS, 128), jnp.float32)
        for tick in range(2):
            mine = lane // (3 * HEADS_DEV) == tick
            for h in range(HEADS_DEV):
                at = ((i * 2 + tick) * HEADS_DEV + h) * ROWS
                column = tick * WIDTH_DEV + h * HD
                o_ref[:, column : column + HD] = out[at : at + ROWS]
                levels = jnp.where(jnp.logical_and(mine, head == h), level[at : at + ROWS], levels)
        high = levels.astype(jnp.bfloat16).astype(jnp.float32)
        middle = (levels - high).astype(jnp.bfloat16).astype(jnp.float32)
        low = levels - high - middle
        pieces = jnp.where(piece == 0, high, jnp.where(piece == 1, middle, low))
        o_ref[:, 2 * WIDTH_DEV :] = pieces.astype(jnp.bfloat16)


def attend_rows(first_d, n_d, shift, lengths_ref, q_ref, k_ref, v_ref, state):
    cx = lax.axis_index("cx")
    cy = lax.axis_index("cy")
    base = cx * NY * ROWS - ((cx + shift) % NX * NY + cy) * KEYS
    least = [segment_start(lengths_ref, segment_of(tick)) + base for tick in range(2)]
    full = jnp.minimum(least[0], least[1]) >= KEYS - 1
    none = jnp.maximum(least[0], least[1]) + NY * ROWS - 1 < 0

    def run(masked):
        q = jnp.concatenate(
            [
                q_ref[cy ^ (first_d + i), tick, :, h * HD : (h + 1) * HD]
                for i in range(n_d)
                for tick in range(2)
                for h in range(HEADS_DEV)
            ],
            0,
        )
        last_offset = None
        if masked:
            row_id = lax.broadcasted_iota(jnp.int32, (n_d * BLOCK, 1), 0)
            owner = (first_d + row_id // BLOCK) ^ cy
            second = row_id // (BLOCK // 2) % 2 == 1
            last_offset = jnp.where(second, least[1], least[0]) + owner * ROWS + row_id % ROWS
        update(q, k_ref, v_ref, last_offset, *state)

    @pl.when(full)
    def _():
        run(False)

    @pl.when(jnp.logical_not(jnp.logical_or(full, none)))
    def _():
        run(True)


def first_kernel(lengths_ref, q_ref, k_ref, v_ref, out_ref, top_ref, total_ref):
    out_ref[...] = jnp.zeros(out_ref.shape, jnp.float32)
    top_ref[...] = jnp.full(top_ref.shape, FLOOR, jnp.float32)
    total_ref[...] = jnp.zeros(total_ref.shape, jnp.float32)

    def one(half, _):
        state = [ref.at[half] for ref in (out_ref, top_ref, total_ref)]
        attend_rows(2 * half, 2, 0, lengths_ref, q_ref, k_ref, v_ref, state)

    lax.fori_loop(0, 2, one, None)


def second_kernel(lengths_ref, q_ref, k_ref, v_ref, *refs):
    inputs, outs = refs[:3], refs[3:]

    def one(half, _):
        for source, target in zip(inputs, outs, strict=True):
            target[half] = source[half]
        state = [ref.at[half] for ref in outs]
        attend_rows(2 * half, 2, NX - 1, lengths_ref, q_ref, k_ref, v_ref, state)

    lax.fori_loop(0, 2, one, None)


def last_kernel(first_d, n_d, *refs):
    lengths_ref, q_ref, k_above, v_above, k_far, v_far = refs[:6]
    inputs, outs, state = refs[6:9], refs[9 : 9 + n_d], refs[9 + n_d :]
    begin = first_d % 2 * BLOCK
    for source, target in zip(inputs, state, strict=True):
        target[...] = source[first_d // 2, begin : begin + n_d * BLOCK]
    attend_rows(first_d, n_d, 1, lengths_ref, q_ref, k_above, v_above, state)
    attend_rows(first_d, n_d, 2, lengths_ref, q_ref, k_far, v_far, state)
    write_packed(finished(*state), outs)


def in_vmem(x):
    return pltpu.with_memory_space_constraint(x, pltpu.VMEM)


def in_hbm(x):
    return pltpu.with_memory_space_constraint(x, pltpu.HBM)


def attend_first(lengths, q_all, k, v):
    return pl.pallas_call(
        first_kernel,
        in_specs=[SMEM] + [VMEM] * 3,
        out_specs=[VMEM] * 3,
        out_shape=[pltpu.VMEM((2, HALF, HD), jnp.float32)] * 3,
        compiler_params=LARGE,
        name="attend_own",
    )(lengths, in_vmem(q_all), in_vmem(k), in_vmem(v))


def attend_second(lengths, *operands):
    return pl.pallas_call(
        second_kernel,
        in_specs=[SMEM] + [VMEM] * len(operands),
        out_specs=[VMEM] * 3,
        out_shape=[pltpu.VMEM((2, HALF, HD), jnp.float32)] * 3,
        compiler_params=LARGE,
        name="attend_below",
    )(lengths, *[in_vmem(x) for x in operands])


def attend_last(first_d, n_d, lengths, *operands):
    return pl.pallas_call(
        functools.partial(last_kernel, first_d, n_d),
        in_specs=[SMEM] + [VMEM] * len(operands),
        out_specs=[VMEM] * n_d,
        out_shape=[pltpu.VMEM((ROWS, PACKED), jnp.bfloat16)] * n_d,
        scratch_shapes=[pltpu.VMEM((n_d * BLOCK, HD), jnp.float32)] * 3,
        compiler_params=LARGE,
        name=f"attend_last_{first_d}",
    )(lengths, *[in_vmem(x) for x in operands])


def merged(parts, tick, live):
    levels = []
    for part_ref in parts:
        pieces = part_ref[:, 2 * WIDTH_DEV :].astype(jnp.float32)
        levels.append(
            pieces
            + pltpu.roll(pieces, 128 - HEADS_DEV, 1)
            + pltpu.roll(pieces, 128 - 2 * HEADS_DEV, 1)
        )
    top = functools.reduce(jnp.maximum, levels)
    shares = [jnp.exp2(level - top) for level in levels]
    inverse = 1.0 / functools.reduce(jnp.add, shares)
    shares = [share * inverse for share in shares]
    columns = []
    for h in range(HEADS_DEV):
        total = jnp.zeros((ROWS, HD), jnp.float32)
        column = tick * WIDTH_DEV + h * HD
        lane = tick * 3 * HEADS_DEV + h
        for part_ref, share in zip(parts, shares, strict=True):
            part = part_ref[:, column : column + HD].astype(jnp.float32)
            total = total + share[:, lane : lane + 1] * part
        columns.append(total)
    return jnp.where(live, jnp.concatenate(columns, 1), 0.0)


def live_rows(lengths_ref, tick):
    first = (lax.axis_index("cx") * NY + lax.axis_index("cy")) * ROWS
    row = first + lax.broadcasted_iota(jnp.int32, (ROWS, 1), 0)
    return row < lengths_ref[segment_of(tick)]


def merge_one_kernel(lengths_ref, rows_ref, *refs):
    parts, (residual_ref, sum_ref) = refs[:NY], refs[NY:]
    total = rows_ref[...].astype(jnp.float32) + merged(parts, 0, live_rows(lengths_ref, 0))
    sum_ref[...] = total
    residual_ref[...] = total.astype(jnp.bfloat16)


def merge_two_kernel(lengths_ref, *refs):
    parts, attended_ref = refs[:NY], refs[NY]
    attended_ref[...] = merged(parts, 1, live_rows(lengths_ref, 1))


def add_kernel(attended_ref, passed_ref, fresh_ref, sum_one_ref, sum_ref, squares_ref):
    first = lax.axis_index("section") == 0
    incoming = jnp.where(first, fresh_ref[...].astype(jnp.float32), passed_ref[...].astype(jnp.float32))
    total = incoming + attended_ref[...]
    sum_ref[...] = total
    ones = jnp.ones((8, WIDTH_DEV), jnp.float32)
    for tick, rows in enumerate((sum_one_ref[...], total)):
        squares = lax.dot_general(
            ones,
            rows * rows,
            (((1,), (1,)), ((), ())),
            precision=lax.Precision.HIGHEST,
            preferred_element_type=jnp.float32,
        )
        squares_ref[tick : tick + 1, :] = squares[:1]


def norm_kernel(squares_ref, sum_one_ref, sum_two_ref, gain_ref, residual_ref, normed_ref):
    gain = gain_ref[...].astype(jnp.float32)
    row = lax.broadcasted_iota(jnp.int32, (ROWS, ROWS), 0)
    lane = lax.broadcasted_iota(jnp.int32, (ROWS, ROWS), 1)
    for tick, sum_ref in enumerate((sum_one_ref, sum_two_ref)):
        scale = lax.rsqrt(squares_ref[tick : tick + 1, :] / FULL_WIDTH + EPSILON)
        column = jnp.sum(jnp.where(row == lane, scale, 0.0), axis=1, keepdims=True)
        residual_ref[tick] = sum_ref[...].astype(jnp.bfloat16)
        normed_ref[tick] = (sum_ref[...] * column * gain).astype(jnp.bfloat16)


def body(queries, key_rows, value_rows, section_rows, fresh_rows, norm_gain, segment_lengths):
    def along_x(value, by):
        return lax.ppermute(value, "cx", [(i, (i + by) % NX) for i in range(NX)])

    def across_y(value, d):
        return lax.ppermute(value, "cy", [(i, i ^ d) for i in range(NY)])

    k, v = key_rows[0], value_rows[0]
    k_below = along_x(k, 1)
    v_above = along_x(v, -1)
    q_own = jnp.broadcast_to(queries[:, 0], (NY, 2, ROWS, WIDTH_DEV))
    q_all = lax.all_to_all(q_own, "cy", 0, 0)
    v_below = along_x(v, 1)
    k_above = along_x(k, -1)
    k_far = along_x(k_below, 1)
    v_far = along_x(v_above, -1)

    state = attend_first(segment_lengths, q_all, k, v)
    state = attend_second(segment_lengths, q_all, k_below, v_below, *state)
    operands = (segment_lengths, q_all, k_above, v_above, k_far, v_far, *state)
    part_two, part_three = attend_last(2, 2, *operands)
    part_three = across_y(part_three, 3)
    part_two = across_y(part_two, 2)
    (part_one,) = attend_last(1, 1, *operands)
    part_one = across_y(part_one, 1)
    (part_own,) = attend_last(0, 1, *operands)
    parts = (part_own, part_one, part_two, part_three)

    rows_bf16 = pltpu.VMEM((ROWS, WIDTH_DEV), jnp.bfloat16)
    rows_f32 = pltpu.VMEM((ROWS, WIDTH_DEV), jnp.float32)
    parts = [in_vmem(part) for part in parts]
    residual_one, sum_one = pl.pallas_call(
        merge_one_kernel,
        in_specs=[SMEM] + [VMEM] * (1 + NY),
        out_specs=[VMEM] * 2,
        out_shape=[rows_bf16, rows_f32],
        compiler_params=SMALL,
        name="merge_one",
    )(segment_lengths, in_vmem(section_rows[0]), *parts)
    attended_two = pl.pallas_call(
        merge_two_kernel,
        in_specs=[SMEM] + [VMEM] * NY,
        out_specs=VMEM,
        out_shape=rows_f32,
        compiler_params=SMALL,
        name="merge_two",
    )(segment_lengths, *parts)
    count = lax.axis_size("section")
    passed = lax.ppermute(residual_one, "section", [(i, i + 1) for i in range(count - 1)])
    sum_two, squares = pl.pallas_call(
        add_kernel,
        in_specs=[VMEM] * 4,
        out_specs=[VMEM] * 2,
        out_shape=[rows_f32, pltpu.VMEM((2, ROWS), jnp.float32)],
        compiler_params=SMALL,
        name="add",
    )(*[in_vmem(x) for x in (attended_two, passed, fresh_rows, sum_one)])
    squares = lax.psum(squares, "tp")
    residual, normed = pl.pallas_call(
        norm_kernel,
        in_specs=[VMEM] * 4,
        out_specs=[VMEM] * 2,
        out_shape=[jax.ShapeDtypeStruct((2, ROWS, WIDTH_DEV), jnp.bfloat16)] * 2,
        compiler_params=SMALL,
        name="norm",
    )(in_vmem(squares), in_vmem(sum_one), in_vmem(sum_two), in_vmem(norm_gain))
    return residual[:, None], normed[:, None]


def solution(mesh):
    grid = Mesh(mesh.devices.reshape(8, NX, NY, 4), ("section", "cx", "cy", "tp"))
    cp = ("cx", "cy")
    in_specs = (
        P(None, "section", cp, "tp"),
        P("section", cp, "tp"),
        P("section", cp, "tp"),
        P("section", cp, "tp"),
        P(cp, "tp"),
        P("section", "tp"),
        P(),
    )
    out_specs = (P(None, "section", cp, "tp"), P(None, "section", cp, "tp"))
    return jax.shard_map(body, mesh=grid, in_specs=in_specs, out_specs=out_specs, check_vma=False)
```

time: 91.3 us -> 86.7 us (0.950)
  the two profiles are of different devices: /device:TPU:200 before, /device:TPU:249 now
where the time goes in v3:
time: 86.7 us; the launch traced here: 86.1 us
  starting transfers between devices  39.2 us (45%)
  Pallas kernels  26.9 us (31%)
  blocking collectives  13.2 us (15%)
  waiting for transfers between devices  4.21 us (5%)
  local copies, waits for them, and re-layouts  1.78 us (2%)
    ppermute x6, starting transfers between devices, along_x(): return lax.ppermute(value, 'cx', [(i, (i + by) % NX) for i in range(NX)])  19.1 us
    psum x1, blocking collectives, body(): squares = lax.psum(squares, 'tp')  13.2 us
    pallas_call x3, Pallas kernels, attend_last(): pl.pallas_call(functools.partial(last_kernel, first_d, n_d), in_specs=[SM...  12.1 us
    ppermute x3, starting transfers between devices, across_y(): return lax.ppermute(value, 'cy', [(i, i ^ d) for i in range(NY)])  8.5 us
    all_to_all x1, starting transfers between devices, body(): q_all = lax.all_to_all(q_own, 'cy', 0, 0)  6.21 us
    pallas_call x1, Pallas kernels, attend_second(): pl.pallas_call(second_kernel, in_specs=[SMEM] + [VMEM] * len(operands), o...  6.07 us
    pallas_call x1, Pallas kernels, attend_first(): pl.pallas_call(first_kernel, in_specs=[SMEM] + [VMEM] * 3, out_specs=[VME...  5.89 us
    ppermute x1, starting transfers between devices, body(): lax.ppermute(residual_one, 'section', [(i, i + 1) for i in range(count -...  5.34 us
  transfers between devices with their start and end apart: 11, of which 4 were waited for; matrix products, arithmetic and copies ran while one was open for 0% of the time, Pallas kernels for 23%

profile of v3, /device:TPU:249, one launch (start us, length us, event | category | flops | bytes accessed | tf_op | source)
XLA Modules:
  0.0 86.1 jit_solution(13029015121848034587)
XLA Ops:
  0.6 1.8 %broadcast_in_dim.9 = bf16[4,2,32,1024]{3,2,1,0:T(8,128)(2,1)} broadcast(bf16[2,32,1024]{2,1,0:T(8,128)(2,1)} %bitcast.14), dimensions={1,2,3} | broadcast | bytes 655360 | tf_op jit(solution)/shard_map/broadcast_in_dim | solution.py:301
  2.4 0.0 copy-start
  2.4 6.2 %all-to-all-start = ((bf16[4,2,32,1024]{3,2,1,0:T(8,128)(2,1)}), bf16[4,2,32,1024]{3,2,1,0:T(8,128)(2,1)S(1)}, u32[]{:S(2)}, u32[]{:S(2)}) async-start(bf16[4,2,32,1024]{3,2,1,0:T(8,128)(2,1)} %broadcast_in_dim.9), calls=%async_computation | async-start | bytes 1048576 | tf_op jit(solution)/shard_map/all_to_all | solution.py:302
  8.6 0.0 copy-done
  8.6 0.0 copy-start.3
  8.6 4.5 %collective-permute-start.1 = (bf16[1536,128]{1,0:T(8,128)(2,1)S(1)}, bf16[1536,128]{1,0:T(8,128)(2,1)S(1)}, u32[]{:S(2)}, u32[]{:S(2)}) collective-permute-start(bf16[1536,128]{1,0:T(8,128)(2,1)S(1)} %bitcast.10), channel_id=1, source_target_pairs={{0,48},{16,0},{32,16},{48,32},{1,49},{17,1},{33,17},{49,33},{2,50}... | collective-permute-start | bytes 1179656 | tf_op jit(solution)/shard_map/ppermute | solution.py:293
  13.1 1.9 %collective-permute-start.2 = (bf16[1536,128]{1,0:T(8,128)(2,1)}, bf16[1536,128]{1,0:T(8,128)(2,1)S(1)}, u32[]{:S(2)}, u32[]{:S(2)}) collective-permute-start(bf16[1536,128]{1,0:T(8,128)(2,1)} %bitcast.1.k_ref), channel_id=1, source_target_pairs={{0,16},{16,32},{32,48},{48,0},{1,17},{17,33},{33,49},{49,1},{2,18}... | collective-permute-start | bytes 1179656 | tf_op jit(solution)/shard_map/ppermute | solution.py:293
  15.0 2.1 %collective-permute-start.5 = (bf16[1536,128]{1,0:T(8,128)(2,1)S(1)}, bf16[1536,128]{1,0:T(8,128)(2,1)S(1)}, u32[]{:S(2)}, u32[]{:S(2)}) collective-permute-start(bf16[1536,128]{1,0:T(8,128)(2,1)S(1)} %bitcast.11), channel_id=1, source_target_pairs={{0,16},{16,32},{32,48},{48,0},{1,17},{17,33},{33,49},{49,1},{2,18}... | collective-permute-start | bytes 1179656 | tf_op jit(solution)/shard_map/ppermute | solution.py:293
  17.2 4.4 %collective-permute-start = (bf16[1536,128]{1,0:T(8,128)(2,1)}, bf16[1536,128]{1,0:T(8,128)(2,1)S(1)}, u32[]{:S(2)}, u32[]{:S(2)}) collective-permute-start(bf16[1536,128]{1,0:T(8,128)(2,1)} %bitcast.1.k_ref), channel_id=1, source_target_pairs={{0,48},{16,0},{32,16},{48,32},{1,49},{17,1},{33,17},{49,33},{2,50}... | collective-permute-start | bytes 1179656 | tf_op jit(solution)/shard_map/ppermute | solution.py:293
  21.6 0.0 collective-permute-done.1.refs_3_
  21.6 4.3 %collective-permute-start.4 = (bf16[1536,128]{1,0:T(8,128)(2,1)S(1)}, bf16[1536,128]{1,0:T(8,128)(2,1)S(1)}, u32[]{:S(2)}, u32[]{:S(2)}) collective-permute-start(bf16[1536,128]{1,0:T(8,128)(2,1)S(1)} %collective-permute-done.1.refs_3_), channel_id=1, source_target_pairs={{0,48},{16,0},{32,16},{48,32},{1,49},{17,1},{33,17},{49,33},{2,50}... | collective-permute-start | bytes 1179656 | tf_op jit(solution)/shard_map/ppermute | solution.py:293
  25.9 0.0 collective-permute-done.2.k_ref
  25.9 1.9 %collective-permute-start.3 = (bf16[1536,128]{1,0:T(8,128)(2,1)S(1)}, bf16[1536,128]{1,0:T(8,128)(2,1)S(1)}, u32[]{:S(2)}, u32[]{:S(2)}) collective-permute-start(bf16[1536,128]{1,0:T(8,128)(2,1)S(1)} %collective-permute-done.2.k_ref), channel_id=1, source_target_pairs={{0,16},{16,32},{32,48},{48,0},{1,17},{17,33},{33,49},{49,1},{2,18}... | collective-permute-start | bytes 1179656 | tf_op jit(solution)/shard_map/ppermute | solution.py:293
  27.8 0.0 all-to-all-done.q_ref.refs_1_
  27.8 0.0 copy-done.3
  27.8 5.9 %attend_own.1 = (f32[2,1024,128]{2,1,0:T(8,128)S(1)}, f32[2,1024,128]{2,1,0:T(8,128)S(1)}, f32[2,1024,128]{2,1,0:T(8,128)S(1)}) custom-call(s32[9]{0:T(128)S(1)} %copy-done.3, bf16[4,2,32,1024]{3,2,1,0:T(8,128)(2,1)S(1)} %all-to-all-done.q_ref.refs_1_, bf16[1536,128]{1,0:T(8,128)(2,1)} %bitcast.1.k_ref, bf16[1536,128]{1,0:T(8,128)(2,1)S(1)} %bitcast.12), custom_call_target="tpu_custom_call" | custom-call | tf_op jit(solution)/shard_map/attend_own/pallas_call | solution.py:187
  33.7 0.5 collective-permute-done.5.v_ref
  34.2 6.1 %attend_below.1 = (f32[2,1024,128]{2,1,0:T(8,128)S(1)}, f32[2,1024,128]{2,1,0:T(8,128)S(1)}, f32[2,1024,128]{2,1,0:T(8,128)S(1)}) custom-call(s32[9]{0:T(128)S(1)} %copy-done.3, bf16[4,2,32,1024]{3,2,1,0:T(8,128)(2,1)S(1)} %all-to-all-done.q_ref.refs_1_, bf16[1536,128]{1,0:T(8,128)(2,1)S(1)} %collective-permute-done.2.k_ref, ...), custom_call_target="tpu_custom_call" | custom-call | tf_op jit(solution)/shard_map/attend_below/pallas_call | solution.py:198
  40.3 0.0 collective-permute-done.refs_2_
  40.3 0.0 collective-permute-done.4.refs_5_
  40.3 2.3 %collective-permute-done.3.refs_4_ = bf16[1536,128]{1,0:T(8,128)(2,1)S(1)} collective-permute-done((bf16[1536,128]{1,0:T(8,128)(2,1)S(1)}, bf16[1536,128]{1,0:T(8,128)(2,1)S(1)}, u32[]{:S(2)}, u32[]{:S(2)}) %collective-permute-start.3) | collective-permute-done | bytes 393248 | tf_op jit(solution)/shard_map/ppermute | solution.py:293
  42.7 5.4 %attend_last_2.1 = (bf16[32,2176]{1,0:T(8,128)(2,1)S(1)}, bf16[32,2176]{1,0:T(8,128)(2,1)S(1)}) custom-call(s32[9]{0:T(128)S(1)} %copy-done.3, bf16[4,2,32,1024]{3,2,1,0:T(8,128)(2,1)S(1)} %all-to-all-done.q_ref.refs_1_, bf16[1536,128]{1,0:T(8,128)(2,1)S(1)} %collective-permute-done.refs_2_, bf16[1536,128]{1,0:T(8,128)(2,1)S(1)} %collective-permute-done.1.refs_3_, ...), custom_call_target="tpu_custom_call" | custom-call | tf_op jit(solution)/shard_map/attend_last_2/pallas_call | solution.py:209
  48.1 2.2 %collective-permute-start.7 = (bf16[32,2176]{1,0:T(8,128)(2,1)S(1)}, bf16[32,2176]{1,0:T(8,128)(2,1)S(1)}, u32[]{:S(2)}, u32[]{:S(2)}) collective-permute-start(bf16[32,2176]{1,0:T(8,128)(2,1)S(1)} %get-tuple-element.22), channel_id=1, source_target_pairs={{0,8},{4,12},{8,0},{12,4},{1,9},{5,13},{9,1},{13,5},{2,10},{6,14},... | collective-permute-start | bytes 417800 | tf_op jit(solution)/shard_map/ppermute | solution.py:296
  50.3 4.0 %collective-permute-start.8 = (bf16[32,2176]{1,0:T(8,128)(2,1)S(1)}, bf16[32,2176]{1,0:T(8,128)(2,1)S(1)}, u32[]{:S(2)}, u32[]{:S(2)}) collective-permute-start(bf16[32,2176]{1,0:T(8,128)(2,1)S(1)} %get-tuple-element.23), channel_id=1, source_target_pairs={{0,12},{4,8},{8,4},{12,0},{1,13},{5,9},{9,5},{13,1},{2,14},{6,10},... | collective-permute-start | bytes 417800 | tf_op jit(solution)/shard_map/ppermute | solution.py:296
  54.3 3.5 %attend_last_1.1 = bf16[32,2176]{1,0:T(8,128)(2,1)S(1)} custom-call(s32[9]{0:T(128)S(1)} %copy-done.3, bf16[4,2,32,1024]{3,2,1,0:T(8,128)(2,1)S(1)} %all-to-all-done.q_ref.refs_1_, bf16[1536,128]{1,0:T(8,128)(2,1)S(1)} %collective-permute-done.refs_2_, bf16[1536,128]{1,0:T(8,128)(2,1)S(1)} %collective-permute-done.1.refs_3_, ...), custom_call_target="tpu_custom_call" | custom-call | tf_op jit(solution)/shard_map/attend_last_1/pallas_call | solution.py:209
  57.8 0.0 copy-start.2
  57.8 2.3 %collective-permute-start.6 = (bf16[32,2176]{1,0:T(8,128)(2,1)S(1)}, bf16[32,2176]{1,0:T(8,128)(2,1)S(1)}, u32[]{:S(2)}, u32[]{:S(2)}) collective-permute-start(bf16[32,2176]{1,0:T(8,128)(2,1)S(1)} %attend_last_1.1), channel_id=1, source_target_pairs={{0,4},{4,0},{8,12},{12,8},{1,5},{5,1},{9,13},{13,9},{2,6},{6,2},{1... | collective-permute-start | bytes 417800 | tf_op jit(solution)/shard_map/ppermute | solution.py:296
  60.1 3.2 %attend_last_0.1.refs_0_ = bf16[32,2176]{1,0:T(8,128)(2,1)S(1)} custom-call(s32[9]{0:T(128)S(1)} %copy-done.3, bf16[4,2,32,1024]{3,2,1,0:T(8,128)(2,1)S(1)} %all-to-all-done.q_ref.refs_1_, bf16[1536,128]{1,0:T(8,128)(2,1)S(1)} %collective-permute-done.refs_2_, bf16[1536,128]{1,0:T(8,128)(2,1)S(1)} %collective-permute-done.1.refs_3_, ...), custom_call_target="tpu_custom_call" | custom-call | tf_op jit(solution)/shard_map/attend_last_0/pallas_call | solution.py:209
  63.4 0.0 collective-permute-done.7.refs_2_
  63.4 0.0 collective-permute-done.8.refs_3_
  63.4 0.9 %collective-permute-done.6.refs_1_ = bf16[32,2176]{1,0:T(8,128)(2,1)S(1)} collective-permute-done((bf16[32,2176]{1,0:T(8,128)(2,1)S(1)}, bf16[32,2176]{1,0:T(8,128)(2,1)S(1)}, u32[]{:S(2)}, u32[]{:S(2)}) %collective-permute-start.6) | collective-permute-done | bytes 139296 | tf_op jit(solution)/shard_map/ppermute | solution.py:296
  64.3 0.0 copy-done.2
  64.3 0.9 %merge_one.1 = (bf16[32,1024]{1,0:T(8,128)(2,1)S(1)}, f32[32,1024]{1,0:T(8,128)S(1)}) custom-call(s32[9]{0:T(128)S(1)} %copy-done.3, bf16[32,1024]{1,0:T(8,128)(2,1)S(1)} %bitcast.13, bf16[32,2176]{1,0:T(8,128)(2,1)S(1)} %attend_last_0.1.refs_0_, bf16[32,2176]{1,0:T(8,128)(2,1)S(1)} %collective-permute-done.6.refs_1_, ...), custom_call_target="tpu_custom_call" | custom-call | tf_op jit(solution)/shard_map/merge_one/pallas_call | solution.py:322
  65.2 0.0 copy-start.1
  65.2 5.3 %collective-permute-start.9 = (bf16[32,1024]{1,0:T(8,128)(2,1)S(1)}, bf16[32,1024]{1,0:T(8,128)(2,1)S(1)}, u32[]{:S(2)}, u32[]{:S(2)}) collective-permute-start(bf16[32,1024]{1,0:T(8,128)(2,1)S(1)} %get-tuple-element.24), channel_id=1, source_target_pairs={{0,64},{64,128},{128,192},{192,256},{256,320},{320,384},{384,448},... | collective-permute-start | bytes 196616 | tf_op jit(solution)/shard_map/ppermute | solution.py:339
  70.6 0.9 %merge_two.1.attended_ref = f32[32,1024]{1,0:T(8,128)S(1)} custom-call(s32[9]{0:T(128)S(1)} %copy-done.3, bf16[32,2176]{1,0:T(8,128)(2,1)S(1)} %attend_last_0.1.refs_0_, bf16[32,2176]{1,0:T(8,128)(2,1)S(1)} %collective-permute-done.6.refs_1_, bf16[32,2176]{1,0:T(8,128)(2,1)S(1)} %collective-permute-done.7.refs_2_, ...), custom_call_target="tpu_custom_call" | custom-call | tf_op jit(solution)/shard_map/merge_two/pallas_call | solution.py:330
  71.4 0.4 collective-permute-done.9.passed_ref
  71.9 0.0 copy-done.1
  71.9 0.3 add.3
  72.2 0.0 copy-start.4
  72.2 13.2 %psum.7.squares_ref = f32[2,32]{1,0:T(2,128)S(1)} all-reduce(f32[2,32]{1,0:T(2,128)S(1)} %get-tuple-element.26), channel_id=1, replica_groups=mesh['section'=8,'cx'=4,'cy'=4,'tp'=4] {'tp'}, use_global_device_ids=true, to_apply=%region_0.0 | all-reduce | flops 64 | bytes 512 | tf_op jit(solution)/shard_map/psum | solution.py:348
  85.3 0.0 copy-done.4
  85.3 0.8 norm.1
Async XLA Ops:
  2.4 6.2 %copy-start = (bf16[1,1536,128]{2,1,0:T(8,128)(2,1)S(1)}, bf16[1,1536,128]{2,1,0:T(8,128)(2,1)}, u32[]{:S(2)}) copy-start(bf16[1,1536,128]{2,1,0:T(8,128)(2,1)} %param.9) | copy-start | bytes 1179652
  2.4 25.4 %all-to-all-start = ((bf16[4,2,32,1024]{3,2,1,0:T(8,128)(2,1)}), bf16[4,2,32,1024]{3,2,1,0:T(8,128)(2,1)S(1)}, u32[]{:S(2)}, u32[]{:S(2)}) async-start(bf16[4,2,32,1024]{3,2,1,0:T(8,128)(2,1)} %broadcast_in_dim.9), calls=%async_computation | async-start | bytes 1048576 | tf_op jit(solution)/shard_map/all_to_all | solution.py:302
  8.6 19.2 %copy-start.3 = (s32[9]{0:T(128)S(1)}, s32[9]{0:T(128)}, u32[]{:S(2)}) copy-start(s32[9]{0:T(128)} %lengths_ref.7) | copy-start | bytes 112
  8.6 13.0 %collective-permute-start.1 = (bf16[1536,128]{1,0:T(8,128)(2,1)S(1)}, bf16[1536,128]{1,0:T(8,128)(2,1)S(1)}, u32[]{:S(2)}, u32[]{:S(2)}) collective-permute-start(bf16[1536,128]{1,0:T(8,128)(2,1)S(1)} %bitcast.10), channel_id=1, source_target_pairs={{0,48},{16,0},{32,16},{48,32},{1,49},{17,1},{33,17},{49,33},{2,50}... | collective-permute-start | bytes 1179656 | tf_op jit(solution)/shard_map/ppermute | solution.py:293
  13.1 12.8 %collective-permute-start.2 = (bf16[1536,128]{1,0:T(8,128)(2,1)}, bf16[1536,128]{1,0:T(8,128)(2,1)S(1)}, u32[]{:S(2)}, u32[]{:S(2)}) collective-permute-start(bf16[1536,128]{1,0:T(8,128)(2,1)} %bitcast.1.k_ref), channel_id=1, source_target_pairs={{0,16},{16,32},{32,48},{48,0},{1,17},{17,33},{33,49},{49,1},{2,18}... | collective-permute-start | bytes 1179656 | tf_op jit(solution)/shard_map/ppermute | solution.py:293
  15.0 19.2 %collective-permute-start.5 = (bf16[1536,128]{1,0:T(8,128)(2,1)S(1)}, bf16[1536,128]{1,0:T(8,128)(2,1)S(1)}, u32[]{:S(2)}, u32[]{:S(2)}) collective-permute-start(bf16[1536,128]{1,0:T(8,128)(2,1)S(1)} %bitcast.11), channel_id=1, source_target_pairs={{0,16},{16,32},{32,48},{48,0},{1,17},{17,33},{33,49},{49,1},{2,18}... | collective-permute-start | bytes 1179656 | tf_op jit(solution)/shard_map/ppermute | solution.py:293
  17.2 23.2 %collective-permute-start = (bf16[1536,128]{1,0:T(8,128)(2,1)}, bf16[1536,128]{1,0:T(8,128)(2,1)S(1)}, u32[]{:S(2)}, u32[]{:S(2)}) collective-permute-start(bf16[1536,128]{1,0:T(8,128)(2,1)} %bitcast.1.k_ref), channel_id=1, source_target_pairs={{0,48},{16,0},{32,16},{48,32},{1,49},{17,1},{33,17},{49,33},{2,50}... | collective-permute-start | bytes 1179656 | tf_op jit(solution)/shard_map/ppermute | solution.py:293
  21.6 18.8 %collective-permute-start.4 = (bf16[1536,128]{1,0:T(8,128)(2,1)S(1)}, bf16[1536,128]{1,0:T(8,128)(2,1)S(1)}, u32[]{:S(2)}, u32[]{:S(2)}) collective-permute-start(bf16[1536,128]{1,0:T(8,128)(2,1)S(1)} %collective-permute-done.1.refs_3_), channel_id=1, source_target_pairs={{0,48},{16,0},{32,16},{48,32},{1,49},{17,1},{33,17},{49,33},{2,50}... | collective-permute-start | bytes 1179656 | tf_op jit(solution)/shard_map/ppermute | solution.py:293
  25.9 16.8 %collective-permute-start.3 = (bf16[1536,128]{1,0:T(8,128)(2,1)S(1)}, bf16[1536,128]{1,0:T(8,128)(2,1)S(1)}, u32[]{:S(2)}, u32[]{:S(2)}) collective-permute-start(bf16[1536,128]{1,0:T(8,128)(2,1)S(1)} %collective-permute-done.2.k_ref), channel_id=1, source_target_pairs={{0,16},{16,32},{32,48},{48,0},{1,17},{17,33},{33,49},{49,1},{2,18}... | collective-permute-start | bytes 1179656 | tf_op jit(solution)/shard_map/ppermute | solution.py:293
  48.1 15.3 %collective-permute-start.7 = (bf16[32,2176]{1,0:T(8,128)(2,1)S(1)}, bf16[32,2176]{1,0:T(8,128)(2,1)S(1)}, u32[]{:S(2)}, u32[]{:S(2)}) collective-permute-start(bf16[32,2176]{1,0:T(8,128)(2,1)S(1)} %get-tuple-element.22), channel_id=1, source_target_pairs={{0,8},{4,12},{8,0},{12,4},{1,9},{5,13},{9,1},{13,5},{2,10},{6,14},... | collective-permute-start | bytes 417800 | tf_op jit(solution)/shard_map/ppermute | solution.py:296
  50.3 13.1 %collective-permute-start.8 = (bf16[32,2176]{1,0:T(8,128)(2,1)S(1)}, bf16[32,2176]{1,0:T(8,128)(2,1)S(1)}, u32[]{:S(2)}, u32[]{:S(2)}) collective-permute-start(bf16[32,2176]{1,0:T(8,128)(2,1)S(1)} %get-tuple-element.23), channel_id=1, source_target_pairs={{0,12},{4,8},{8,4},{12,0},{1,13},{5,9},{9,5},{13,1},{2,14},{6,10},... | collective-permute-start | bytes 417800 | tf_op jit(solution)/shard_map/ppermute | solution.py:296
  57.8 6.6 %copy-start.2 = (bf16[1,32,1024]{2,1,0:T(8,128)(2,1)S(1)}, bf16[1,32,1024]{2,1,0:T(8,128)(2,1)}, u32[]{:S(2)}) copy-start(bf16[1,32,1024]{2,1,0:T(8,128)(2,1)} %param.10) | copy-start | bytes 196612
  57.8 6.5 %collective-permute-start.6 = (bf16[32,2176]{1,0:T(8,128)(2,1)S(1)}, bf16[32,2176]{1,0:T(8,128)(2,1)S(1)}, u32[]{:S(2)}, u32[]{:S(2)}) collective-permute-start(bf16[32,2176]{1,0:T(8,128)(2,1)S(1)} %attend_last_1.1), channel_id=1, source_target_pairs={{0,4},{4,0},{8,12},{12,8},{1,5},{5,1},{9,13},{13,9},{2,6},{6,2},{1... | collective-permute-start | bytes 417800 | tf_op jit(solution)/shard_map/ppermute | solution.py:296
  65.2 6.7 %copy-start.1 = (bf16[32,1024]{1,0:T(8,128)(2,1)S(1)}, bf16[32,1024]{1,0:T(8,128)(2,1)}, u32[]{:S(2)}) copy-start(bf16[32,1024]{1,0:T(8,128)(2,1)} %fresh_ref.1) | copy-start | bytes 196612
  65.2 6.7 %collective-permute-start.9 = (bf16[32,1024]{1,0:T(8,128)(2,1)S(1)}, bf16[32,1024]{1,0:T(8,128)(2,1)S(1)}, u32[]{:S(2)}, u32[]{:S(2)}) collective-permute-start(bf16[32,1024]{1,0:T(8,128)(2,1)S(1)} %get-tuple-element.24), channel_id=1, source_target_pairs={{0,64},{64,128},{128,192},{192,256},{256,320},{320,384},{384,448},... | collective-permute-start | bytes 196616 | tf_op jit(solution)/shard_map/ppermute | solution.py:339
  72.2 13.2 %copy-start.4 = (bf16[1,1024]{1,0:T(2,128)(2,1)S(1)}, bf16[1,1024]{1,0:T(2,128)(2,1)}, u32[]{:S(2)}) copy-start(bf16[1,1024]{1,0:T(2,128)(2,1)} %gain_ref.1) | copy-start | bytes 6148

commit v4 on v3

--- a/solution.py
+++ b/solution.py
@@ -19,11 +19,12 @@
 N_SEG = 9
 FULL_WIDTH = 4096
 PACKED = 2 * WIDTH_DEV + 128
-TILE = 1536
 BLOCK = 2 * HEADS_DEV * ROWS
 HALF = 2 * BLOCK
 NEGATIVE = -1e30
 FLOOR = -1e28
+EMPTY = (0.0, FLOOR, 0.0)
+OWN_TILE = 512
 TINY = 1e-30
 EPSILON = 1e-05
 LOG2_SCALE = float(np.log2(np.e) / np.sqrt(HD))
@@ -48,34 +49,33 @@
     return start
 
 
-def update(q, k_ref, v_ref, last_offset, out_ref, top_ref, total_ref):
-    def one(t, _):
-        tile = pl.ds(pl.multiple_of(t * TILE, TILE), TILE)
+def update(state, q, k_ref, v_ref, last_offset, length):
+    out, top, total = state
+    for begin in range(0, KEYS, length):
+        tile = slice(begin, begin + length)
         s = lax.dot_general(
             q, k_ref[tile], (((1,), (1,)), ((), ())), preferred_element_type=jnp.float32
         )
         if last_offset is not None:
-            offset = t * TILE + lax.broadcasted_iota(jnp.int32, (1, TILE), 1)
+            offset = begin + lax.broadcasted_iota(jnp.int32, (1, length), 1)
             s = jnp.where(offset <= last_offset, s, NEGATIVE)
         part = s[:, :HD]
-        for u in range(1, TILE // HD):
+        for u in range(1, length // HD):
             part = jnp.maximum(part, s[:, u * HD : (u + 1) * HD])
-        top = top_ref[...]
         tile_top = jnp.max(part, axis=1, keepdims=True) * LOG2_SCALE
         new_top = jnp.maximum(top, jnp.broadcast_to(tile_top, top.shape))
         groups = [
             jnp.exp2(s[:, u * HD : (u + 1) * HD] * LOG2_SCALE - new_top)
-            for u in range(TILE // HD)
+            for u in range(length // HD)
         ]
         lane_sum = functools.reduce(jnp.add, groups)
         p = jnp.concatenate([group.astype(jnp.bfloat16) for group in groups], 1)
         mixed = jnp.dot(p, v_ref[tile], preferred_element_type=jnp.float32)
         rescale = jnp.exp2(top - new_top)
-        out_ref[...] = out_ref[...] * rescale + mixed
-        total_ref[...] = total_ref[...] * rescale + lane_sum
-        top_ref[...] = new_top
-
-    lax.fori_loop(0, KEYS // TILE, one, None)
+        out = out * rescale + mixed
+        total = total * rescale + lane_sum
+        top = new_top
+    return out, top, total
 
 
 def finished(out_ref, top_ref, total_ref):
@@ -105,7 +105,7 @@
         o_ref[:, 2 * WIDTH_DEV :] = pieces.astype(jnp.bfloat16)
 
 
-def attend_rows(first_d, n_d, shift, lengths_ref, q_ref, k_ref, v_ref, state):
+def attend_rows(first_d, n_d, shift, lengths_ref, q_ref, k_ref, v_ref, state, started=True):
     cx = lax.axis_index("cx")
     cy = lax.axis_index("cy")
     base = cx * NY * ROWS - ((cx + shift) % NX * NY + cy) * KEYS
@@ -129,7 +129,14 @@
             owner = (first_d + row_id // BLOCK) ^ cy
             second = row_id // (BLOCK // 2) % 2 == 1
             last_offset = jnp.where(second, least[1], least[0]) + owner * ROWS + row_id % ROWS
-        update(q, k_ref, v_ref, last_offset, *state)
+        if started:
+            held = tuple(ref[...] for ref in state)
+        else:
+            held = tuple(jnp.full((n_d * BLOCK, HD), x, jnp.float32) for x in EMPTY)
+        length = KEYS if started else OWN_TILE
+        result = update(held, q, k_ref, v_ref, last_offset, length)
+        for ref, value in zip(state, result, strict=True):
+            ref[...] = value
 
     @pl.when(full)
     def _():
@@ -139,15 +146,18 @@
     def _():
         run(True)
 
+    if not started:
+
+        @pl.when(none)
+        def _():
+            for ref, value in zip(state, EMPTY, strict=True):
+                ref[...] = jnp.full(ref.shape, value, jnp.float32)
+
 
 def first_kernel(lengths_ref, q_ref, k_ref, v_ref, out_ref, top_ref, total_ref):
-    out_ref[...] = jnp.zeros(out_ref.shape, jnp.float32)
-    top_ref[...] = jnp.full(top_ref.shape, FLOOR, jnp.float32)
-    total_ref[...] = jnp.zeros(total_ref.shape, jnp.float32)
-
     def one(half, _):
         state = [ref.at[half] for ref in (out_ref, top_ref, total_ref)]
-        attend_rows(2 * half, 2, 0, lengths_ref, q_ref, k_ref, v_ref, state)
+        attend_rows(2 * half, 2, 0, lengths_ref, q_ref, k_ref, v_ref, state, started=False)
 
     lax.fori_loop(0, 2, one, None)
 
@@ -164,15 +174,29 @@
     lax.fori_loop(0, 2, one, None)
 
 
-def last_kernel(first_d, n_d, *refs):
+def above_kernel(lengths_ref, q_ref, k_ref, v_ref, *refs):
+    inputs, outs = refs[:3], refs[3:]
+    for source, target in zip(inputs, outs, strict=True):
+        target[...] = source[1]
+    attend_rows(2, 2, 1, lengths_ref, q_ref, k_ref, v_ref, outs)
+
+
+def far_kernel(lengths_ref, q_ref, k_ref, v_ref, *refs):
+    inputs, outs, state = refs[:3], refs[3:5], refs[5:]
+    for source, target in zip(inputs, state, strict=True):
+        target[...] = source[...]
+    attend_rows(2, 2, 2, lengths_ref, q_ref, k_ref, v_ref, state)
+    write_packed(finished(*state), outs)
+
+
+def near_kernel(d, *refs):
     lengths_ref, q_ref, k_above, v_above, k_far, v_far = refs[:6]
-    inputs, outs, state = refs[6:9], refs[9 : 9 + n_d], refs[9 + n_d :]
-    begin = first_d % 2 * BLOCK
+    inputs, o_ref, state = refs[6:9], refs[9], refs[10:]
     for source, target in zip(inputs, state, strict=True):
-        target[...] = source[first_d // 2, begin : begin + n_d * BLOCK]
-    attend_rows(first_d, n_d, 1, lengths_ref, q_ref, k_above, v_above, state)
-    attend_rows(first_d, n_d, 2, lengths_ref, q_ref, k_far, v_far, state)
-    write_packed(finished(*state), outs)
+        target[...] = source[0, d * BLOCK : (d + 1) * BLOCK]
+    attend_rows(d, 1, 1, lengths_ref, q_ref, k_above, v_above, state)
+    attend_rows(d, 1, 2, lengths_ref, q_ref, k_far, v_far, state)
+    write_packed(finished(*state), [o_ref])
 
 
 def in_vmem(x):
@@ -183,37 +207,15 @@
     return pltpu.with_memory_space_constraint(x, pltpu.HBM)
 
 
-def attend_first(lengths, q_all, k, v):
+def attend(kernel, name, out_shape, scratch_rows, lengths, *operands):
     return pl.pallas_call(
-        first_kernel,
-        in_specs=[SMEM] + [VMEM] * 3,
-        out_specs=[VMEM] * 3,
-        out_shape=[pltpu.VMEM((2, HALF, HD), jnp.float32)] * 3,
+        kernel,
+        in_specs=[SMEM] + [VMEM] * len(operands),
+        out_specs=[VMEM] * len(out_shape),
+        out_shape=out_shape,
+        scratch_shapes=[pltpu.VMEM((scratch_rows, HD), jnp.float32)] * 3 if scratch_rows else [],
         compiler_params=LARGE,
-        name="attend_own",
-    )(lengths, in_vmem(q_all), in_vmem(k), in_vmem(v))
-
-
-def attend_second(lengths, *operands):
-    return pl.pallas_call(
-        second_kernel,
-        in_specs=[SMEM] + [VMEM] * len(operands),
-        out_specs=[VMEM] * 3,
-        out_shape=[pltpu.VMEM((2, HALF, HD), jnp.float32)] * 3,
-        compiler_params=LARGE,
-        name="attend_below",
-    )(lengths, *[in_vmem(x) for x in operands])
-
-
-def attend_last(first_d, n_d, lengths, *operands):
-    return pl.pallas_call(
-        functools.partial(last_kernel, first_d, n_d),
-        in_specs=[SMEM] + [VMEM] * len(operands),
-        out_specs=[VMEM] * n_d,
-        out_shape=[pltpu.VMEM((ROWS, PACKED), jnp.bfloat16)] * n_d,
-        scratch_shapes=[pltpu.VMEM((n_d * BLOCK, HD), jnp.float32)] * 3,
-        compiler_params=LARGE,
-        name=f"attend_last_{first_d}",
+        name=name,
     )(lengths, *[in_vmem(x) for x in operands])
 
 
@@ -282,7 +284,10 @@
     row = lax.broadcasted_iota(jnp.int32, (ROWS, ROWS), 0)
     lane = lax.broadcasted_iota(jnp.int32, (ROWS, ROWS), 1)
     for tick, sum_ref in enumerate((sum_one_ref, sum_two_ref)):
-        scale = lax.rsqrt(squares_ref[tick : tick + 1, :] / FULL_WIDTH + EPSILON)
+        squares = functools.reduce(
+            jnp.add, [squares_ref[i, tick : tick + 1, :] for i in range(squares_ref.shape[0])]
+        )
+        scale = lax.rsqrt(squares / FULL_WIDTH + EPSILON)
         column = jnp.sum(jnp.where(row == lane, scale, 0.0), axis=1, keepdims=True)
         residual_ref[tick] = sum_ref[...].astype(jnp.bfloat16)
         normed_ref[tick] = (sum_ref[...] * column * gain).astype(jnp.bfloat16)
@@ -305,16 +310,34 @@
     k_far = along_x(k_below, 1)
     v_far = along_x(v_above, -1)
 
-    state = attend_first(segment_lengths, q_all, k, v)
-    state = attend_second(segment_lengths, q_all, k_below, v_below, *state)
-    operands = (segment_lengths, q_all, k_above, v_above, k_far, v_far, *state)
-    part_two, part_three = attend_last(2, 2, *operands)
+    both = [pltpu.VMEM((2, HALF, HD), jnp.float32)] * 3
+    one = [pltpu.VMEM((HALF, HD), jnp.float32)] * 3
+    packed = pltpu.VMEM((ROWS, PACKED), jnp.bfloat16)
+    common = (segment_lengths, q_all)
+    state = attend(first_kernel, "attend_own", both, 0, *common, k, v)
+    state = attend(second_kernel, "attend_below", both, 0, *common, k_below, v_below, *state)
+    upper = attend(above_kernel, "attend_above", one, 0, *common, k_above, v_above, *state)
+    part_two, part_three = attend(
+        far_kernel, "attend_far", [packed] * 2, HALF, *common, k_far, v_far, *upper
+    )
     part_three = across_y(part_three, 3)
     part_two = across_y(part_two, 2)
-    (part_one,) = attend_last(1, 1, *operands)
-    part_one = across_y(part_one, 1)
-    (part_own,) = attend_last(0, 1, *operands)
-    parts = (part_own, part_one, part_two, part_three)
+    near = [
+        attend(
+            functools.partial(near_kernel, d),
+            f"attend_near_{d}",
+            [packed],
+            BLOCK,
+            *common,
+            k_above,
+            v_above,
+            k_far,
+            v_far,
+            *state,
+        )[0]
+        for d in range(2)
+    ]
+    parts = (near[0], across_y(near[1], 1), part_two, part_three)
 
     rows_bf16 = pltpu.VMEM((ROWS, WIDTH_DEV), jnp.bfloat16)
     rows_f32 = pltpu.VMEM((ROWS, WIDTH_DEV), jnp.float32)
@@ -345,7 +368,7 @@
         compiler_params=SMALL,
         name="add",
     )(*[in_vmem(x) for x in (attended_two, passed, fresh_rows, sum_one)])
-    squares = lax.psum(squares, "tp")
+    squares = lax.all_gather(squares, "tp")
     residual, normed = pl.pallas_call(
         norm_kernel,
         in_specs=[VMEM] * 4,

time: 86.7 us -> 86.8 us (level)
  blocking collectives: 13.2 us -> 15.1 us
  waiting for transfers between devices: 4.21 us -> 2.32 us
    all_gather x0 -> x1, blocking collectives: none -> 15.1 us  [body(): squares = lax.all_gather(squares, 'tp')]
    psum x1 -> x0, blocking collectives: 13.2 us -> none  [body(): squares = lax.psum(squares, 'tp')]
    ppermute x6, waiting for transfers between devices: 2.83 us -> 0.78 us  [along_x(): return lax.ppermute(value, 'cx', [(i, (i + by) % NX) for i in range(NX)])]
    pallas_call x5 -> x6, Pallas kernels: 24.1 us -> 24.6 us  [attend(): pl.pallas_call(kernel, in_specs=[SMEM] + [VMEM] * len(operands), out_spec...]
  transfers between devices with their start and end apart: 11 -> 11, of which waited for: 4 -> 3; matrix products, arithmetic and copies ran while one was open for 0% -> 0% of each run, Pallas kernels for 23% -> 26%
where the time goes in v4:
time: 86.8 us; the launch traced here: 86.2 us
  starting transfers between devices  38.7 us (45%)
  Pallas kernels  27.4 us (32%)
  blocking collectives  15.1 us (17%)
  waiting for transfers between devices  2.32 us (3%)
  local copies, waits for them, and re-layouts  1.79 us (2%)
    pallas_call x6, Pallas kernels, attend(): pl.pallas_call(kernel, in_specs=[SMEM] + [VMEM] * len(operands), out_spec...  24.6 us
    ppermute x6, starting transfers between devices, along_x(): return lax.ppermute(value, 'cx', [(i, (i + by) % NX) for i in range(NX)])  19.1 us
    all_gather x1, blocking collectives, body(): squares = lax.all_gather(squares, 'tp')  15.1 us
    ppermute x3, starting transfers between devices, across_y(): return lax.ppermute(value, 'cy', [(i, i ^ d) for i in range(NY)])  8.51 us
    all_to_all x1, starting transfers between devices, body(): q_all = lax.all_to_all(q_own, 'cy', 0, 0)  6.21 us
    ppermute x1, starting transfers between devices, body(): lax.ppermute(residual_one, 'section', [(i, i + 1) for i in range(count -...  4.84 us
    broadcast_in_dim x1, local copies, waits for them, and re-layouts, body(): q_own = jnp.broadcast_to(queries[:, 0], (NY, 2, ROWS, WIDTH_DEV))  1.77 us
  transfers between devices with their start and end apart: 11, of which 3 were waited for; matrix products, arithmetic and copies ran while one was open for 0% of the time, Pallas kernels for 26%

profile of v4, /device:TPU:249, one launch (start us, length us, event | category | flops | bytes accessed | tf_op | source)
XLA Modules:
  0.0 86.2 jit_solution(7932130134084802034)
XLA Ops:
  0.6 1.8 %broadcast_in_dim.9 = bf16[4,2,32,1024]{3,2,1,0:T(8,128)(2,1)} broadcast(bf16[2,32,1024]{2,1,0:T(8,128)(2,1)} %bitcast.16), dimensions={1,2,3} | broadcast | bytes 655360 | tf_op jit(solution)/shard_map/broadcast_in_dim | solution.py:306
  2.4 0.0 copy-start
  2.4 6.2 %all-to-all-start = ((bf16[4,2,32,1024]{3,2,1,0:T(8,128)(2,1)}), bf16[4,2,32,1024]{3,2,1,0:T(8,128)(2,1)S(1)}, u32[]{:S(2)}, u32[]{:S(2)}) async-start(bf16[4,2,32,1024]{3,2,1,0:T(8,128)(2,1)} %broadcast_in_dim.9), calls=%async_computation | async-start | bytes 1048576 | tf_op jit(solution)/shard_map/all_to_all | solution.py:307
  8.6 0.0 copy-done
  8.6 0.0 copy-start.3
  8.6 4.5 %collective-permute-start.1 = (bf16[1536,128]{1,0:T(8,128)(2,1)S(1)}, bf16[1536,128]{1,0:T(8,128)(2,1)S(1)}, u32[]{:S(2)}, u32[]{:S(2)}) collective-permute-start(bf16[1536,128]{1,0:T(8,128)(2,1)S(1)} %bitcast.11), channel_id=1, source_target_pairs={{0,48},{16,0},{32,16},{48,32},{1,49},{17,1},{33,17},{49,33},{2,50}... | collective-permute-start | bytes 1179656 | tf_op jit(solution)/shard_map/ppermute | solution.py:298
  13.1 1.9 %collective-permute-start.2 = (bf16[1536,128]{1,0:T(8,128)(2,1)}, bf16[1536,128]{1,0:T(8,128)(2,1)S(1)}, u32[]{:S(2)}, u32[]{:S(2)}) collective-permute-start(bf16[1536,128]{1,0:T(8,128)(2,1)} %bitcast.1.k_ref), channel_id=1, source_target_pairs={{0,16},{16,32},{32,48},{48,0},{1,17},{17,33},{33,49},{49,1},{2,18}... | collective-permute-start | bytes 1179656 | tf_op jit(solution)/shard_map/ppermute | solution.py:298
  15.1 2.1 %collective-permute-start.5 = (bf16[1536,128]{1,0:T(8,128)(2,1)S(1)}, bf16[1536,128]{1,0:T(8,128)(2,1)S(1)}, u32[]{:S(2)}, u32[]{:S(2)}) collective-permute-start(bf16[1536,128]{1,0:T(8,128)(2,1)S(1)} %bitcast.12), channel_id=1, source_target_pairs={{0,16},{16,32},{32,48},{48,0},{1,17},{17,33},{33,49},{49,1},{2,18}... | collective-permute-start | bytes 1179656 | tf_op jit(solution)/shard_map/ppermute | solution.py:298
  17.2 4.4 %collective-permute-start = (bf16[1536,128]{1,0:T(8,128)(2,1)}, bf16[1536,128]{1,0:T(8,128)(2,1)S(1)}, u32[]{:S(2)}, u32[]{:S(2)}) collective-permute-start(bf16[1536,128]{1,0:T(8,128)(2,1)} %bitcast.1.k_ref), channel_id=1, source_target_pairs={{0,48},{16,0},{32,16},{48,32},{1,49},{17,1},{33,17},{49,33},{2,50}... | collective-permute-start | bytes 1179656 | tf_op jit(solution)/shard_map/ppermute | solution.py:298
  21.6 0.0 collective-permute-done.1.refs_3_.v_ref
  21.6 4.3 %collective-permute-start.4 = (bf16[1536,128]{1,0:T(8,128)(2,1)S(1)}, bf16[1536,128]{1,0:T(8,128)(2,1)S(1)}, u32[]{:S(2)}, u32[]{:S(2)}) collective-permute-start(bf16[1536,128]{1,0:T(8,128)(2,1)S(1)} %collective-permute-done.1.refs_3_.v_ref), channel_id=1, source_target_pairs={{0,48},{16,0},{32,16},{48,32},{1,49},{17,1},{33,17},{49,33},{2,50}... | collective-permute-start | bytes 1179656 | tf_op jit(solution)/shard_map/ppermute | solution.py:298
  25.9 0.0 collective-permute-done.2.k_ref
  25.9 1.9 %collective-permute-start.3 = (bf16[1536,128]{1,0:T(8,128)(2,1)S(1)}, bf16[1536,128]{1,0:T(8,128)(2,1)S(1)}, u32[]{:S(2)}, u32[]{:S(2)}) collective-permute-start(bf16[1536,128]{1,0:T(8,128)(2,1)S(1)} %collective-permute-done.2.k_ref), channel_id=1, source_target_pairs={{0,16},{16,32},{32,48},{48,0},{1,17},{17,33},{33,49},{49,1},{2,18}... | collective-permute-start | bytes 1179656 | tf_op jit(solution)/shard_map/ppermute | solution.py:298
  27.8 0.0 all-to-all-done.q_ref.refs_1_
  27.8 0.0 copy-done.3
  27.8 5.6 %attend_own.1 = (f32[2,1024,128]{2,1,0:T(8,128)S(1)}, f32[2,1024,128]{2,1,0:T(8,128)S(1)}, f32[2,1024,128]{2,1,0:T(8,128)S(1)}) custom-call(s32[9]{0:T(128)S(1)} %copy-done.3, bf16[4,2,32,1024]{3,2,1,0:T(8,128)(2,1)S(1)} %all-to-all-done.q_ref.refs_1_, bf16[1536,128]{1,0:T(8,128)(2,1)} %bitcast.1.k_ref, bf16[1536,128]{1,0:T(8,128)(2,1)S(1)} %bitcast.13), custom_call_target="tpu_custom_call" | custom-call | tf_op jit(solution)/shard_map/attend_own/pallas_call | solution.py:211
  33.5 0.8 collective-permute-done.5.v_ref
  34.2 6.1 %attend_below.1 = (f32[2,1024,128]{2,1,0:T(8,128)S(1)}, f32[2,1024,128]{2,1,0:T(8,128)S(1)}, f32[2,1024,128]{2,1,0:T(8,128)S(1)}) custom-call(s32[9]{0:T(128)S(1)} %copy-done.3, bf16[4,2,32,1024]{3,2,1,0:T(8,128)(2,1)S(1)} %all-to-all-done.q_ref.refs_1_, bf16[1536,128]{1,0:T(8,128)(2,1)S(1)} %collective-permute-done.2.k_ref, ...), custom_call_target="tpu_custom_call" | custom-call | tf_op jit(solution)/shard_map/attend_below/pallas_call | solution.py:211
  40.3 0.0 collective-permute-done.refs_2_.k_ref
  40.3 3.1 %attend_above.1 = (f32[1024,128]{1,0:T(8,128)S(1)}, f32[1024,128]{1,0:T(8,128)S(1)}, f32[1024,128]{1,0:T(8,128)S(1)}) custom-call(s32[9]{0:T(128)S(1)} %copy-done.3, bf16[4,2,32,1024]{3,2,1,0:T(8,128)(2,1)S(1)} %all-to-all-done.q_ref.refs_1_, bf16[1536,128]{1,0:T(8,128)(2,1)S(1)} %collective-permute-done.refs_2_.k_ref, ...), custom_call_target="tpu_custom_call" | custom-call | tf_op jit(solution)/shard_map/attend_above/pallas_call | solution.py:211
  43.5 0.0 collective-permute-done.4.refs_5_.v_ref
  43.5 0.0 collective-permute-done.3.refs_4_.k_ref
  43.5 3.1 %attend_far.1 = (bf16[32,2176]{1,0:T(8,128)(2,1)S(1)}, bf16[32,2176]{1,0:T(8,128)(2,1)S(1)}) custom-call(s32[9]{0:T(128)S(1)} %copy-done.3, bf16[4,2,32,1024]{3,2,1,0:T(8,128)(2,1)S(1)} %all-to-all-done.q_ref.refs_1_, bf16[1536,128]{1,0:T(8,128)(2,1)S(1)} %collective-permute-done.3.refs_4_.k_ref, bf16[1536,128]{1,0:T(8,128)(2,1)S(1)} %collective-permute-done.4.refs_5_.v_ref, ...), custom_call_target="tpu_custom_call" | custom-call | tf_op jit(solution)/shard_map/attend_far/pallas_call | solution.py:211
  46.5 1.9 %collective-permute-start.7 = (bf16[32,2176]{1,0:T(8,128)(2,1)S(1)}, bf16[32,2176]{1,0:T(8,128)(2,1)S(1)}, u32[]{:S(2)}, u32[]{:S(2)}) collective-permute-start(bf16[32,2176]{1,0:T(8,128)(2,1)S(1)} %get-tuple-element.28), channel_id=1, source_target_pairs={{0,8},{4,12},{8,0},{12,4},{1,9},{5,13},{9,1},{13,5},{2,10},{6,14},... | collective-permute-start | bytes 417800 | tf_op jit(solution)/shard_map/ppermute | solution.py:301
  48.5 4.3 %collective-permute-start.8 = (bf16[32,2176]{1,0:T(8,128)(2,1)S(1)}, bf16[32,2176]{1,0:T(8,128)(2,1)S(1)}, u32[]{:S(2)}, u32[]{:S(2)}) collective-permute-start(bf16[32,2176]{1,0:T(8,128)(2,1)S(1)} %get-tuple-element.29), channel_id=1, source_target_pairs={{0,12},{4,8},{8,4},{12,0},{1,13},{5,9},{9,5},{13,1},{2,14},{6,10},... | collective-permute-start | bytes 417800 | tf_op jit(solution)/shard_map/ppermute | solution.py:301
  52.7 3.5 %attend_near_1.1 = bf16[32,2176]{1,0:T(8,128)(2,1)S(1)} custom-call(s32[9]{0:T(128)S(1)} %copy-done.3, bf16[4,2,32,1024]{3,2,1,0:T(8,128)(2,1)S(1)} %all-to-all-done.q_ref.refs_1_, bf16[1536,128]{1,0:T(8,128)(2,1)S(1)} %collective-permute-done.refs_2_.k_ref, bf16[1536,128]{1,0:T(8,128)(2,1)S(1)} %collective-permute-done.1.refs_3_.v_ref, ...), custom_call_target="tpu_custom_call" | custom-call | tf_op jit(solution)/shard_map/attend_near_1/pallas_call | solution.py:211
  56.2 0.0 copy-start.2
  56.2 2.3 %collective-permute-start.6 = (bf16[32,2176]{1,0:T(8,128)(2,1)S(1)}, bf16[32,2176]{1,0:T(8,128)(2,1)S(1)}, u32[]{:S(2)}, u32[]{:S(2)}) collective-permute-start(bf16[32,2176]{1,0:T(8,128)(2,1)S(1)} %attend_near_1.1), channel_id=1, source_target_pairs={{0,4},{4,0},{8,12},{12,8},{1,5},{5,1},{9,13},{13,9},{2,6},{6,2},{1... | collective-permute-start | bytes 417800 | tf_op jit(solution)/shard_map/ppermute | solution.py:301
  58.6 3.2 %attend_near_0.1.refs_0_ = bf16[32,2176]{1,0:T(8,128)(2,1)S(1)} custom-call(s32[9]{0:T(128)S(1)} %copy-done.3, bf16[4,2,32,1024]{3,2,1,0:T(8,128)(2,1)S(1)} %all-to-all-done.q_ref.refs_1_, bf16[1536,128]{1,0:T(8,128)(2,1)S(1)} %collective-permute-done.refs_2_.k_ref, bf16[1536,128]{1,0:T(8,128)(2,1)S(1)} %collective-permute-done.1.refs_3_.v_ref, ...), custom_call_target="tpu_custom_call" | custom-call | tf_op jit(solution)/shard_map/attend_near_0/pallas_call | solution.py:211
  61.8 0.0 collective-permute-done.7.refs_2_
  61.8 0.0 collective-permute-done.8.refs_3_
  61.8 1.1 %collective-permute-done.6.refs_1_ = bf16[32,2176]{1,0:T(8,128)(2,1)S(1)} collective-permute-done((bf16[32,2176]{1,0:T(8,128)(2,1)S(1)}, bf16[32,2176]{1,0:T(8,128)(2,1)S(1)}, u32[]{:S(2)}, u32[]{:S(2)}) %collective-permute-start.6) | collective-permute-done | bytes 139296 | tf_op jit(solution)/shard_map/ppermute | solution.py:301
  62.9 0.0 copy-done.2
  62.9 0.9 %merge_one.1 = (bf16[32,1024]{1,0:T(8,128)(2,1)S(1)}, f32[32,1024]{1,0:T(8,128)S(1)}) custom-call(s32[9]{0:T(128)S(1)} %copy-done.3, bf16[32,1024]{1,0:T(8,128)(2,1)S(1)} %bitcast.14, bf16[32,2176]{1,0:T(8,128)(2,1)S(1)} %attend_near_0.1.refs_0_, bf16[32,2176]{1,0:T(8,128)(2,1)S(1)} %collective-permute-done.6.refs_1_, ...), custom_call_target="tpu_custom_call" | custom-call | tf_op jit(solution)/shard_map/merge_one/pallas_call | solution.py:345
  63.8 0.0 copy-start.1
  63.8 4.8 %collective-permute-start.9 = (bf16[32,1024]{1,0:T(8,128)(2,1)S(1)}, bf16[32,1024]{1,0:T(8,128)(2,1)S(1)}, u32[]{:S(2)}, u32[]{:S(2)}) collective-permute-start(bf16[32,1024]{1,0:T(8,128)(2,1)S(1)} %get-tuple-element.30), channel_id=1, source_target_pairs={{0,64},{64,128},{128,192},{192,256},{256,320},{320,384},{384,448},... | collective-permute-start | bytes 196616 | tf_op jit(solution)/shard_map/ppermute | solution.py:362
  68.7 0.9 %merge_two.1.attended_ref = f32[32,1024]{1,0:T(8,128)S(1)} custom-call(s32[9]{0:T(128)S(1)} %copy-done.3, bf16[32,2176]{1,0:T(8,128)(2,1)S(1)} %attend_near_0.1.refs_0_, bf16[32,2176]{1,0:T(8,128)(2,1)S(1)} %collective-permute-done.6.refs_1_, bf16[32,2176]{1,0:T(8,128)(2,1)S(1)} %collective-permute-done.7.refs_2_, ...), custom_call_target="tpu_custom_call" | custom-call | tf_op jit(solution)/shard_map/merge_two/pallas_call | solution.py:353
  69.5 0.4 collective-permute-done.9.passed_ref
  70.0 0.0 copy-done.1
  70.0 0.3 add.1
  70.3 0.0 copy-start.4
  70.3 15.1 %all-gather.1.squares_ref = f32[4,2,32]{2,1,0:T(2,128)S(1)} all-gather(f32[1,2,32]{2,1,0:T(2,128)S(1)} %bitcast.15), channel_id=2, replica_groups=mesh['section'=8,'cx'=4,'cy'=4,'tp'=4] {'tp'}, dimensions={0}, use_global_device_ids=true | all-gather | bytes 1280 | tf_op jit(solution)/shard_map/all_gather | solution.py:371
  85.4 0.0 copy-done.4
  85.4 0.8 norm.1
Async XLA Ops:
  2.4 6.2 %copy-start = (bf16[1,1536,128]{2,1,0:T(8,128)(2,1)S(1)}, bf16[1,1536,128]{2,1,0:T(8,128)(2,1)}, u32[]{:S(2)}) copy-start(bf16[1,1536,128]{2,1,0:T(8,128)(2,1)} %param.9) | copy-start | bytes 1179652
  2.4 25.4 %all-to-all-start = ((bf16[4,2,32,1024]{3,2,1,0:T(8,128)(2,1)}), bf16[4,2,32,1024]{3,2,1,0:T(8,128)(2,1)S(1)}, u32[]{:S(2)}, u32[]{:S(2)}) async-start(bf16[4,2,32,1024]{3,2,1,0:T(8,128)(2,1)} %broadcast_in_dim.9), calls=%async_computation | async-start | bytes 1048576 | tf_op jit(solution)/shard_map/all_to_all | solution.py:307
  8.6 19.2 %copy-start.3 = (s32[9]{0:T(128)S(1)}, s32[9]{0:T(128)}, u32[]{:S(2)}) copy-start(s32[9]{0:T(128)} %lengths_ref.11) | copy-start | bytes 112
  8.6 13.0 %collective-permute-start.1 = (bf16[1536,128]{1,0:T(8,128)(2,1)S(1)}, bf16[1536,128]{1,0:T(8,128)(2,1)S(1)}, u32[]{:S(2)}, u32[]{:S(2)}) collective-permute-start(bf16[1536,128]{1,0:T(8,128)(2,1)S(1)} %bitcast.11), channel_id=1, source_target_pairs={{0,48},{16,0},{32,16},{48,32},{1,49},{17,1},{33,17},{49,33},{2,50}... | collective-permute-start | bytes 1179656 | tf_op jit(solution)/shard_map/ppermute | solution.py:298
  13.1 12.8 %collective-permute-start.2 = (bf16[1536,128]{1,0:T(8,128)(2,1)}, bf16[1536,128]{1,0:T(8,128)(2,1)S(1)}, u32[]{:S(2)}, u32[]{:S(2)}) collective-permute-start(bf16[1536,128]{1,0:T(8,128)(2,1)} %bitcast.1.k_ref), channel_id=1, source_target_pairs={{0,16},{16,32},{32,48},{48,0},{1,17},{17,33},{33,49},{49,1},{2,18}... | collective-permute-start | bytes 1179656 | tf_op jit(solution)/shard_map/ppermute | solution.py:298
  15.1 19.2 %collective-permute-start.5 = (bf16[1536,128]{1,0:T(8,128)(2,1)S(1)}, bf16[1536,128]{1,0:T(8,128)(2,1)S(1)}, u32[]{:S(2)}, u32[]{:S(2)}) collective-permute-start(bf16[1536,128]{1,0:T(8,128)(2,1)S(1)} %bitcast.12), channel_id=1, source_target_pairs={{0,16},{16,32},{32,48},{48,0},{1,17},{17,33},{33,49},{49,1},{2,18}... | collective-permute-start | bytes 1179656 | tf_op jit(solution)/shard_map/ppermute | solution.py:298
  17.2 23.2 %collective-permute-start = (bf16[1536,128]{1,0:T(8,128)(2,1)}, bf16[1536,128]{1,0:T(8,128)(2,1)S(1)}, u32[]{:S(2)}, u32[]{:S(2)}) collective-permute-start(bf16[1536,128]{1,0:T(8,128)(2,1)} %bitcast.1.k_ref), channel_id=1, source_target_pairs={{0,48},{16,0},{32,16},{48,32},{1,49},{17,1},{33,17},{49,33},{2,50}... | collective-permute-start | bytes 1179656 | tf_op jit(solution)/shard_map/ppermute | solution.py:298
  21.6 21.9 %collective-permute-start.4 = (bf16[1536,128]{1,0:T(8,128)(2,1)S(1)}, bf16[1536,128]{1,0:T(8,128)(2,1)S(1)}, u32[]{:S(2)}, u32[]{:S(2)}) collective-permute-start(bf16[1536,128]{1,0:T(8,128)(2,1)S(1)} %collective-permute-done.1.refs_3_.v_ref), channel_id=1, source_target_pairs={{0,48},{16,0},{32,16},{48,32},{1,49},{17,1},{33,17},{49,33},{2,50}... | collective-permute-start | bytes 1179656 | tf_op jit(solution)/shard_map/ppermute | solution.py:298
  25.9 17.6 %collective-permute-start.3 = (bf16[1536,128]{1,0:T(8,128)(2,1)S(1)}, bf16[1536,128]{1,0:T(8,128)(2,1)S(1)}, u32[]{:S(2)}, u32[]{:S(2)}) collective-permute-start(bf16[1536,128]{1,0:T(8,128)(2,1)S(1)} %collective-permute-done.2.k_ref), channel_id=1, source_target_pairs={{0,16},{16,32},{32,48},{48,0},{1,17},{17,33},{33,49},{49,1},{2,18}... | collective-permute-start | bytes 1179656 | tf_op jit(solution)/shard_map/ppermute | solution.py:298
  46.5 15.3 %collective-permute-start.7 = (bf16[32,2176]{1,0:T(8,128)(2,1)S(1)}, bf16[32,2176]{1,0:T(8,128)(2,1)S(1)}, u32[]{:S(2)}, u32[]{:S(2)}) collective-permute-start(bf16[32,2176]{1,0:T(8,128)(2,1)S(1)} %get-tuple-element.28), channel_id=1, source_target_pairs={{0,8},{4,12},{8,0},{12,4},{1,9},{5,13},{9,1},{13,5},{2,10},{6,14},... | collective-permute-start | bytes 417800 | tf_op jit(solution)/shard_map/ppermute | solution.py:301
  48.5 13.3 %collective-permute-start.8 = (bf16[32,2176]{1,0:T(8,128)(2,1)S(1)}, bf16[32,2176]{1,0:T(8,128)(2,1)S(1)}, u32[]{:S(2)}, u32[]{:S(2)}) collective-permute-start(bf16[32,2176]{1,0:T(8,128)(2,1)S(1)} %get-tuple-element.29), channel_id=1, source_target_pairs={{0,12},{4,8},{8,4},{12,0},{1,13},{5,9},{9,5},{13,1},{2,14},{6,10},... | collective-permute-start | bytes 417800 | tf_op jit(solution)/shard_map/ppermute | solution.py:301
  56.2 6.7 %copy-start.2 = (bf16[1,32,1024]{2,1,0:T(8,128)(2,1)S(1)}, bf16[1,32,1024]{2,1,0:T(8,128)(2,1)}, u32[]{:S(2)}) copy-start(bf16[1,32,1024]{2,1,0:T(8,128)(2,1)} %param.10) | copy-start | bytes 196612
  56.2 6.7 %collective-permute-start.6 = (bf16[32,2176]{1,0:T(8,128)(2,1)S(1)}, bf16[32,2176]{1,0:T(8,128)(2,1)S(1)}, u32[]{:S(2)}, u32[]{:S(2)}) collective-permute-start(bf16[32,2176]{1,0:T(8,128)(2,1)S(1)} %attend_near_1.1), channel_id=1, source_target_pairs={{0,4},{4,0},{8,12},{12,8},{1,5},{5,1},{9,13},{13,9},{2,6},{6,2},{1... | collective-permute-start | bytes 417800 | tf_op jit(solution)/shard_map/ppermute | solution.py:301
  63.8 6.2 %copy-start.1 = (bf16[32,1024]{1,0:T(8,128)(2,1)S(1)}, bf16[32,1024]{1,0:T(8,128)(2,1)}, u32[]{:S(2)}) copy-start(bf16[32,1024]{1,0:T(8,128)(2,1)} %fresh_ref.1) | copy-start | bytes 196612
  63.8 6.2 %collective-permute-start.9 = (bf16[32,1024]{1,0:T(8,128)(2,1)S(1)}, bf16[32,1024]{1,0:T(8,128)(2,1)S(1)}, u32[]{:S(2)}, u32[]{:S(2)}) collective-permute-start(bf16[32,1024]{1,0:T(8,128)(2,1)S(1)} %get-tuple-element.30), channel_id=1, source_target_pairs={{0,64},{64,128},{128,192},{192,256},{256,320},{320,384},{384,448},... | collective-permute-start | bytes 196616 | tf_op jit(solution)/shard_map/ppermute | solution.py:362
  70.3 15.1 %copy-start.4 = (bf16[1,1024]{1,0:T(2,128)(2,1)S(1)}, bf16[1,1024]{1,0:T(2,128)(2,1)}, u32[]{:S(2)}) copy-start(bf16[1,1024]{1,0:T(2,128)(2,1)} %gain_ref.1) | copy-start | bytes 6148

commit v5 on v4

--- a/solution.py
+++ b/solution.py
@@ -305,7 +305,8 @@
     v_above = along_x(v, -1)
     q_own = jnp.broadcast_to(queries[:, 0], (NY, 2, ROWS, WIDTH_DEV))
     q_all = lax.all_to_all(q_own, "cy", 0, 0)
-    v_below = along_x(v, 1)
+    v_next, k_below = lax.optimization_barrier((v, k_below))
+    v_below = along_x(v_next, 1)
     k_above = along_x(k, -1)
     k_far = along_x(k_below, 1)
     v_far = along_x(v_above, -1)

time: 86.8 us -> 86.1 us (level)
  starting transfers between devices: 38.7 us -> 39.7 us
  blocking collectives: 15.1 us -> 14.2 us
    all_gather x1, blocking collectives: 15.1 us -> 14.2 us  [body(): squares = lax.all_gather(squares, 'tp')]
  transfers between devices with their start and end apart: 11 -> 11, of which waited for: 3 -> 2; matrix products, arithmetic and copies ran while one was open for 0% -> 2% of each run, Pallas kernels for 26% -> 26%
where the time goes in v5:
time: 86.1 us; the launch traced here: 85.5 us
  starting transfers between devices  39.7 us (46%)
  Pallas kernels  27.4 us (32%)
  blocking collectives  14.2 us (16%)
  local copies, waits for them, and re-layouts  1.79 us (2%)
  waiting for transfers between devices  1.56 us (2%)
    pallas_call x6, Pallas kernels, attend(): pl.pallas_call(kernel, in_specs=[SMEM] + [VMEM] * len(operands), out_spec...  24.6 us
    ppermute x6, starting transfers between devices, along_x(): return lax.ppermute(value, 'cx', [(i, (i + by) % NX) for i in range(NX)])  19.6 us
    all_gather x1, blocking collectives, body(): squares = lax.all_gather(squares, 'tp')  14.2 us
    ppermute x3, starting transfers between devices, across_y(): return lax.ppermute(value, 'cy', [(i, i ^ d) for i in range(NY)])  8.51 us
    all_to_all x1, starting transfers between devices, body(): q_all = lax.all_to_all(q_own, 'cy', 0, 0)  6.21 us
    ppermute x1, starting transfers between devices, body(): lax.ppermute(residual_one, 'section', [(i, i + 1) for i in range(count -...  5.35 us
    broadcast_in_dim x1, local copies, waits for them, and re-layouts, body(): q_own = jnp.broadcast_to(queries[:, 0], (NY, 2, ROWS, WIDTH_DEV))  1.77 us
  transfers between devices with their start and end apart: 11, of which 2 were waited for; matrix products, arithmetic and copies ran while one was open for 2% of the time, Pallas kernels for 26%

profile of v5, /device:TPU:249, one launch (start us, length us, event | category | flops | bytes accessed | tf_op | source)
XLA Modules:
  0.0 85.5 jit_solution(3247551126590170531)
XLA Ops:
  0.6 3.1 %collective-permute-start.2 = (bf16[1536,128]{1,0:T(8,128)(2,1)}, bf16[1536,128]{1,0:T(8,128)(2,1)S(1)}, u32[]{:S(2)}, u32[]{:S(2)}) collective-permute-start(bf16[1536,128]{1,0:T(8,128)(2,1)} %bitcast.1.k_ref), channel_id=1, source_target_pairs={{0,16},{16,32},{32,48},{48,0},{1,17},{17,33},{33,49},{49,1},{2,18}... | collective-permute-start | bytes 1179656 | tf_op jit(solution)/shard_map/ppermute | solution.py:298
  3.8 1.8 %broadcast_in_dim.9 = bf16[4,2,32,1024]{3,2,1,0:T(8,128)(2,1)} broadcast(bf16[2,32,1024]{2,1,0:T(8,128)(2,1)} %bitcast.16), dimensions={1,2,3} | broadcast | bytes 655360 | tf_op jit(solution)/shard_map/broadcast_in_dim | solution.py:306
  5.5 0.0 copy-start
  5.5 6.2 %all-to-all-start = ((bf16[4,2,32,1024]{3,2,1,0:T(8,128)(2,1)}), bf16[4,2,32,1024]{3,2,1,0:T(8,128)(2,1)S(1)}, u32[]{:S(2)}, u32[]{:S(2)}) async-start(bf16[4,2,32,1024]{3,2,1,0:T(8,128)(2,1)} %broadcast_in_dim.9), calls=%async_computation | async-start | bytes 1048576 | tf_op jit(solution)/shard_map/all_to_all | solution.py:307
  11.7 0.0 copy-start.3
  11.7 0.0 copy-done
  11.7 3.5 %collective-permute-start.1 = (bf16[1536,128]{1,0:T(8,128)(2,1)S(1)}, bf16[1536,128]{1,0:T(8,128)(2,1)S(1)}, u32[]{:S(2)}, u32[]{:S(2)}) collective-permute-start(bf16[1536,128]{1,0:T(8,128)(2,1)S(1)} %bitcast.11), channel_id=1, source_target_pairs={{0,48},{16,0},{32,16},{48,32},{1,49},{17,1},{33,17},{49,33},{2,50}... | collective-permute-start | bytes 1179656 | tf_op jit(solution)/shard_map/ppermute | solution.py:298
  15.2 0.0 collective-permute-done.2.k_ref
  15.3 1.9 %collective-permute-start.5 = (bf16[1536,128]{1,0:T(8,128)(2,1)S(1)}, bf16[1536,128]{1,0:T(8,128)(2,1)S(1)}, u32[]{:S(2)}, u32[]{:S(2)}) collective-permute-start(bf16[1536,128]{1,0:T(8,128)(2,1)S(1)} %bitcast.12), channel_id=1, source_target_pairs={{0,16},{16,32},{32,48},{48,0},{1,17},{17,33},{33,49},{49,1},{2,18}... | collective-permute-start | bytes 1179656 | tf_op jit(solution)/shard_map/ppermute | solution.py:298
  17.2 4.6 %collective-permute-start = (bf16[1536,128]{1,0:T(8,128)(2,1)}, bf16[1536,128]{1,0:T(8,128)(2,1)S(1)}, u32[]{:S(2)}, u32[]{:S(2)}) collective-permute-start(bf16[1536,128]{1,0:T(8,128)(2,1)} %bitcast.1.k_ref), channel_id=1, source_target_pairs={{0,48},{16,0},{32,16},{48,32},{1,49},{17,1},{33,17},{49,33},{2,50}... | collective-permute-start | bytes 1179656 | tf_op jit(solution)/shard_map/ppermute | solution.py:298
  21.8 1.9 %collective-permute-start.3 = (bf16[1536,128]{1,0:T(8,128)(2,1)S(1)}, bf16[1536,128]{1,0:T(8,128)(2,1)S(1)}, u32[]{:S(2)}, u32[]{:S(2)}) collective-permute-start(bf16[1536,128]{1,0:T(8,128)(2,1)S(1)} %collective-permute-done.2.k_ref), channel_id=1, source_target_pairs={{0,16},{16,32},{32,48},{48,0},{1,17},{17,33},{33,49},{49,1},{2,18}... | collective-permute-start | bytes 1179656 | tf_op jit(solution)/shard_map/ppermute | solution.py:298
  23.7 0.0 collective-permute-done.1.refs_3_.v_ref
  23.7 4.6 %collective-permute-start.4 = (bf16[1536,128]{1,0:T(8,128)(2,1)S(1)}, bf16[1536,128]{1,0:T(8,128)(2,1)S(1)}, u32[]{:S(2)}, u32[]{:S(2)}) collective-permute-start(bf16[1536,128]{1,0:T(8,128)(2,1)S(1)} %collective-permute-done.1.refs_3_.v_ref), channel_id=1, source_target_pairs={{0,48},{16,0},{32,16},{48,32},{1,49},{17,1},{33,17},{49,33},{2,50}... | collective-permute-start | bytes 1179656 | tf_op jit(solution)/shard_map/ppermute | solution.py:298
  28.3 0.0 all-to-all-done.q_ref.refs_1_
  28.3 0.0 copy-done.3
  28.3 5.6 %attend_own.1 = (f32[2,1024,128]{2,1,0:T(8,128)S(1)}, f32[2,1024,128]{2,1,0:T(8,128)S(1)}, f32[2,1024,128]{2,1,0:T(8,128)S(1)}) custom-call(s32[9]{0:T(128)S(1)} %copy-done.3, bf16[4,2,32,1024]{3,2,1,0:T(8,128)(2,1)S(1)} %all-to-all-done.q_ref.refs_1_, bf16[1536,128]{1,0:T(8,128)(2,1)} %bitcast.1.k_ref, bf16[1536,128]{1,0:T(8,128)(2,1)S(1)} %bitcast.13), custom_call_target="tpu_custom_call" | custom-call | tf_op jit(solution)/shard_map/attend_own/pallas_call | solution.py:211
  33.9 0.0 collective-permute-done.5.v_ref
  33.9 6.1 %attend_below.1 = (f32[2,1024,128]{2,1,0:T(8,128)S(1)}, f32[2,1024,128]{2,1,0:T(8,128)S(1)}, f32[2,1024,128]{2,1,0:T(8,128)S(1)}) custom-call(s32[9]{0:T(128)S(1)} %copy-done.3, bf16[4,2,32,1024]{3,2,1,0:T(8,128)(2,1)S(1)} %all-to-all-done.q_ref.refs_1_, bf16[1536,128]{1,0:T(8,128)(2,1)S(1)} %collective-permute-done.2.k_ref, ...), custom_call_target="tpu_custom_call" | custom-call | tf_op jit(solution)/shard_map/attend_below/pallas_call | solution.py:211
  40.0 0.0 collective-permute-done.refs_2_.k_ref
  40.0 3.1 %attend_above.1 = (f32[1024,128]{1,0:T(8,128)S(1)}, f32[1024,128]{1,0:T(8,128)S(1)}, f32[1024,128]{1,0:T(8,128)S(1)}) custom-call(s32[9]{0:T(128)S(1)} %copy-done.3, bf16[4,2,32,1024]{3,2,1,0:T(8,128)(2,1)S(1)} %all-to-all-done.q_ref.refs_1_, bf16[1536,128]{1,0:T(8,128)(2,1)S(1)} %collective-permute-done.refs_2_.k_ref, ...), custom_call_target="tpu_custom_call" | custom-call | tf_op jit(solution)/shard_map/attend_above/pallas_call | solution.py:211
  43.2 0.0 collective-permute-done.3.refs_4_.k_ref
  43.2 0.0 collective-permute-done.4.refs_5_.v_ref
  43.2 3.1 %attend_far.1 = (bf16[32,2176]{1,0:T(8,128)(2,1)S(1)}, bf16[32,2176]{1,0:T(8,128)(2,1)S(1)}) custom-call(s32[9]{0:T(128)S(1)} %copy-done.3, bf16[4,2,32,1024]{3,2,1,0:T(8,128)(2,1)S(1)} %all-to-all-done.q_ref.refs_1_, bf16[1536,128]{1,0:T(8,128)(2,1)S(1)} %collective-permute-done.3.refs_4_.k_ref, bf16[1536,128]{1,0:T(8,128)(2,1)S(1)} %collective-permute-done.4.refs_5_.v_ref, ...), custom_call_target="tpu_custom_call" | custom-call | tf_op jit(solution)/shard_map/attend_far/pallas_call | solution.py:211
  46.2 1.9 %collective-permute-start.7 = (bf16[32,2176]{1,0:T(8,128)(2,1)S(1)}, bf16[32,2176]{1,0:T(8,128)(2,1)S(1)}, u32[]{:S(2)}, u32[]{:S(2)}) collective-permute-start(bf16[32,2176]{1,0:T(8,128)(2,1)S(1)} %get-tuple-element.32), channel_id=1, source_target_pairs={{0,8},{4,12},{8,0},{12,4},{1,9},{5,13},{9,1},{13,5},{2,10},{6,14},... | collective-permute-start | bytes 417800 | tf_op jit(solution)/shard_map/ppermute | solution.py:301
  48.2 4.3 %collective-permute-start.8 = (bf16[32,2176]{1,0:T(8,128)(2,1)S(1)}, bf16[32,2176]{1,0:T(8,128)(2,1)S(1)}, u32[]{:S(2)}, u32[]{:S(2)}) collective-permute-start(bf16[32,2176]{1,0:T(8,128)(2,1)S(1)} %get-tuple-element.33), channel_id=1, source_target_pairs={{0,12},{4,8},{8,4},{12,0},{1,13},{5,9},{9,5},{13,1},{2,14},{6,10},... | collective-permute-start | bytes 417800 | tf_op jit(solution)/shard_map/ppermute | solution.py:301
  52.4 3.5 %attend_near_1.1 = bf16[32,2176]{1,0:T(8,128)(2,1)S(1)} custom-call(s32[9]{0:T(128)S(1)} %copy-done.3, bf16[4,2,32,1024]{3,2,1,0:T(8,128)(2,1)S(1)} %all-to-all-done.q_ref.refs_1_, bf16[1536,128]{1,0:T(8,128)(2,1)S(1)} %collective-permute-done.refs_2_.k_ref, bf16[1536,128]{1,0:T(8,128)(2,1)S(1)} %collective-permute-done.1.refs_3_.v_ref, ...), custom_call_target="tpu_custom_call" | custom-call | tf_op jit(solution)/shard_map/attend_near_1/pallas_call | solution.py:211
  55.9 0.0 copy-start.2
  55.9 2.3 %collective-permute-start.6 = (bf16[32,2176]{1,0:T(8,128)(2,1)S(1)}, bf16[32,2176]{1,0:T(8,128)(2,1)S(1)}, u32[]{:S(2)}, u32[]{:S(2)}) collective-permute-start(bf16[32,2176]{1,0:T(8,128)(2,1)S(1)} %attend_near_1.1), channel_id=1, source_target_pairs={{0,4},{4,0},{8,12},{12,8},{1,5},{5,1},{9,13},{13,9},{2,6},{6,2},{1... | collective-permute-start | bytes 417800 | tf_op jit(solution)/shard_map/ppermute | solution.py:301
  58.3 3.2 %attend_near_0.1.refs_0_ = bf16[32,2176]{1,0:T(8,128)(2,1)S(1)} custom-call(s32[9]{0:T(128)S(1)} %copy-done.3, bf16[4,2,32,1024]{3,2,1,0:T(8,128)(2,1)S(1)} %all-to-all-done.q_ref.refs_1_, bf16[1536,128]{1,0:T(8,128)(2,1)S(1)} %collective-permute-done.refs_2_.k_ref, bf16[1536,128]{1,0:T(8,128)(2,1)S(1)} %collective-permute-done.1.refs_3_.v_ref, ...), custom_call_target="tpu_custom_call" | custom-call | tf_op jit(solution)/shard_map/attend_near_0/pallas_call | solution.py:211
  61.5 0.0 collective-permute-done.7.refs_2_
  61.5 0.0 collective-permute-done.8.refs_3_
  61.5 1.1 %collective-permute-done.6.refs_1_ = bf16[32,2176]{1,0:T(8,128)(2,1)S(1)} collective-permute-done((bf16[32,2176]{1,0:T(8,128)(2,1)S(1)}, bf16[32,2176]{1,0:T(8,128)(2,1)S(1)}, u32[]{:S(2)}, u32[]{:S(2)}) %collective-permute-start.6) | collective-permute-done | bytes 139296 | tf_op jit(solution)/shard_map/ppermute | solution.py:301
  62.6 0.0 copy-done.2
  62.6 0.9 %merge_one.1 = (bf16[32,1024]{1,0:T(8,128)(2,1)S(1)}, f32[32,1024]{1,0:T(8,128)S(1)}) custom-call(s32[9]{0:T(128)S(1)} %copy-done.3, bf16[32,1024]{1,0:T(8,128)(2,1)S(1)} %bitcast.14, bf16[32,2176]{1,0:T(8,128)(2,1)S(1)} %attend_near_0.1.refs_0_, bf16[32,2176]{1,0:T(8,128)(2,1)S(1)} %collective-permute-done.6.refs_1_, ...), custom_call_target="tpu_custom_call" | custom-call | tf_op jit(solution)/shard_map/merge_one/pallas_call | solution.py:346
  63.5 0.0 copy-start.1
  63.5 5.3 %collective-permute-start.9 = (bf16[32,1024]{1,0:T(8,128)(2,1)S(1)}, bf16[32,1024]{1,0:T(8,128)(2,1)S(1)}, u32[]{:S(2)}, u32[]{:S(2)}) collective-permute-start(bf16[32,1024]{1,0:T(8,128)(2,1)S(1)} %get-tuple-element.34), channel_id=1, source_target_pairs={{0,64},{64,128},{128,192},{192,256},{256,320},{320,384},{384,448},... | collective-permute-start | bytes 196616 | tf_op jit(solution)/shard_map/ppermute | solution.py:363
  68.9 0.9 %merge_two.1.attended_ref = f32[32,1024]{1,0:T(8,128)S(1)} custom-call(s32[9]{0:T(128)S(1)} %copy-done.3, bf16[32,2176]{1,0:T(8,128)(2,1)S(1)} %attend_near_0.1.refs_0_, bf16[32,2176]{1,0:T(8,128)(2,1)S(1)} %collective-permute-done.6.refs_1_, bf16[32,2176]{1,0:T(8,128)(2,1)S(1)} %collective-permute-done.7.refs_2_, ...), custom_call_target="tpu_custom_call" | custom-call | tf_op jit(solution)/shard_map/merge_two/pallas_call | solution.py:354
  69.7 0.4 collective-permute-done.9.passed_ref
  70.2 0.0 copy-done.1
  70.2 0.3 add.1
  70.5 0.0 copy-start.4
  70.5 14.2 %all-gather.1.squares_ref = f32[4,2,32]{2,1,0:T(2,128)S(1)} all-gather(f32[1,2,32]{2,1,0:T(2,128)S(1)} %bitcast.15), channel_id=2, replica_groups=mesh['section'=8,'cx'=4,'cy'=4,'tp'=4] {'tp'}, dimensions={0}, use_global_device_ids=true | all-gather | bytes 1280 | tf_op jit(solution)/shard_map/all_gather | solution.py:372
  84.7 0.0 copy-done.4
  84.7 0.8 norm.1
Async XLA Ops:
  0.6 14.6 %collective-permute-start.2 = (bf16[1536,128]{1,0:T(8,128)(2,1)}, bf16[1536,128]{1,0:T(8,128)(2,1)S(1)}, u32[]{:S(2)}, u32[]{:S(2)}) collective-permute-start(bf16[1536,128]{1,0:T(8,128)(2,1)} %bitcast.1.k_ref), channel_id=1, source_target_pairs={{0,16},{16,32},{32,48},{48,0},{1,17},{17,33},{33,49},{49,1},{2,18}... | collective-permute-start | bytes 1179656 | tf_op jit(solution)/shard_map/ppermute | solution.py:298
  5.5 6.2 %copy-start = (bf16[1,1536,128]{2,1,0:T(8,128)(2,1)S(1)}, bf16[1,1536,128]{2,1,0:T(8,128)(2,1)}, u32[]{:S(2)}) copy-start(bf16[1,1536,128]{2,1,0:T(8,128)(2,1)} %param.9) | copy-start | bytes 1179652
  5.5 22.8 %all-to-all-start = ((bf16[4,2,32,1024]{3,2,1,0:T(8,128)(2,1)}), bf16[4,2,32,1024]{3,2,1,0:T(8,128)(2,1)S(1)}, u32[]{:S(2)}, u32[]{:S(2)}) async-start(bf16[4,2,32,1024]{3,2,1,0:T(8,128)(2,1)} %broadcast_in_dim.9), calls=%async_computation | async-start | bytes 1048576 | tf_op jit(solution)/shard_map/all_to_all | solution.py:307
  11.7 16.6 %copy-start.3 = (s32[9]{0:T(128)S(1)}, s32[9]{0:T(128)}, u32[]{:S(2)}) copy-start(s32[9]{0:T(128)} %lengths_ref.11) | copy-start | bytes 112
  11.7 12.0 %collective-permute-start.1 = (bf16[1536,128]{1,0:T(8,128)(2,1)S(1)}, bf16[1536,128]{1,0:T(8,128)(2,1)S(1)}, u32[]{:S(2)}, u32[]{:S(2)}) collective-permute-start(bf16[1536,128]{1,0:T(8,128)(2,1)S(1)} %bitcast.11), channel_id=1, source_target_pairs={{0,48},{16,0},{32,16},{48,32},{1,49},{17,1},{33,17},{49,33},{2,50}... | collective-permute-start | bytes 1179656 | tf_op jit(solution)/shard_map/ppermute | solution.py:298
  15.3 18.7 %collective-permute-start.5 = (bf16[1536,128]{1,0:T(8,128)(2,1)S(1)}, bf16[1536,128]{1,0:T(8,128)(2,1)S(1)}, u32[]{:S(2)}, u32[]{:S(2)}) collective-permute-start(bf16[1536,128]{1,0:T(8,128)(2,1)S(1)} %bitcast.12), channel_id=1, source_target_pairs={{0,16},{16,32},{32,48},{48,0},{1,17},{17,33},{33,49},{49,1},{2,18}... | collective-permute-start | bytes 1179656 | tf_op jit(solution)/shard_map/ppermute | solution.py:298
  17.2 22.8 %collective-permute-start = (bf16[1536,128]{1,0:T(8,128)(2,1)}, bf16[1536,128]{1,0:T(8,128)(2,1)S(1)}, u32[]{:S(2)}, u32[]{:S(2)}) collective-permute-start(bf16[1536,128]{1,0:T(8,128)(2,1)} %bitcast.1.k_ref), channel_id=1, source_target_pairs={{0,48},{16,0},{32,16},{48,32},{1,49},{17,1},{33,17},{49,33},{2,50}... | collective-permute-start | bytes 1179656 | tf_op jit(solution)/shard_map/ppermute | solution.py:298
  21.8 21.4 %collective-permute-start.3 = (bf16[1536,128]{1,0:T(8,128)(2,1)S(1)}, bf16[1536,128]{1,0:T(8,128)(2,1)S(1)}, u32[]{:S(2)}, u32[]{:S(2)}) collective-permute-start(bf16[1536,128]{1,0:T(8,128)(2,1)S(1)} %collective-permute-done.2.k_ref), channel_id=1, source_target_pairs={{0,16},{16,32},{32,48},{48,0},{1,17},{17,33},{33,49},{49,1},{2,18}... | collective-permute-start | bytes 1179656 | tf_op jit(solution)/shard_map/ppermute | solution.py:298
  23.7 19.5 %collective-permute-start.4 = (bf16[1536,128]{1,0:T(8,128)(2,1)S(1)}, bf16[1536,128]{1,0:T(8,128)(2,1)S(1)}, u32[]{:S(2)}, u32[]{:S(2)}) collective-permute-start(bf16[1536,128]{1,0:T(8,128)(2,1)S(1)} %collective-permute-done.1.refs_3_.v_ref), channel_id=1, source_target_pairs={{0,48},{16,0},{32,16},{48,32},{1,49},{17,1},{33,17},{49,33},{2,50}... | collective-permute-start | bytes 1179656 | tf_op jit(solution)/shard_map/ppermute | solution.py:298
  46.2 15.3 %collective-permute-start.7 = (bf16[32,2176]{1,0:T(8,128)(2,1)S(1)}, bf16[32,2176]{1,0:T(8,128)(2,1)S(1)}, u32[]{:S(2)}, u32[]{:S(2)}) collective-permute-start(bf16[32,2176]{1,0:T(8,128)(2,1)S(1)} %get-tuple-element.32), channel_id=1, source_target_pairs={{0,8},{4,12},{8,0},{12,4},{1,9},{5,13},{9,1},{13,5},{2,10},{6,14},... | collective-permute-start | bytes 417800 | tf_op jit(solution)/shard_map/ppermute | solution.py:301
  48.2 13.3 %collective-permute-start.8 = (bf16[32,2176]{1,0:T(8,128)(2,1)S(1)}, bf16[32,2176]{1,0:T(8,128)(2,1)S(1)}, u32[]{:S(2)}, u32[]{:S(2)}) collective-permute-start(bf16[32,2176]{1,0:T(8,128)(2,1)S(1)} %get-tuple-element.33), channel_id=1, source_target_pairs={{0,12},{4,8},{8,4},{12,0},{1,13},{5,9},{9,5},{13,1},{2,14},{6,10},... | collective-permute-start | bytes 417800 | tf_op jit(solution)/shard_map/ppermute | solution.py:301
  55.9 6.7 %copy-start.2 = (bf16[1,32,1024]{2,1,0:T(8,128)(2,1)S(1)}, bf16[1,32,1024]{2,1,0:T(8,128)(2,1)}, u32[]{:S(2)}) copy-start(bf16[1,32,1024]{2,1,0:T(8,128)(2,1)} %param.10) | copy-start | bytes 196612
  55.9 6.7 %collective-permute-start.6 = (bf16[32,2176]{1,0:T(8,128)(2,1)S(1)}, bf16[32,2176]{1,0:T(8,128)(2,1)S(1)}, u32[]{:S(2)}, u32[]{:S(2)}) collective-permute-start(bf16[32,2176]{1,0:T(8,128)(2,1)S(1)} %attend_near_1.1), channel_id=1, source_target_pairs={{0,4},{4,0},{8,12},{12,8},{1,5},{5,1},{9,13},{13,9},{2,6},{6,2},{1... | collective-permute-start | bytes 417800 | tf_op jit(solution)/shard_map/ppermute | solution.py:301
  63.5 6.7 %copy-start.1 = (bf16[32,1024]{1,0:T(8,128)(2,1)S(1)}, bf16[32,1024]{1,0:T(8,128)(2,1)}, u32[]{:S(2)}) copy-start(bf16[32,1024]{1,0:T(8,128)(2,1)} %fresh_ref.1) | copy-start | bytes 196612
  63.5 6.7 %collective-permute-start.9 = (bf16[32,1024]{1,0:T(8,128)(2,1)S(1)}, bf16[32,1024]{1,0:T(8,128)(2,1)S(1)}, u32[]{:S(2)}, u32[]{:S(2)}) collective-permute-start(bf16[32,1024]{1,0:T(8,128)(2,1)S(1)} %get-tuple-element.34), channel_id=1, source_target_pairs={{0,64},{64,128},{128,192},{192,256},{256,320},{320,384},{384,448},... | collective-permute-start | bytes 196616 | tf_op jit(solution)/shard_map/ppermute | solution.py:363
  70.5 14.2 %copy-start.4 = (bf16[1,1024]{1,0:T(2,128)(2,1)S(1)}, bf16[1,1024]{1,0:T(2,128)(2,1)}, u32[]{:S(2)}) copy-start(bf16[1,1024]{1,0:T(2,128)(2,1)} %gain_ref.1) | copy-start | bytes 6148

commit v6 on v5

--- a/solution.py
+++ b/solution.py
@@ -309,13 +309,14 @@
     v_below = along_x(v_next, 1)
     k_above = along_x(k, -1)
     k_far = along_x(k_below, 1)
-    v_far = along_x(v_above, -1)
 
     both = [pltpu.VMEM((2, HALF, HD), jnp.float32)] * 3
     one = [pltpu.VMEM((HALF, HD), jnp.float32)] * 3
     packed = pltpu.VMEM((ROWS, PACKED), jnp.bfloat16)
     common = (segment_lengths, q_all)
     state = attend(first_kernel, "attend_own", both, 0, *common, k, v)
+    v_next, state = lax.optimization_barrier((v_above, state))
+    v_far = along_x(v_next, -1)
     state = attend(second_kernel, "attend_below", both, 0, *common, k_below, v_below, *state)
     upper = attend(above_kernel, "attend_above", one, 0, *common, k_above, v_above, *state)
     part_two, part_three = attend(

time: 86.1 us -> 87.3 us (1.014)
  waiting for transfers between devices: 1.56 us -> 4.62 us
  starting transfers between devices: 39.7 us -> 38.3 us
    ppermute x6, waiting for transfers between devices: 0.02 us -> 3.08 us  [along_x(): return lax.ppermute(value, 'cx', [(i, (i + by) % NX) for i in range(NX)])]
  transfers between devices with their start and end apart: 11 -> 11, of which waited for: 2 -> 3; matrix products, arithmetic and copies ran while one was open for 2% -> 0% of each run, Pallas kernels for 26% -> 25%
where the time goes in v6:
time: 87.3 us; the launch traced here: 86.8 us
  starting transfers between devices  38.3 us (44%)
  Pallas kernels  27 us (31%)
  blocking collectives  14.2 us (16%)
  waiting for transfers between devices  4.62 us (5%)
  local copies, waits for them, and re-layouts  1.8 us (2%)
    pallas_call x6, Pallas kernels, attend(): pl.pallas_call(kernel, in_specs=[SMEM] + [VMEM] * len(operands), out_spec...  24.2 us
    ppermute x6, starting transfers between devices, along_x(): return lax.ppermute(value, 'cx', [(i, (i + by) % NX) for i in range(NX)])  19 us
    all_gather x1, blocking collectives, body(): squares = lax.all_gather(squares, 'tp')  14.2 us
    ppermute x3, starting transfers between devices, across_y(): return lax.ppermute(value, 'cy', [(i, i ^ d) for i in range(NY)])  8.5 us
    all_to_all x1, starting transfers between devices, body(): q_all = lax.all_to_all(q_own, 'cy', 0, 0)  6.21 us
    ppermute x1, starting transfers between devices, body(): lax.ppermute(residual_one, 'section', [(i, i + 1) for i in range(count -...  4.58 us
    ppermute x6, waiting for transfers between devices, along_x(): return lax.ppermute(value, 'cx', [(i, (i + by) % NX) for i in range(NX)])  3.08 us
    broadcast_in_dim x1, local copies, waits for them, and re-layouts, body(): q_own = jnp.broadcast_to(queries[:, 0], (NY, 2, ROWS, WIDTH_DEV))  1.77 us
  transfers between devices with their start and end apart: 11, of which 3 were waited for; matrix products, arithmetic and copies ran while one was open for 0% of the time, Pallas kernels for 25%

profile of v6, /device:TPU:249, one launch (start us, length us, event | category | flops | bytes accessed | tf_op | source)
XLA Modules:
  0.0 86.8 jit_solution(5986658004012289417)
XLA Ops:
  0.6 1.8 %broadcast_in_dim.9 = bf16[4,2,32,1024]{3,2,1,0:T(8,128)(2,1)} broadcast(bf16[2,32,1024]{2,1,0:T(8,128)(2,1)} %bitcast.19), dimensions={1,2,3} | broadcast | bytes 655360 | tf_op jit(solution)/shard_map/broadcast_in_dim | solution.py:306
  2.4 0.0 copy-start.1
  2.4 0.0 copy-start
  2.4 6.2 %all-to-all-start = ((bf16[4,2,32,1024]{3,2,1,0:T(8,128)(2,1)}), bf16[4,2,32,1024]{3,2,1,0:T(8,128)(2,1)S(1)}, u32[]{:S(2)}, u32[]{:S(2)}) async-start(bf16[4,2,32,1024]{3,2,1,0:T(8,128)(2,1)} %broadcast_in_dim.9), calls=%async_computation | async-start | bytes 1048576 | tf_op jit(solution)/shard_map/all_to_all | solution.py:307
  8.6 0.0 copy-done.1
  8.6 0.0 copy-start.4
  8.6 3.2 %collective-permute-start.2 = (bf16[1536,128]{1,0:T(8,128)(2,1)S(1)}, bf16[1536,128]{1,0:T(8,128)(2,1)S(1)}, u32[]{:S(2)}, u32[]{:S(2)}) collective-permute-start(bf16[1536,128]{1,0:T(8,128)(2,1)S(1)} %bitcast.14), channel_id=1, source_target_pairs={{0,16},{16,32},{32,48},{48,0},{1,17},{17,33},{33,49},{49,1},{2,18}... | collective-permute-start | bytes 1179656 | tf_op jit(solution)/shard_map/ppermute | solution.py:298
  11.9 0.0 copy-done
  11.9 3.4 %collective-permute-start.1 = (bf16[1536,128]{1,0:T(8,128)(2,1)S(1)}, bf16[1536,128]{1,0:T(8,128)(2,1)S(1)}, u32[]{:S(2)}, u32[]{:S(2)}) collective-permute-start(bf16[1536,128]{1,0:T(8,128)(2,1)S(1)} %bitcast.11), channel_id=1, source_target_pairs={{0,48},{16,0},{32,16},{48,32},{1,49},{17,1},{33,17},{49,33},{2,50}... | collective-permute-start | bytes 1179656 | tf_op jit(solution)/shard_map/ppermute | solution.py:298
  15.3 3.2 %collective-permute-start = (bf16[1536,128]{1,0:T(8,128)(2,1)S(1)}, bf16[1536,128]{1,0:T(8,128)(2,1)S(1)}, u32[]{:S(2)}, u32[]{:S(2)}) collective-permute-start(bf16[1536,128]{1,0:T(8,128)(2,1)S(1)} %bitcast.15), channel_id=1, source_target_pairs={{0,48},{16,0},{32,16},{48,32},{1,49},{17,1},{33,17},{49,33},{2,50}... | collective-permute-start | bytes 1179656 | tf_op jit(solution)/shard_map/ppermute | solution.py:298
  18.4 3.1 %collective-permute-done.2.k_ref = bf16[1536,128]{1,0:T(8,128)(2,1)S(1)} collective-permute-done((bf16[1536,128]{1,0:T(8,128)(2,1)S(1)}, bf16[1536,128]{1,0:T(8,128)(2,1)S(1)}, u32[]{:S(2)}, u32[]{:S(2)}) %collective-permute-start.2) | collective-permute-done | bytes 393248 | tf_op jit(solution)/shard_map/ppermute | solution.py:298
  21.5 1.9 %collective-permute-start.5 = (bf16[1536,128]{1,0:T(8,128)(2,1)S(1)}, bf16[1536,128]{1,0:T(8,128)(2,1)S(1)}, u32[]{:S(2)}, u32[]{:S(2)}) collective-permute-start(bf16[1536,128]{1,0:T(8,128)(2,1)S(1)} %bitcast.12), channel_id=1, source_target_pairs={{0,16},{16,32},{32,48},{48,0},{1,17},{17,33},{33,49},{49,1},{2,18}... | collective-permute-start | bytes 1179656 | tf_op jit(solution)/shard_map/ppermute | solution.py:298
  23.4 3.1 %collective-permute-start.3 = (bf16[1536,128]{1,0:T(8,128)(2,1)S(1)}, bf16[1536,128]{1,0:T(8,128)(2,1)S(1)}, u32[]{:S(2)}, u32[]{:S(2)}) collective-permute-start(bf16[1536,128]{1,0:T(8,128)(2,1)S(1)} %collective-permute-done.2.k_ref), channel_id=1, source_target_pairs={{0,16},{16,32},{32,48},{48,0},{1,17},{17,33},{33,49},{49,1},{2,18}... | collective-permute-start | bytes 1179656 | tf_op jit(solution)/shard_map/ppermute | solution.py:298
  26.5 0.0 all-to-all-done.q_ref.refs_1_
  26.6 0.0 copy-done.4
  26.6 5.2 %attend_own.1 = (f32[2,1024,128]{2,1,0:T(8,128)S(1)}, f32[2,1024,128]{2,1,0:T(8,128)S(1)}, f32[2,1024,128]{2,1,0:T(8,128)S(1)}) custom-call(s32[9]{0:T(128)S(1)} %copy-done.4, bf16[4,2,32,1024]{3,2,1,0:T(8,128)(2,1)S(1)} %all-to-all-done.q_ref.refs_1_, bf16[1536,128]{1,0:T(8,128)(2,1)S(1)} %bitcast.16, bf16[1536,128]{1,0:T(8,128)(2,1)S(1)} %bitcast.13), custom_call_target="tpu_custom_call" | custom-call | tf_op jit(solution)/shard_map/attend_own/pallas_call | solution.py:211
  31.8 0.0 collective-permute-done.1.refs_3_.v_ref
  31.8 4.2 %collective-permute-start.4 = (bf16[1536,128]{1,0:T(8,128)(2,1)S(1)}, bf16[1536,128]{1,0:T(8,128)(2,1)S(1)}, u32[]{:S(2)}, u32[]{:S(2)}) collective-permute-start(bf16[1536,128]{1,0:T(8,128)(2,1)S(1)} %collective-permute-done.1.refs_3_.v_ref), channel_id=1, source_target_pairs={{0,48},{16,0},{32,16},{48,32},{1,49},{17,1},{33,17},{49,33},{2,50}... | collective-permute-start | bytes 1179656 | tf_op jit(solution)/shard_map/ppermute | solution.py:298
  36.0 0.0 collective-permute-done.5.v_ref
  36.0 6.1 %attend_below.1 = (f32[2,1024,128]{2,1,0:T(8,128)S(1)}, f32[2,1024,128]{2,1,0:T(8,128)S(1)}, f32[2,1024,128]{2,1,0:T(8,128)S(1)}) custom-call(s32[9]{0:T(128)S(1)} %copy-done.4, bf16[4,2,32,1024]{3,2,1,0:T(8,128)(2,1)S(1)} %all-to-all-done.q_ref.refs_1_, bf16[1536,128]{1,0:T(8,128)(2,1)S(1)} %collective-permute-done.2.k_ref, ...), custom_call_target="tpu_custom_call" | custom-call | tf_op jit(solution)/shard_map/attend_below/pallas_call | solution.py:211
  42.1 0.0 collective-permute-done.refs_2_.k_ref
  42.1 3.1 %attend_above.1 = (f32[1024,128]{1,0:T(8,128)S(1)}, f32[1024,128]{1,0:T(8,128)S(1)}, f32[1024,128]{1,0:T(8,128)S(1)}) custom-call(s32[9]{0:T(128)S(1)} %copy-done.4, bf16[4,2,32,1024]{3,2,1,0:T(8,128)(2,1)S(1)} %all-to-all-done.q_ref.refs_1_, bf16[1536,128]{1,0:T(8,128)(2,1)S(1)} %collective-permute-done.refs_2_.k_ref, ...), custom_call_target="tpu_custom_call" | custom-call | tf_op jit(solution)/shard_map/attend_above/pallas_call | solution.py:211
  45.2 0.0 collective-permute-done.3.refs_4_.k_ref
  45.2 0.0 collective-permute-done.4.refs_5_.v_ref
  45.3 3.1 %attend_far.1 = (bf16[32,2176]{1,0:T(8,128)(2,1)S(1)}, bf16[32,2176]{1,0:T(8,128)(2,1)S(1)}) custom-call(s32[9]{0:T(128)S(1)} %copy-done.4, bf16[4,2,32,1024]{3,2,1,0:T(8,128)(2,1)S(1)} %all-to-all-done.q_ref.refs_1_, bf16[1536,128]{1,0:T(8,128)(2,1)S(1)} %collective-permute-done.3.refs_4_.k_ref, bf16[1536,128]{1,0:T(8,128)(2,1)S(1)} %collective-permute-done.4.refs_5_.v_ref, ...), custom_call_target="tpu_custom_call" | custom-call | tf_op jit(solution)/shard_map/attend_far/pallas_call | solution.py:211
  48.3 1.9 %collective-permute-start.7 = (bf16[32,2176]{1,0:T(8,128)(2,1)S(1)}, bf16[32,2176]{1,0:T(8,128)(2,1)S(1)}, u32[]{:S(2)}, u32[]{:S(2)}) collective-permute-start(bf16[32,2176]{1,0:T(8,128)(2,1)S(1)} %get-tuple-element.40), channel_id=1, source_target_pairs={{0,8},{4,12},{8,0},{12,4},{1,9},{5,13},{9,1},{13,5},{2,10},{6,14},... | collective-permute-start | bytes 417800 | tf_op jit(solution)/shard_map/ppermute | solution.py:301
  50.3 4.3 %collective-permute-start.8 = (bf16[32,2176]{1,0:T(8,128)(2,1)S(1)}, bf16[32,2176]{1,0:T(8,128)(2,1)S(1)}, u32[]{:S(2)}, u32[]{:S(2)}) collective-permute-start(bf16[32,2176]{1,0:T(8,128)(2,1)S(1)} %get-tuple-element.41), channel_id=1, source_target_pairs={{0,12},{4,8},{8,4},{12,0},{1,13},{5,9},{9,5},{13,1},{2,14},{6,10},... | collective-permute-start | bytes 417800 | tf_op jit(solution)/shard_map/ppermute | solution.py:301
  54.5 3.5 %attend_near_1.1 = bf16[32,2176]{1,0:T(8,128)(2,1)S(1)} custom-call(s32[9]{0:T(128)S(1)} %copy-done.4, bf16[4,2,32,1024]{3,2,1,0:T(8,128)(2,1)S(1)} %all-to-all-done.q_ref.refs_1_, bf16[1536,128]{1,0:T(8,128)(2,1)S(1)} %collective-permute-done.refs_2_.k_ref, bf16[1536,128]{1,0:T(8,128)(2,1)S(1)} %collective-permute-done.1.refs_3_.v_ref, ...), custom_call_target="tpu_custom_call" | custom-call | tf_op jit(solution)/shard_map/attend_near_1/pallas_call | solution.py:211
  58.0 0.0 copy-start.3
  58.0 2.3 %collective-permute-start.6 = (bf16[32,2176]{1,0:T(8,128)(2,1)S(1)}, bf16[32,2176]{1,0:T(8,128)(2,1)S(1)}, u32[]{:S(2)}, u32[]{:S(2)}) collective-permute-start(bf16[32,2176]{1,0:T(8,128)(2,1)S(1)} %attend_near_1.1), channel_id=1, source_target_pairs={{0,4},{4,0},{8,12},{12,8},{1,5},{5,1},{9,13},{13,9},{2,6},{6,2},{1... | collective-permute-start | bytes 417800 | tf_op jit(solution)/shard_map/ppermute | solution.py:301
  60.3 3.3 %attend_near_0.1.refs_0_ = bf16[32,2176]{1,0:T(8,128)(2,1)S(1)} custom-call(s32[9]{0:T(128)S(1)} %copy-done.4, bf16[4,2,32,1024]{3,2,1,0:T(8,128)(2,1)S(1)} %all-to-all-done.q_ref.refs_1_, bf16[1536,128]{1,0:T(8,128)(2,1)S(1)} %collective-permute-done.refs_2_.k_ref, bf16[1536,128]{1,0:T(8,128)(2,1)S(1)} %collective-permute-done.1.refs_3_.v_ref, ...), custom_call_target="tpu_custom_call" | custom-call | tf_op jit(solution)/shard_map/attend_near_0/pallas_call | solution.py:211
  63.6 0.0 collective-permute-done.7.refs_2_
  63.6 0.0 collective-permute-done.8.refs_3_
  63.6 1.1 %collective-permute-done.6.refs_1_ = bf16[32,2176]{1,0:T(8,128)(2,1)S(1)} collective-permute-done((bf16[32,2176]{1,0:T(8,128)(2,1)S(1)}, bf16[32,2176]{1,0:T(8,128)(2,1)S(1)}, u32[]{:S(2)}, u32[]{:S(2)}) %collective-permute-start.6) | collective-permute-done | bytes 139296 | tf_op jit(solution)/shard_map/ppermute | solution.py:301
  64.7 0.0 copy-done.3
  64.7 0.9 %merge_one.1 = (bf16[32,1024]{1,0:T(8,128)(2,1)S(1)}, f32[32,1024]{1,0:T(8,128)S(1)}) custom-call(s32[9]{0:T(128)S(1)} %copy-done.4, bf16[32,1024]{1,0:T(8,128)(2,1)S(1)} %bitcast.17, bf16[32,2176]{1,0:T(8,128)(2,1)S(1)} %attend_near_0.1.refs_0_, bf16[32,2176]{1,0:T(8,128)(2,1)S(1)} %collective-permute-done.6.refs_1_, ...), custom_call_target="tpu_custom_call" | custom-call | tf_op jit(solution)/shard_map/merge_one/pallas_call | solution.py:347
  65.6 0.0 copy-start.2
  65.6 4.6 %collective-permute-start.9 = (bf16[32,1024]{1,0:T(8,128)(2,1)S(1)}, bf16[32,1024]{1,0:T(8,128)(2,1)S(1)}, u32[]{:S(2)}, u32[]{:S(2)}) collective-permute-start(bf16[32,1024]{1,0:T(8,128)(2,1)S(1)} %get-tuple-element.42), channel_id=1, source_target_pairs={{0,64},{64,128},{128,192},{192,256},{256,320},{320,384},{384,448},... | collective-permute-start | bytes 196616 | tf_op jit(solution)/shard_map/ppermute | solution.py:364
  70.2 0.9 merge_two.1.attended_ref
  71.1 0.4 collective-permute-done.9.passed_ref
  71.5 0.0 copy-done.2
  71.5 0.3 add.1
  71.8 0.0 copy-start.5
  71.8 14.2 %all-gather.1.squares_ref = f32[4,2,32]{2,1,0:T(2,128)S(1)} all-gather(f32[1,2,32]{2,1,0:T(2,128)S(1)} %bitcast.18), channel_id=2, replica_groups=mesh['section'=8,'cx'=4,'cy'=4,'tp'=4] {'tp'}, dimensions={0}, use_global_device_ids=true | all-gather | bytes 1280 | tf_op jit(solution)/shard_map/all_gather | solution.py:373
  86.0 0.0 copy-done.5
  86.0 0.8 norm.1
Async XLA Ops:
  2.4 6.2 %copy-start.1 = (bf16[1,1536,128]{2,1,0:T(8,128)(2,1)S(1)}, bf16[1,1536,128]{2,1,0:T(8,128)(2,1)}, u32[]{:S(2)}) copy-start(bf16[1,1536,128]{2,1,0:T(8,128)(2,1)} %param.8) | copy-start | bytes 1179652
  2.4 9.5 %copy-start = (bf16[1,1536,128]{2,1,0:T(8,128)(2,1)S(1)}, bf16[1,1536,128]{2,1,0:T(8,128)(2,1)}, u32[]{:S(2)}) copy-start(bf16[1,1536,128]{2,1,0:T(8,128)(2,1)} %param.9) | copy-start | bytes 1179652
  2.4 24.1 %all-to-all-start = ((bf16[4,2,32,1024]{3,2,1,0:T(8,128)(2,1)}), bf16[4,2,32,1024]{3,2,1,0:T(8,128)(2,1)S(1)}, u32[]{:S(2)}, u32[]{:S(2)}) async-start(bf16[4,2,32,1024]{3,2,1,0:T(8,128)(2,1)} %broadcast_in_dim.9), calls=%async_computation | async-start | bytes 1048576 | tf_op jit(solution)/shard_map/all_to_all | solution.py:307
  8.6 17.9 %copy-start.4 = (s32[9]{0:T(128)S(1)}, s32[9]{0:T(128)}, u32[]{:S(2)}) copy-start(s32[9]{0:T(128)} %lengths_ref.11) | copy-start | bytes 112
  8.6 12.9 %collective-permute-start.2 = (bf16[1536,128]{1,0:T(8,128)(2,1)S(1)}, bf16[1536,128]{1,0:T(8,128)(2,1)S(1)}, u32[]{:S(2)}, u32[]{:S(2)}) collective-permute-start(bf16[1536,128]{1,0:T(8,128)(2,1)S(1)} %bitcast.14), channel_id=1, source_target_pairs={{0,16},{16,32},{32,48},{48,0},{1,17},{17,33},{33,49},{49,1},{2,18}... | collective-permute-start | bytes 1179656 | tf_op jit(solution)/shard_map/ppermute | solution.py:298
  11.9 19.9 %collective-permute-start.1 = (bf16[1536,128]{1,0:T(8,128)(2,1)S(1)}, bf16[1536,128]{1,0:T(8,128)(2,1)S(1)}, u32[]{:S(2)}, u32[]{:S(2)}) collective-permute-start(bf16[1536,128]{1,0:T(8,128)(2,1)S(1)} %bitcast.11), channel_id=1, source_target_pairs={{0,48},{16,0},{32,16},{48,32},{1,49},{17,1},{33,17},{49,33},{2,50}... | collective-permute-start | bytes 1179656 | tf_op jit(solution)/shard_map/ppermute | solution.py:298
  15.3 26.8 %collective-permute-start = (bf16[1536,128]{1,0:T(8,128)(2,1)S(1)}, bf16[1536,128]{1,0:T(8,128)(2,1)S(1)}, u32[]{:S(2)}, u32[]{:S(2)}) collective-permute-start(bf16[1536,128]{1,0:T(8,128)(2,1)S(1)} %bitcast.15), channel_id=1, source_target_pairs={{0,48},{16,0},{32,16},{48,32},{1,49},{17,1},{33,17},{49,33},{2,50}... | collective-permute-start | bytes 1179656 | tf_op jit(solution)/shard_map/ppermute | solution.py:298
  21.5 14.5 %collective-permute-start.5 = (bf16[1536,128]{1,0:T(8,128)(2,1)S(1)}, bf16[1536,128]{1,0:T(8,128)(2,1)S(1)}, u32[]{:S(2)}, u32[]{:S(2)}) collective-permute-start(bf16[1536,128]{1,0:T(8,128)(2,1)S(1)} %bitcast.12), channel_id=1, source_target_pairs={{0,16},{16,32},{32,48},{48,0},{1,17},{17,33},{33,49},{49,1},{2,18}... | collective-permute-start | bytes 1179656 | tf_op jit(solution)/shard_map/ppermute | solution.py:298
  23.4 21.8 %collective-permute-start.3 = (bf16[1536,128]{1,0:T(8,128)(2,1)S(1)}, bf16[1536,128]{1,0:T(8,128)(2,1)S(1)}, u32[]{:S(2)}, u32[]{:S(2)}) collective-permute-start(bf16[1536,128]{1,0:T(8,128)(2,1)S(1)} %collective-permute-done.2.k_ref), channel_id=1, source_target_pairs={{0,16},{16,32},{32,48},{48,0},{1,17},{17,33},{33,49},{49,1},{2,18}... | collective-permute-start | bytes 1179656 | tf_op jit(solution)/shard_map/ppermute | solution.py:298
  31.8 13.5 %collective-permute-start.4 = (bf16[1536,128]{1,0:T(8,128)(2,1)S(1)}, bf16[1536,128]{1,0:T(8,128)(2,1)S(1)}, u32[]{:S(2)}, u32[]{:S(2)}) collective-permute-start(bf16[1536,128]{1,0:T(8,128)(2,1)S(1)} %collective-permute-done.1.refs_3_.v_ref), channel_id=1, source_target_pairs={{0,48},{16,0},{32,16},{48,32},{1,49},{17,1},{33,17},{49,33},{2,50}... | collective-permute-start | bytes 1179656 | tf_op jit(solution)/shard_map/ppermute | solution.py:298
  48.3 15.3 %collective-permute-start.7 = (bf16[32,2176]{1,0:T(8,128)(2,1)S(1)}, bf16[32,2176]{1,0:T(8,128)(2,1)S(1)}, u32[]{:S(2)}, u32[]{:S(2)}) collective-permute-start(bf16[32,2176]{1,0:T(8,128)(2,1)S(1)} %get-tuple-element.40), channel_id=1, source_target_pairs={{0,8},{4,12},{8,0},{12,4},{1,9},{5,13},{9,1},{13,5},{2,10},{6,14},... | collective-permute-start | bytes 417800 | tf_op jit(solution)/shard_map/ppermute | solution.py:301
  50.3 13.4 %collective-permute-start.8 = (bf16[32,2176]{1,0:T(8,128)(2,1)S(1)}, bf16[32,2176]{1,0:T(8,128)(2,1)S(1)}, u32[]{:S(2)}, u32[]{:S(2)}) collective-permute-start(bf16[32,2176]{1,0:T(8,128)(2,1)S(1)} %get-tuple-element.41), channel_id=1, source_target_pairs={{0,12},{4,8},{8,4},{12,0},{1,13},{5,9},{9,5},{13,1},{2,14},{6,10},... | collective-permute-start | bytes 417800 | tf_op jit(solution)/shard_map/ppermute | solution.py:301
  58.0 6.7 %copy-start.3 = (bf16[1,32,1024]{2,1,0:T(8,128)(2,1)S(1)}, bf16[1,32,1024]{2,1,0:T(8,128)(2,1)}, u32[]{:S(2)}) copy-start(bf16[1,32,1024]{2,1,0:T(8,128)(2,1)} %param.10) | copy-start | bytes 196612
  58.0 6.7 %collective-permute-start.6 = (bf16[32,2176]{1,0:T(8,128)(2,1)S(1)}, bf16[32,2176]{1,0:T(8,128)(2,1)S(1)}, u32[]{:S(2)}, u32[]{:S(2)}) collective-permute-start(bf16[32,2176]{1,0:T(8,128)(2,1)S(1)} %attend_near_1.1), channel_id=1, source_target_pairs={{0,4},{4,0},{8,12},{12,8},{1,5},{5,1},{9,13},{13,9},{2,6},{6,2},{1... | collective-permute-start | bytes 417800 | tf_op jit(solution)/shard_map/ppermute | solution.py:301
  65.6 5.9 %copy-start.2 = (bf16[32,1024]{1,0:T(8,128)(2,1)S(1)}, bf16[32,1024]{1,0:T(8,128)(2,1)}, u32[]{:S(2)}) copy-start(bf16[32,1024]{1,0:T(8,128)(2,1)} %fresh_ref.1) | copy-start | bytes 196612
  65.6 5.9 %collective-permute-start.9 = (bf16[32,1024]{1,0:T(8,128)(2,1)S(1)}, bf16[32,1024]{1,0:T(8,128)(2,1)S(1)}, u32[]{:S(2)}, u32[]{:S(2)}) collective-permute-start(bf16[32,1024]{1,0:T(8,128)(2,1)S(1)} %get-tuple-element.42), channel_id=1, source_target_pairs={{0,64},{64,128},{128,192},{192,256},{256,320},{320,384},{384,448},... | collective-permute-start | bytes 196616 | tf_op jit(solution)/shard_map/ppermute | solution.py:364
  71.8 14.2 %copy-start.5 = (bf16[1,1024]{1,0:T(2,128)(2,1)S(1)}, bf16[1,1024]{1,0:T(2,128)(2,1)}, u32[]{:S(2)}) copy-start(bf16[1,1024]{1,0:T(2,128)(2,1)} %gain_ref.1) | copy-start | bytes 6148
